TPU v7x, 256 devices: a whole 4x4x8 slice. The times are simulated.
256 devices in a mesh: dp: 16 (over z_hi, x, core), mp: 16 (over y, z_lo).
Axes of the slice: x: 4, y: 4, z: 8 (z_hi: 2, z_lo: 4; z = z_hi * 4 + z_lo), core: 2. Of those that a mesh axis runs over, the one named last changes fastest.
Arguments:
- tokens: bfloat16 [2048, 4096], P('dp', 'mp'), may hold values from -6 to 6
- cotangent: bfloat16 [2048, 4096], P('dp', 'mp'), may hold values from -6 to 6
- gate_blocks: bfloat16 [128, 2048, 128], P('mp', 'dp'), may hold values from -0.125 to 0.125
- up_blocks: bfloat16 [128, 2048, 128], P('mp', 'dp'), may hold values from -0.125 to 0.125
- down_blocks: bfloat16 [128, 128, 2048], P('mp', None, 'dp'), may hold values from -0.0625 to 0.0625
- owner: int32 [112], replicated, may hold values from 0 to 15, as said below
- up_rows: int32 [112, 16], replicated, may hold values from 0 to 31, as said below
- down_cols: int32 [112, 16], replicated, may hold values from 0 to 31, as said below
Outputs:
- output: bfloat16 [2048, 4096], P('dp', 'mp')
- input_grad: bfloat16 [2048, 4096], P('dp', 'mp')
- gate_grad: float32 [128, 2048, 128], P('mp', 'dp')
- up_grad: float32 [128, 2048, 128], P('mp', 'dp')
- down_grad: float32 [128, 128, 2048], P('mp', None, 'dp')
Inputs may be any that keep to these rules, and one draw needn't show every extreme that they name: Each owner holds at most 8 hidden blocks and some owner holds exactly 8. `up_rows`: each row lists 16 different row blocks. `down_cols`: each row lists 16 different column blocks.
All inputs are finite; a program needn't handle non-finite values.
Results may differ from a plain program's by a relative error of at most 0.022.
Values may be sent and summed in bfloat16 or wider, within the bound.
No kernel may reach another device: no remote copies, remote signals or barrier semaphores. Data moves between devices by JAX's collectives and lax.ppermute only.
A program may use at most 128 MiB of HBM per device.

v0:
```python
import jax
import jax.numpy as jnp
from jax import lax
from jax.sharding import PartitionSpec as P


def slot_tables(owner, up_rows, down_cols, owner_at, owner_count, capacity):
    onehot = (owner[:, None] == jnp.arange(owner_count, dtype=jnp.int32)[None, :]).astype(jnp.int32)
    ranks = jnp.sum(jnp.cumsum(onehot, 0) * onehot, 1) - 1
    select = (
        (owner[None, :] == owner_at)
        & (ranks[None, :] == jnp.arange(capacity, dtype=jnp.int32)[:, None])
    ).astype(jnp.int32)
    row_ids = jnp.sum(select[:, :, None] * up_rows[None, :, :], 1)
    col_ids = jnp.sum(select[:, :, None] * down_cols[None, :, :], 1)
    live_mask = jnp.sum(select, 1).astype(jnp.float32)
    return (row_ids, col_ids, live_mask)


def pick_blocks(values, ids, block_size):
    count = values.shape[0]
    shaped = values.reshape(count, values.shape[1] // block_size, block_size)
    taken = jnp.take(shaped, ids.reshape(-1), axis=1)
    return taken.reshape(count, ids.shape[0], ids.shape[1] * block_size)


def place_blocks(terms, ids, live_mask, row_blocks, block_size):
    count = terms.shape[0]
    slots = ids.shape[0] * ids.shape[1]
    flags = (ids.reshape(-1)[:, None] == jnp.arange(row_blocks, dtype=jnp.int32)[None, :]).astype(
        jnp.float32
    )
    flags = flags * jnp.repeat(live_mask, ids.shape[1])[:, None]
    placed = jnp.einsum(
        "tsb,sk->tkb",
        terms.reshape(count, slots, block_size),
        flags,
        precision=lax.Precision.HIGHEST,
    )
    return placed.reshape(count, row_blocks * block_size)


def shards(tokens, cotangent, gate_blocks, up_blocks, down_blocks, owner, up_rows, down_cols):
    f32 = jnp.float32
    owner_at = lax.axis_index("mp")
    owner_count = lax.axis_size("mp")
    capacity = gate_blocks.shape[0]
    block_size = gate_blocks.shape[2]
    features, grad_out = (
        lax.all_gather(tokens, "mp", axis=1, tiled=True),
        lax.all_gather(cotangent, "mp", axis=1, tiled=True),
    )
    row_blocks = features.shape[1] // block_size
    row_ids, col_ids, live_mask = slot_tables(
        owner, up_rows, down_cols, owner_at, owner_count, capacity
    )
    picked = pick_blocks(features, row_ids, block_size)
    down_full = lax.all_gather(down_blocks, "dp", axis=2, tiled=True)
    gate_full, up_full = (
        lax.all_gather(gate_blocks, "dp", axis=1, tiled=True),
        lax.all_gather(up_blocks, "dp", axis=1, tiled=True),
    )
    gate_pre = jnp.einsum("tck,ckh->tch", picked, gate_full, preferred_element_type=f32)
    up_pre = jnp.einsum("tck,ckh->tch", picked, up_full, preferred_element_type=f32)
    sig_gate = jax.nn.sigmoid(gate_pre)
    hidden = (live_mask[None, :, None] * gate_pre * sig_gate * up_pre).astype(jnp.bfloat16)
    down_terms = jnp.einsum("tch,chk->tck", hidden, down_full, preferred_element_type=f32)
    out_part = place_blocks(down_terms, col_ids, live_mask, row_blocks, block_size)
    output = lax.psum_scatter(out_part.astype(jnp.bfloat16), "mp", scatter_dimension=1, tiled=True)
    picked_grad = pick_blocks(grad_out, col_ids, block_size)
    down_part = jnp.einsum("tch,tck->chk", hidden, picked_grad, preferred_element_type=f32)
    grad_hidden = live_mask[None, :, None] * jnp.einsum(
        "tck,chk->tch", picked_grad, down_full, preferred_element_type=f32
    )
    up_term = (grad_hidden * gate_pre * sig_gate).astype(jnp.bfloat16)
    gate_term = (grad_hidden * up_pre * sig_gate * (1.0 + gate_pre * (1.0 - sig_gate))).astype(
        jnp.bfloat16
    )
    gate_part = jnp.einsum("tck,tch->ckh", picked, gate_term, preferred_element_type=f32)
    up_part = jnp.einsum("tck,tch->ckh", picked, up_term, preferred_element_type=f32)
    in_terms = jnp.einsum("tch,ckh->tck", gate_term, gate_full, preferred_element_type=f32)
    in_terms = in_terms + jnp.einsum("tch,ckh->tck", up_term, up_full, preferred_element_type=f32)
    in_part = place_blocks(in_terms, row_ids, live_mask, row_blocks, block_size)
    input_grad = lax.psum_scatter(
        in_part.astype(jnp.bfloat16), "mp", scatter_dimension=1, tiled=True
    )
    gate_grad, up_grad = (
        lax.psum_scatter(
            gate_part.astype(jnp.bfloat16), "dp", scatter_dimension=1, tiled=True
        ).astype(jnp.float32),
        lax.psum_scatter(
            up_part.astype(jnp.bfloat16), "dp", scatter_dimension=1, tiled=True
        ).astype(jnp.float32),
    )
    down_grad = lax.psum_scatter(
        down_part.astype(jnp.bfloat16), "dp", scatter_dimension=2, tiled=True
    ).astype(jnp.float32)
    return (output, input_grad, gate_grad, up_grad, down_grad)


def solution(mesh):
    return jax.shard_map(
        shards,
        mesh=mesh,
        in_specs=(
            P("dp", "mp"),
            P("dp", "mp"),
            P("mp", "dp", None),
            P("mp", "dp", None),
            P("mp", None, "dp"),
            P(),
            P(),
            P(),
        ),
        out_specs=(
            P("dp", "mp"),
            P("dp", "mp"),
            P("mp", "dp", None),
            P("mp", "dp", None),
            P("mp", None, "dp"),
        ),
        check_vma=False,
    )
```

profile of v0, /device:TPU:1, one launch (start us, length us, event | category | flops | bytes accessed | tf_op | source)
XLA Modules:
  0.0 906.8 jit_solution(5511139723836971537)
XLA Ops:
  16.3 70.3 %all-gather.6.cloned.1.call-done = bf16[128,4096]{0,1:T(8,128)(2,1)} async-done(((bf16[128,256]{0,1:T(8,128)(2,1)}), bf16[128,4096]{0,1:T(8,128)(2,1)}) %all-gather.6.cloned.1.call-update) | async-done | bytes 1048592 | tf_op jit(solution)/shard_map/all_gather | solution.py:50
  91.2 4.6 select_bitcast_fusion.1
  95.8 6.3 copy.67
  102.1 67.5 %all-gather.14.cloned.1.call-done = bf16[128,4096]{0,1:T(8,128)(2,1)} async-done(((bf16[128,256]{0,1:T(8,128)(2,1)}), bf16[128,4096]{0,1:T(8,128)(2,1)}) %all-gather.14.cloned.1.call-update) | async-done | bytes 1048592 | tf_op jit(solution)/shard_map/all_gather | solution.py:51
  171.2 3.0 gather_fusion.1
  174.3 4.6 select_bitcast_fusion
  178.9 6.4 copy.74
  185.2 73.2 %all-gather.10.cloned.1.call-done = bf16[8,2048,128]{2,1,0:T(8,128)(2,1)} async-done(((bf16[8,128,128]{2,1,0:T(8,128)(2,1)}), bf16[8,2048,128]{2,1,0:T(8,128)(2,1)}) %all-gather.10.cloned.1.call-update) | async-done | bytes 4194320 | tf_op jit(solution)/shard_map/all_gather | solution.py:61
  258.4 4.8 convolution_bitcast_fusion.1
  263.2 70.7 %all-gather.8.cloned.1.call-done = bf16[8,2048,128]{2,1,0:T(8,128)(2,1)} async-done(((bf16[8,128,128]{2,1,0:T(8,128)(2,1)}), bf16[8,2048,128]{2,1,0:T(8,128)(2,1)}) %all-gather.8.cloned.1.call-update) | async-done | bytes 4194320 | tf_op jit(solution)/shard_map/all_gather | solution.py:60
  333.9 4.8 convolution_bitcast_fusion.2
  338.7 71.4 %all-gather.12.cloned.1.call-done = bf16[8,128,2048]{2,1,0:T(8,128)(2,1)} async-done(((bf16[8,128,128]{2,1,0:T(8,128)(2,1)}), bf16[8,128,2048]{2,1,0:T(8,128)(2,1)}) %all-gather.12.cloned.1.call-update) | async-done | bytes 4194320 | tf_op jit(solution)/shard_map/all_gather | solution.py:58
  410.1 5.2 multiply_convert_fusion
  415.2 3.3 convolution_convert_fusion
  418.5 6.7 copy.85
  425.2 5.2 copy.94
  430.7 5.4 convolution_convert_fusion.2
  436.1 5.5 convolution_convert_fusion.1
  441.9 3.8 fusion.17
  445.8 4.5 add_bitcast_fusion
  450.3 9.2 %copy.76 = f32[128,8,2048]{0,2,1:T(8,128)} copy(f32[128,8,2048]{2,0,1:T(8,128)} %add_bitcast_fusion) | data formatting | bytes 16777216 | tf_op jit(solution)/shard_map/add | solution.py:82
  459.5 9.4 %copy.77 = f32[128,128,128]{2,1,0:T(8,128)} copy(f32[128,128,128]{0,2,1:T(8,128)} %bitcast.69) | data formatting | bytes 16777216 | tf_op jit(solution)/shard_map/reshape | solution.py:36
  468.9 6.7 convolution_convert_fusion.3
  477.3 6.6 convolution_bitcast_fusion
  484.0 9.1 %copy.70 = f32[128,8,2048]{0,2,1:T(8,128)} copy(f32[128,8,2048]{2,0,1:T(8,128)} %convolution_bitcast_fusion) | data formatting | bytes 16777216 | tf_op jit(solution)/shard_map/tch,chk->tck/transpose | solution.py:67
  493.1 9.4 %copy.71 = f32[128,128,128]{2,1,0:T(8,128)} copy(f32[128,128,128]{0,2,1:T(8,128)} %bitcast.70) | data formatting | bytes 16777216 | tf_op jit(solution)/shard_map/reshape | solution.py:36
  502.5 6.7 convolution_convert_fusion.4
  510.7 18.4 %reduce-scatter.16.cloned.1.call-done = bf16[128,1024]{1,0:T(8,128)(2,1)} async-done(((bf16[2048,1024]{1,0:T(8,128)(2,1)}), bf16[128,1024]{1,0:T(8,128)(2,1)}) %reduce-scatter.16.cloned.1.call-update) | async-done | bytes 262160
  531.1 102.9 %reduce-scatter.12.cloned.1.call-done = bf16[8,128,128]{2,1,0:T(8,128)(2,1)} async-done(((bf16[8,2048,128]{2,1,0:T(8,128)(2,1)}), bf16[8,128,128]{2,1,0:T(8,128)(2,1)}) %reduce-scatter.12.cloned.1.call-update) | async-done | bytes 262160 | tf_op jit(solution)/shard_map/reduce_scatter | solution.py:88
  635.8 102.6 %reduce-scatter.14.cloned.1.call-done = bf16[8,128,128]{2,1,0:T(8,128)(2,1)} async-done(((bf16[8,2048,128]{2,1,0:T(8,128)(2,1)}), bf16[8,128,128]{2,1,0:T(8,128)(2,1)}) %reduce-scatter.14.cloned.1.call-update) | async-done | bytes 262160 | tf_op jit(solution)/shard_map/reduce_scatter | solution.py:91
  740.1 74.2 %reduce-scatter.10.cloned.1.call-done = bf16[128,256]{1,0:T(8,128)(2,1)} async-done(((bf16[128,4096]{1,0:T(8,128)(2,1)}), bf16[128,256]{1,0:T(8,128)(2,1)}) %reduce-scatter.10.cloned.1.call-update) | async-done | bytes 65552 | tf_op jit(solution)/shard_map/reduce_scatter | solution.py:84
  814.3 85.7 %reduce-scatter.8.cloned.1.call-done = bf16[128,256]{1,0:T(8,128)(2,1)} async-done(((bf16[128,4096]{1,0:T(8,128)(2,1)}), bf16[128,256]{1,0:T(8,128)(2,1)}) %reduce-scatter.8.cloned.1.call-update) | async-done | bytes 65552 | tf_op jit(solution)/shard_map/reduce_scatter | solution.py:69
  (55 shorter events, 24.5 us)
Async XLA Ops:
  7.2 79.4 %all-gather.6.cloned.1.call-start = ((), (), s32[]{:S(2)}) async-start(), calls=%async_computation.5 | async-start | bytes 1114112 | tf_op jit(solution)/shard_map/all_gather | solution.py:50
  8.8 160.8 %all-gather.14.cloned.1.call-start = ((), (), s32[]{:S(2)}) async-start(), calls=%async_computation.10 | async-start | bytes 1114112 | tf_op jit(solution)/shard_map/all_gather | solution.py:51
  10.5 248.0 %all-gather.10.cloned.1.call-start = ((), (), s32[]{:S(2)}) async-start(), calls=%async_computation.7 | async-start | bytes 4456448 | tf_op jit(solution)/shard_map/all_gather | solution.py:61
  11.2 322.7 %all-gather.8.cloned.1.call-start = ((), (), s32[]{:S(2)}) async-start(), calls=%async_computation.6 | async-start | bytes 4456448 | tf_op jit(solution)/shard_map/all_gather | solution.py:60
  11.8 398.3 %all-gather.12.cloned.1.call-start = ((), (), s32[]{:S(2)}) async-start(), calls=%async_computation.8 | async-start | bytes 4456448 | tf_op jit(solution)/shard_map/all_gather | solution.py:58
  12.4 516.7 %reduce-scatter.16.cloned.1.call-start = ((), (), s32[]{:S(2)}) async-start(), calls=%async_computation.14 | async-start | bytes 4456448
  410.1 5.2 copy-start
  430.5 203.5 %reduce-scatter.12.cloned.1.call-start = ((), (), s32[]{:S(2)}) async-start(), calls=%async_computation.12 | async-start | bytes 4456448 | tf_op jit(solution)/shard_map/reduce_scatter | solution.py:88
  436.1 302.3 %reduce-scatter.14.cloned.1.call-start = ((), (), s32[]{:S(2)}) async-start(), calls=%async_computation.13 | async-start | bytes 4456448 | tf_op jit(solution)/shard_map/reduce_scatter | solution.py:91
  441.7 372.6 %reduce-scatter.10.cloned.1.call-start = ((), (), s32[]{:S(2)}) async-start(), calls=%async_computation.11 | async-start | bytes 1114112 | tf_op jit(solution)/shard_map/reduce_scatter | solution.py:84
  441.9 3.9 copy-start.1
  477.1 422.9 %reduce-scatter.8.cloned.1.call-start = ((), (), s32[]{:S(2)}) async-start(), calls=%async_computation.9 | async-start | bytes 1114112 | tf_op jit(solution)/shard_map/reduce_scatter | solution.py:69
Sparse Core Ops, SparseCore 0:
  10.4 76.1 all-gather.5
  88.9 80.6 all-gather.13
  172.4 85.9 all-gather.9
  261.0 72.7 all-gather.7
  336.3 73.7 all-gather.11
  430.6 98.4 reduce-scatter.15
  534.0 99.9 reduce-scatter.11
  638.3 99.9 reduce-scatter.13
  741.6 72.6 reduce-scatter.9
  817.3 82.7 reduce-scatter.7
where the time goes:
time: 919 us; the launch traced here: 907 us
  waiting for transfers between devices  739 us (80%)
  local copies, waits for them, and re-layouts  78.7 us (9%)
  matrix products  57.2 us (6%)
  other arithmetic  17.2 us (2%)
  between operations  14.3 us (2%)
    reduce_scatter x1, waiting for transfers between devices, shards(): lax.psum_scatter(gate_part.astype(jnp.bfloat16), 'dp', scatter_dimension=...  103 us
    reduce_scatter x1, waiting for transfers between devices, shards(): lax.psum_scatter(up_part.astype(jnp.bfloat16), 'dp', scatter_dimension=1,...  103 us
    reduce_scatter x1, waiting for transfers between devices, shards(): lax.psum_scatter(out_part.astype(jnp.bfloat16), 'mp', scatter_dimension=1...  85.7 us
    reduce_scatter x1, waiting for transfers between devices, shards(): lax.psum_scatter(in_part.astype(jnp.bfloat16), 'mp', scatter_dimension=1,...  74.2 us
    all_gather x1, waiting for transfers between devices, shards(): lax.all_gather(up_blocks, 'dp', axis=1, tiled=True)  73.2 us
    all_gather x1, waiting for transfers between devices, shards(): down_full = lax.all_gather(down_blocks, 'dp', axis=2, tiled=True)  71.4 us
    all_gather x1, waiting for transfers between devices, shards(): lax.all_gather(gate_blocks, 'dp', axis=1, tiled=True)  70.7 us
    all_gather x1, waiting for transfers between devices, shards(): lax.all_gather(tokens, 'mp', axis=1, tiled=True)  70.3 us
  transfers between devices with their start and end apart: 10, of which 10 were waited for; matrix products, arithmetic and copies ran while one was open for 14% of the time, Pallas kernels for 0%

commit v1 on v0

v1 whole, which is shorter than its diff:
```python
import functools

import jax
import jax.numpy as jnp
from jax import lax
from jax.experimental import pallas as pl
from jax.experimental.pallas import tpu as pltpu
from jax.sharding import Mesh, PartitionSpec as P

BF16 = jnp.bfloat16
F32 = jnp.float32
BLK = 128
HALF = 4
PIECES = 8
CHUNKS = 1


def rot(value, axis, step):
    n = lax.axis_size(axis)
    return lax.ppermute(value, axis, [(i, (i + step) % n) for i in range(n)])


def dot(a, b, ca, cb):
    return lax.dot_general(a, b, (((ca,), (cb,)), ((), ())), preferred_element_type=F32)


def layer_kernel(first, last, slots, *refs):
    up_ids, down_ids, live = refs[:3]
    acts = refs[3:11]
    at = 11
    carried = ()
    if not first:
        carried = refs[at : at + 2]
        at += 2
    weights = refs[at : at + PIECES]
    at += PIECES
    own_out, other_out = refs[at : at + 2]
    at += 2
    grads = refs[at : at + PIECES]
    at += PIECES
    xv, acc, pk, pg, wgu, wd, sems = refs[at:]
    s = pl.program_id(0)

    @pl.when(s == 0)
    def _():
        for i in range(8):
            pltpu.make_async_copy(
                acts[i], xv.at[i // 4, pl.ds((i % 4) * 8, 8)], sems.at[i]
            ).start()
        acc[...] = jnp.zeros_like(acc)
        for i in range(8):
            pltpu.make_async_copy(
                acts[i], xv.at[i // 4, pl.ds((i % 4) * 8, 8)], sems.at[i]
            ).wait()

    for b in range(16):
        u = up_ids[s, b]
        d = down_ids[s, b]
        cols = slice(b * BLK, (b + 1) * BLK)
        for c in range(2):
            rows = slice(c * BLK, (c + 1) * BLK)
            pk[rows, cols] = xv[c, u, 0]
            pg[rows, cols] = xv[c, d, 1]
        w = weights[b // 2]
        wgu[cols, 0:BLK] = w[b % 2, 0, 0]
        wgu[cols, BLK : 2 * BLK] = w[b % 2, 0, 1]
        wd[:, cols] = w[b % 2, 0, 2]

    alive = live[s]
    gate_up = dot(pk[...], wgu[...], 1, 0)
    gate = gate_up[:, :BLK]
    up = gate_up[:, BLK:]
    grad_hidden = alive * dot(pg[...], wd[...], 1, 1)
    sig = jax.nn.sigmoid(gate)
    hidden = (alive * gate * sig * up).astype(BF16)
    up_term = (grad_hidden * gate * sig).astype(BF16)
    gate_term = (grad_hidden * up * sig * (1.0 + gate * (1.0 - sig))).astype(BF16)
    terms = jnp.concatenate([gate_term, up_term], axis=1)

    for q in range(4):
        cols = slice(q * 512, (q + 1) * 512)
        out_terms = dot(hidden, wd[:, cols], 1, 0)
        in_terms = dot(terms, wgu[cols, :], 1, 1)
        dgu = dot(pk[:, cols], terms, 0, 0)
        dd = dot(hidden, pg[:, cols], 0, 0)
        for r in range(4):
            b = q * 4 + r
            part = slice(r * BLK, (r + 1) * BLK)
            u = up_ids[s, b]
            d = down_ids[s, b]
            acc[d, 0] += out_terms[:, part]
            acc[u, 1] += in_terms[:, part]
            g = grads[b // 2]
            g[b % 2, 0, 0] = dgu[part, :BLK].astype(BF16)
            g[b % 2, 0, 1] = dgu[part, BLK:].astype(BF16)
            g[b % 2, 0, 2] = dd[:, part].astype(BF16)

    @pl.when(s == slots - 1)
    def _():
        own = acc[:, :, :BLK, :]
        other = acc[:, :, BLK:, :]
        if not first:
            own = own + carried[0][...].astype(F32)
            other = other + carried[1][...].astype(F32)
        own_out[...] = own.astype(BF16)
        other_out[...] = other.astype(BF16)


def layer(first, last, up_ids, down_ids, live, acts, carried, weights):
    slots = weights[0].shape[1]
    smem = pl.BlockSpec(memory_space=pltpu.SMEM)
    anys = pl.BlockSpec(memory_space=pl.ANY)
    whole = pl.BlockSpec((32, 2, BLK, BLK), lambda s: (0, 0, 0, 0), pipeline_mode=pl.Buffered(1))
    piece = pl.BlockSpec((2, 1, 3, BLK, BLK), lambda s: (0, s, 0, 0, 0))
    part = jax.ShapeDtypeStruct((32, 2, BLK, BLK), BF16)
    grad = jax.ShapeDtypeStruct(weights[0].shape, BF16)
    outs = pl.pallas_call(
        functools.partial(layer_kernel, first, last, slots),
        grid=(slots,),
        in_specs=[smem] * 3 + [anys] * 8 + [whole] * len(carried) + [piece] * PIECES,
        out_specs=[whole] * 2 + [piece] * PIECES,
        out_shape=[part] * 2 + [grad] * PIECES,
        scratch_shapes=[
            pltpu.VMEM((2, 32, 2, BLK, BLK), BF16),
            pltpu.VMEM((32, 2, 2 * BLK, BLK), F32),
            pltpu.VMEM((2 * BLK, 2048), BF16),
            pltpu.VMEM((2 * BLK, 2048), BF16),
            pltpu.VMEM((2048, 2 * BLK), BF16),
            pltpu.VMEM((BLK, 2048), BF16),
            pltpu.SemaphoreType.DMA((8,)),
        ],
        compiler_params=pltpu.CompilerParams(vmem_limit_bytes=48 * 1024 * 1024),
        cost_estimate=pl.CostEstimate(
            flops=slots * 1_200_000_000, bytes_accessed=16 * 1024 * 1024, transcendentals=0
        ),
        name="layer",
    )(up_ids, down_ids, live, *acts, *carried, *weights)
    return outs[:2], outs[2:]


def tables(owner, up_rows, down_cols):
    zh, x, c = (lax.axis_index(a) for a in ("zh", "x", "c"))
    y, zl = lax.axis_index("y"), lax.axis_index("zl")
    me = y * 4 + zl
    count = owner.shape[0]
    f = jnp.arange(count, dtype=jnp.int32)
    earlier = (owner[None, :] == me) & (f[None, :] < f[:, None])
    rank = jnp.sum(earlier.astype(jnp.int32), 1)
    slot = c * HALF + jnp.arange(HALF, dtype=jnp.int32)
    select = ((owner == me)[None, :] & (rank[None, :] == slot[:, None])).astype(jnp.int32)
    b = jnp.arange(16, dtype=jnp.int32)
    held = (zh ^ ((b // 2) % 2)) * 8 + ((x - b // 4) % 4) * 2 + (c ^ (b % 2))

    def ids(table):
        raw = jnp.sum(select[:, :, None] * jnp.take(table, held, axis=1)[None], 1)
        home = raw // 2
        return (((y - home // 4) % 4) * 4 + (zl - home % 4) % 4) * 2 + raw % 2

    live = jnp.sum(select, 1).astype(F32)
    return ids(up_rows), ids(down_cols), live


def add(*values):
    return sum(v.astype(F32) for v in values)


def shards(tokens, cotangent, gate_blocks, up_blocks, down_blocks, owner, up_rows, down_cols):
    c = lax.axis_index("c")
    up_ids, down_ids, live = tables(owner, up_rows, down_cols)

    acts = jnp.stack([tokens, cotangent]).reshape(2, BLK, 2, BLK).transpose(2, 0, 1, 3)
    line = jnp.concatenate([acts] + [rot(acts, "zl", k) for k in (1, 2, 3)])
    ring = [line] + [rot(line, "y", k) for k in (1, 2, 3)]
    ring = ring + [rot(v, "c", 1) for v in ring]

    packed = jnp.stack([gate_blocks, up_blocks, down_blocks], 1)
    mine = lax.dynamic_slice_in_dim(packed, c * HALF, HALF, 0)
    theirs = lax.dynamic_slice_in_dim(packed, (1 - c) * HALF, HALF, 0)
    base = jnp.stack([mine, rot(theirs, "c", 1)])

    size = HALF // CHUNKS
    parts = ()
    sums = []
    for n in range(CHUNKS):
        take = slice(n * size, (n + 1) * size)
        near = base[:, take]
        far = rot(near, "zh", 1)
        weights = [near, far]
        for k in (1, 2, 3):
            weights += [rot(near, "x", k), rot(far, "x", k)]
        parts, grads = layer(
            n == 0, n == CHUNKS - 1, up_ids[take], down_ids[take], live[take], ring, parts, weights
        )
        far_sum = add(grads[1], *[rot(grads[2 * k + 1], "x", -k) for k in (1, 2, 3)]).astype(BF16)
        near_sum = add(grads[0], *[rot(grads[2 * k], "x", -k) for k in (1, 2, 3)])
        sums.append(add(near_sum, rot(far_sum, "zh", 1)))
    total = jnp.concatenate(sums, 1)
    received = rot(total[1].astype(BF16), "c", 1).astype(F32)
    lower = jnp.where(c == 0, total[0], received)
    upper = jnp.where(c == 0, received, total[0])
    grads = [jnp.concatenate([lower[:, i], upper[:, i]]) for i in range(3)]

    both = add(parts[0], rot(parts[1], "c", 1)).astype(BF16)
    both = both.reshape(4, 8, 2, BLK, BLK)
    line = add(both[0], *[rot(both[k], "y", -k) for k in (1, 2, 3)]).astype(BF16)
    line = line.reshape(4, 2, 2, BLK, BLK)
    done = add(line[0], *[rot(line[k], "zl", -k) for k in (1, 2, 3)]).astype(BF16)
    done = done.transpose(1, 2, 0, 3).reshape(2, BLK, 2 * BLK)
    return (done[0], done[1], *grads)


def solution(mesh):
    fine = Mesh(mesh.devices.reshape(2, 4, 2, 4, 4), ("zh", "x", "c", "y", "zl"))
    dp = ("zh", "x", "c")
    mp = ("y", "zl")
    return jax.shard_map(
        shards,
        mesh=fine,
        in_specs=(P(dp, mp), P(dp, mp), P(mp, dp, None), P(mp, dp, None), P(mp, None, dp), P(), P(), P()),
        out_specs=(P(dp, mp), P(dp, mp), P(mp, dp, None), P(mp, dp, None), P(mp, None, dp)),
        check_vma=False,
    )
```

time: 919 us -> 268 us (0.29); the launches traced: 907 us -> 267 us
  waiting for transfers between devices: 739 us -> 179 us
  local copies, waits for them, and re-layouts: 78.7 us -> 7.17 us
  matrix products: 57.2 us -> 0 us
  starting transfers between devices: 0.8 us -> 54.3 us
  Pallas kernels: 0 us -> 15.1 us
  between operations: 14.3 us -> 0.94 us
    reduce_scatter x4 -> x0, waiting for transfers between devices: 365 us -> none  [the longest x1 103 us: shards(): lax.psum_scatter(gate_part.astype(jnp.bfloat16), 'dp', scatter_dimension=...]
    all_gather x5 -> x0, waiting for transfers between devices: 353 us -> none  [the longest x1 73.2 us: shards(): lax.all_gather(up_blocks, 'dp', axis=1, tiled=True)]
    ppermute x0 -> x33, waiting for transfers between devices: none -> 179 us  [rot(): return lax.ppermute(value, axis, [(i, (i + step) % n) for i in range(n)])]
    dot_general x11 -> x0, matrix products: 57.2 us -> none  [the longest x2 13.4 us: place_blocks(): jnp.einsum('tsb,sk->tkb', terms.reshape(count, slots, block_size), flags,...]
    ppermute x0 -> x33, starting transfers between devices: none -> 54.3 us  [rot(): return lax.ppermute(value, axis, [(i, (i + step) % n) for i in range(n)])]
    reshape x5 -> x0, local copies, waits for them, and re-layouts: 22.2 us -> none  [the longest x2 18.9 us: place_blocks(): terms.reshape(count, slots, block_size)]
    unnamed x11 -> x0, waiting for transfers between devices: 20.2 us -> none
    pallas_call x0 -> x1, Pallas kernels: none -> 15.1 us  [layer(): pl.pallas_call(functools.partial(layer_kernel, first, last, slots), grid=...]
  transfers between devices with their start and end apart: 10 -> 33, of which waited for: 10 -> 18; matrix products, arithmetic and copies ran while one was open for 14% -> 4% of each run, Pallas kernels for 0% -> 0%
where the time goes in v1:
time: 268 us; the launch traced here: 267 us
  waiting for transfers between devices  179 us (67%)
  starting transfers between devices  54.3 us (20%)
  Pallas kernels  15.1 us (6%)
  other arithmetic  10.7 us (4%)
  local copies, waits for them, and re-layouts  7.17 us (3%)
    ppermute x33, waiting for transfers between devices, rot(): return lax.ppermute(value, axis, [(i, (i + step) % n) for i in range(n)])  179 us
    ppermute x33, starting transfers between devices, rot(): return lax.ppermute(value, axis, [(i, (i + step) % n) for i in range(n)])  54.3 us
    pallas_call x1, Pallas kernels, layer(): pl.pallas_call(functools.partial(layer_kernel, first, last, slots), grid=...  15.1 us
  transfers between devices with their start and end apart: 33, of which 18 were waited for; matrix products, arithmetic and copies ran while one was open for 4% of the time, Pallas kernels for 0%

profile of v1, /device:TPU:1, one launch (start us, length us, event | category | flops | bytes accessed | tf_op | source)
XLA Modules:
  0.0 266.8 jit_solution(12025791835142498690)
XLA Ops:
  2.9 5.3 %collective-permute-start.2 = (bf16[2,2,128,128]{3,2,1,0:T(8,128)(2,1)S(1)}, bf16[2,2,128,128]{3,2,1,0:T(8,128)(2,1)S(1)}, u32[]{:S(2)}, u32[]{:S(2)}) collective-permute-start(bf16[2,2,128,128]{3,2,1,0:T(8,128)(2,1)S(1)} %maximum_bitcast_fusion), channel_id=1, source_target_pairs={{0,3},{1,0},{2,1},{3,2},{4,7},{5,4},{6,5},{7,6},{8,11},{9,8},{10,9... | collective-permute-start | bytes 393224 | tf_op jit(solution)/shard_map/ppermute | solution.py:20
  10.5 1.2 collective-permute-start.10
  11.8 7.4 %collective-permute-done.1 = bf16[2,2,128,128]{3,2,1,0:T(8,128)(2,1)S(1)} collective-permute-done((bf16[2,2,128,128]{3,2,1,0:T(8,128)(2,1)S(1)}, bf16[2,2,128,128]{3,2,1,0:T(8,128)(2,1)S(1)}, u32[]{:S(2)}, u32[]{:S(2)}) %collective-permute-start.1) | collective-permute-done | bytes 131104 | tf_op jit(solution)/shard_map/ppermute | solution.py:20
  20.4 2.7 %collective-permute-start.5 = (bf16[8,2,128,128]{3,2,1,0:T(8,128)(2,1)S(1)}, bf16[8,2,128,128]{3,2,1,0:T(8,128)(2,1)S(1)}, u32[]{:S(2)}, u32[]{:S(2)}) collective-permute-start(bf16[8,2,128,128]{3,2,1,0:T(8,128)(2,1)S(1)} %pad_maximum_fusion.2.refs_3_), channel_id=1, source_target_pairs={{0,12},{4,0},{8,4},{12,8},{1,13},{5,1},{9,5},{13,9},{2,14},{6,2},{... | collective-permute-start | bytes 1572872 | tf_op jit(solution)/shard_map/ppermute | solution.py:20
  24.2 2.0 pad_maximum_fusion.1.refs_11_
  26.2 2.5 collective-permute-start.16
  28.7 5.2 %collective-permute-start.11 = (bf16[2,4,3,128,128]{4,3,2,1,0:T(8,128)(2,1)}, bf16[2,4,3,128,128]{4,3,2,1,0:T(8,128)(2,1)}, u32[]{:S(2)}, u32[]{:S(2)}) collective-permute-start(bf16[2,4,3,128,128]{4,3,2,1,0:T(8,128)(2,1)} %pad_maximum_fusion.1.refs_11_), channel_id=1, source_target_pairs={{0,128},{128,0},{1,129},{129,1},{2,130},{130,2},{3,131},{131,3},{4... | collective-permute-start | bytes 2359304 | tf_op jit(solution)/shard_map/ppermute | solution.py:20
  33.9 11.7 %collective-permute-done.5.refs_6_ = bf16[8,2,128,128]{3,2,1,0:T(8,128)(2,1)S(1)} collective-permute-done((bf16[8,2,128,128]{3,2,1,0:T(8,128)(2,1)S(1)}, bf16[8,2,128,128]{3,2,1,0:T(8,128)(2,1)S(1)}, u32[]{:S(2)}, u32[]{:S(2)}) %collective-permute-start.5) | collective-permute-done | bytes 524320 | tf_op jit(solution)/shard_map/ppermute | solution.py:20
  46.6 3.3 %collective-permute-done.3.refs_4_ = bf16[8,2,128,128]{3,2,1,0:T(8,128)(2,1)S(1)} collective-permute-done((bf16[8,2,128,128]{3,2,1,0:T(8,128)(2,1)S(1)}, bf16[8,2,128,128]{3,2,1,0:T(8,128)(2,1)S(1)}, u32[]{:S(2)}, u32[]{:S(2)}) %collective-permute-start.3) | collective-permute-done | bytes 524320 | tf_op jit(solution)/shard_map/ppermute | solution.py:20
  51.8 2.8 %collective-permute-start.14 = (bf16[2,4,3,128,128]{4,3,2,1,0:T(8,128)(2,1)}, bf16[2,4,3,128,128]{4,3,2,1,0:T(8,128)(2,1)S(1)}, u32[]{:S(2)}, u32[]{:S(2)}) collective-permute-start(bf16[2,4,3,128,128]{4,3,2,1,0:T(8,128)(2,1)} %pad_maximum_fusion.1.refs_11_), channel_id=1, source_target_pairs={{0,64},{32,96},{64,0},{96,32},{1,65},{33,97},{65,1},{97,33},{2,66}... | collective-permute-start | bytes 2359304 | tf_op jit(solution)/shard_map/ppermute | solution.py:20
  54.9 2.4 collective-permute-start.17
  58.4 14.2 %collective-permute-done.14.refs_15_ = bf16[2,4,3,128,128]{4,3,2,1,0:T(8,128)(2,1)S(1)} collective-permute-done((bf16[2,4,3,128,128]{4,3,2,1,0:T(8,128)(2,1)}, bf16[2,4,3,128,128]{4,3,2,1,0:T(8,128)(2,1)S(1)}, u32[]{:S(2)}, u32[]{:S(2)}) %collective-permute-start.14) | collective-permute-done | bytes 786464 | tf_op jit(solution)/shard_map/ppermute | solution.py:20
  72.6 17.7 %collective-permute-done.12.refs_13_ = bf16[2,4,3,128,128]{4,3,2,1,0:T(8,128)(2,1)S(1)} collective-permute-done((bf16[2,4,3,128,128]{4,3,2,1,0:T(8,128)(2,1)}, bf16[2,4,3,128,128]{4,3,2,1,0:T(8,128)(2,1)S(1)}, u32[]{:S(2)}, u32[]{:S(2)}) %collective-permute-start.12) | collective-permute-done | bytes 786464 | tf_op jit(solution)/shard_map/ppermute | solution.py:20
  90.3 16.0 %collective-permute-done.15.refs_16_ = bf16[2,4,3,128,128]{4,3,2,1,0:T(8,128)(2,1)S(1)} collective-permute-done((bf16[2,4,3,128,128]{4,3,2,1,0:T(8,128)(2,1)}, bf16[2,4,3,128,128]{4,3,2,1,0:T(8,128)(2,1)S(1)}, u32[]{:S(2)}, u32[]{:S(2)}) %collective-permute-start.15) | collective-permute-done | bytes 786464 | tf_op jit(solution)/shard_map/ppermute | solution.py:20
  106.4 17.2 %collective-permute-done.13.refs_14_ = bf16[2,4,3,128,128]{4,3,2,1,0:T(8,128)(2,1)S(1)} collective-permute-done((bf16[2,4,3,128,128]{4,3,2,1,0:T(8,128)(2,1)}, bf16[2,4,3,128,128]{4,3,2,1,0:T(8,128)(2,1)S(1)}, u32[]{:S(2)}, u32[]{:S(2)}) %collective-permute-start.13) | collective-permute-done | bytes 786464 | tf_op jit(solution)/shard_map/ppermute | solution.py:20
  124.5 15.1 %layer.1 = (bf16[32,2,128,128]{3,2,1,0:T(8,128)(2,1)}, bf16[32,2,128,128]{3,2,1,0:T(8,128)(2,1)}, bf16[2,4,3,128,128]{4,3,2,1,0:T(8,128)(2,1)S(1)}, bf16[2,4,3,1...) custom-call(s32[4,16]{1,0:T(4,128)S(1)} %get-tuple-element.58.refs_0, ...), custom_call_target="tpu_custom_call" | custom-call | flops 4800000000 | bytes 16777216 | tf_op jit(solution)/shard_map/layer/pallas_call | solution.py:117
  139.7 2.6 collective-permute-start.29
  142.4 2.7 %collective-permute-start.25 = (bf16[2,4,3,128,128]{4,3,2,1,0:T(8,128)(2,1)}, bf16[2,4,3,128,128]{4,3,2,1,0:T(8,128)(2,1)S(1)}, u32[]{:S(2)}, u32[]{:S(2)}) collective-permute-start(bf16[2,4,3,128,128]{4,3,2,1,0:T(8,128)(2,1)} %get-tuple-element.19), channel_id=1, source_target_pairs={{0,96},{32,0},{64,32},{96,64},{1,97},{33,1},{65,33},{97,65},{2,98}... | collective-permute-start | bytes 2359304 | tf_op jit(solution)/shard_map/ppermute | solution.py:20
  145.1 13.5 %collective-permute-done.28 = bf16[2,4,3,128,128]{4,3,2,1,0:T(8,128)(2,1)S(1)} collective-permute-done((bf16[2,4,3,128,128]{4,3,2,1,0:T(8,128)(2,1)}, bf16[2,4,3,128,128]{4,3,2,1,0:T(8,128)(2,1)S(1)}, u32[]{:S(2)}, u32[]{:S(2)}) %collective-permute-start.28) | collective-permute-done | bytes 786464 | tf_op jit(solution)/shard_map/ppermute | solution.py:20
  159.6 19.7 %collective-permute-done.30 = bf16[2,4,3,128,128]{4,3,2,1,0:T(8,128)(2,1)S(1)} collective-permute-done((bf16[2,4,3,128,128]{4,3,2,1,0:T(8,128)(2,1)}, bf16[2,4,3,128,128]{4,3,2,1,0:T(8,128)(2,1)S(1)}, u32[]{:S(2)}, u32[]{:S(2)}) %collective-permute-start.30) | collective-permute-done | bytes 786464 | tf_op jit(solution)/shard_map/ppermute | solution.py:20
  179.9 5.3 %collective-permute-start.31 = (bf16[2,4,3,128,128]{4,3,2,1,0:T(8,128)(2,1)S(1)}, bf16[2,4,3,128,128]{4,3,2,1,0:T(8,128)(2,1)S(1)}, u32[]{:S(2)}, u32[]{:S(2)}) collective-permute-start(bf16[2,4,3,128,128]{4,3,2,1,0:T(8,128)(2,1)S(1)} %add_convert_fusion.1), channel_id=1, source_target_pairs={{0,128},{128,0},{1,129},{129,1},{2,130},{130,2},{3,131},{131,3},{4... | collective-permute-start | bytes 2359304 | tf_op jit(solution)/shard_map/ppermute | solution.py:20
  186.2 6.1 %collective-permute-done.25 = bf16[2,4,3,128,128]{4,3,2,1,0:T(8,128)(2,1)S(1)} collective-permute-done((bf16[2,4,3,128,128]{4,3,2,1,0:T(8,128)(2,1)}, bf16[2,4,3,128,128]{4,3,2,1,0:T(8,128)(2,1)S(1)}, u32[]{:S(2)}, u32[]{:S(2)}) %collective-permute-start.25) | collective-permute-done | bytes 786464 | tf_op jit(solution)/shard_map/ppermute | solution.py:20
  193.3 18.1 %collective-permute-done.27 = bf16[2,4,3,128,128]{4,3,2,1,0:T(8,128)(2,1)S(1)} collective-permute-done((bf16[2,4,3,128,128]{4,3,2,1,0:T(8,128)(2,1)}, bf16[2,4,3,128,128]{4,3,2,1,0:T(8,128)(2,1)S(1)}, u32[]{:S(2)}, u32[]{:S(2)}) %collective-permute-start.27) | collective-permute-done | bytes 786464 | tf_op jit(solution)/shard_map/ppermute | solution.py:20
  212.9 1.3 collective-permute-done.32
  214.5 2.4 add_convert_fusion
  220.1 10.4 %collective-permute-done.19 = bf16[8,2,128,128]{3,2,1,0:T(8,128)(2,1)S(1)} collective-permute-done((bf16[8,2,128,128]{3,2,1,0:T(8,128)(2,1)S(1)}, bf16[8,2,128,128]{3,2,1,0:T(8,128)(2,1)S(1)}, u32[]{:S(2)}, u32[]{:S(2)}) %collective-permute-start.19) | collective-permute-done | bytes 524320 | tf_op jit(solution)/shard_map/ppermute | solution.py:20
  230.5 12.4 %collective-permute-done.21 = bf16[8,2,128,128]{3,2,1,0:T(8,128)(2,1)S(1)} collective-permute-done((bf16[8,2,128,128]{3,2,1,0:T(8,128)(2,1)S(1)}, bf16[8,2,128,128]{3,2,1,0:T(8,128)(2,1)S(1)}, u32[]{:S(2)}, u32[]{:S(2)}) %collective-permute-start.21) | collective-permute-done | bytes 524320 | tf_op jit(solution)/shard_map/ppermute | solution.py:20
  243.4 1.3 collective-permute-start.22
  244.7 8.0 %collective-permute-start.24 = (bf16[2,2,128,128]{3,2,1,0:T(8,128)(2,1)S(1)}, bf16[2,2,128,128]{3,2,1,0:T(8,128)(2,1)S(1)}, u32[]{:S(2)}, u32[]{:S(2)}) collective-permute-start(bf16[2,2,128,128]{3,2,1,0:T(8,128)(2,1)S(1)} %get-tuple-element.52), channel_id=1, source_target_pairs={{0,1},{1,2},{2,3},{3,0},{4,5},{5,6},{6,7},{7,4},{8,9},{9,10},{10,1... | collective-permute-start | bytes 393224 | tf_op jit(solution)/shard_map/ppermute | solution.py:20
  252.7 3.0 %collective-permute-start.23 = (bf16[2,2,128,128]{3,2,1,0:T(8,128)(2,1)S(1)}, bf16[2,2,128,128]{3,2,1,0:T(8,128)(2,1)S(1)}, u32[]{:S(2)}, u32[]{:S(2)}) collective-permute-start(bf16[2,2,128,128]{3,2,1,0:T(8,128)(2,1)S(1)} %get-tuple-element.53), channel_id=1, source_target_pairs={{0,2},{1,3},{2,0},{3,1},{4,6},{5,7},{6,4},{7,5},{8,10},{9,11},{10,... | collective-permute-start | bytes 393224 | tf_op jit(solution)/shard_map/ppermute | solution.py:20
  257.4 2.6 collective-permute-done.24
  260.1 4.9 %collective-permute-done.23 = bf16[2,2,128,128]{3,2,1,0:T(8,128)(2,1)S(1)} collective-permute-done((bf16[2,2,128,128]{3,2,1,0:T(8,128)(2,1)S(1)}, bf16[2,2,128,128]{3,2,1,0:T(8,128)(2,1)S(1)}, u32[]{:S(2)}, u32[]{:S(2)}) %collective-permute-start.23) | collective-permute-done | bytes 131104 | tf_op jit(solution)/shard_map/ppermute | solution.py:20
  (95 shorter events, 24.5 us)
Async XLA Ops:
  2.9 8.9 %collective-permute-start.2 = (bf16[2,2,128,128]{3,2,1,0:T(8,128)(2,1)S(1)}, bf16[2,2,128,128]{3,2,1,0:T(8,128)(2,1)S(1)}, u32[]{:S(2)}, u32[]{:S(2)}) collective-permute-start(bf16[2,2,128,128]{3,2,1,0:T(8,128)(2,1)S(1)} %maximum_bitcast_fusion), channel_id=1, source_target_pairs={{0,3},{1,0},{2,1},{3,2},{4,7},{5,4},{6,5},{7,6},{8,11},{9,8},{10,9... | collective-permute-start | bytes 393224 | tf_op jit(solution)/shard_map/ppermute | solution.py:20
  8.1 11.0 %collective-permute-start.1 = (bf16[2,2,128,128]{3,2,1,0:T(8,128)(2,1)S(1)}, bf16[2,2,128,128]{3,2,1,0:T(8,128)(2,1)S(1)}, u32[]{:S(2)}, u32[]{:S(2)}) collective-permute-start(bf16[2,2,128,128]{3,2,1,0:T(8,128)(2,1)S(1)} %maximum_bitcast_fusion), channel_id=1, source_target_pairs={{0,2},{1,3},{2,0},{3,1},{4,6},{5,7},{6,4},{7,5},{8,10},{9,11},{10,... | collective-permute-start | bytes 393224 | tf_op jit(solution)/shard_map/ppermute | solution.py:20
  8.1 11.0 %collective-permute-start = (bf16[2,2,128,128]{3,2,1,0:T(8,128)(2,1)S(1)}, bf16[2,2,128,128]{3,2,1,0:T(8,128)(2,1)S(1)}, u32[]{:S(2)}, u32[]{:S(2)}) collective-permute-start(bf16[2,2,128,128]{3,2,1,0:T(8,128)(2,1)S(1)} %maximum_bitcast_fusion), channel_id=1, source_target_pairs={{0,1},{1,2},{2,3},{3,0},{4,5},{5,6},{6,7},{7,4},{8,9},{9,10},{10,1... | collective-permute-start | bytes 393224 | tf_op jit(solution)/shard_map/ppermute | solution.py:20
  10.5 13.7 %collective-permute-start.10 = (bf16[4,3,128,128]{3,2,1,0:T(8,128)(2,1)}, bf16[4,3,128,128]{3,2,1,0:T(8,128)(2,1)}, u32[]{:S(2)}, u32[]{:S(2)}) collective-permute-start(bf16[4,3,128,128]{3,2,1,0:T(8,128)(2,1)} %get-tuple-element.50), channel_id=1, source_target_pairs={{0,16},{16,0},{1,17},{17,1},{2,18},{18,2},{3,19},{19,3},{4,20},{20... | collective-permute-start | bytes 1179656 | tf_op jit(solution)/shard_map/ppermute | solution.py:20
  19.2 9.5 %collective-permute-start.6 = (bf16[8,2,128,128]{3,2,1,0:T(8,128)(2,1)S(1)}, bf16[8,2,128,128]{3,2,1,0:T(8,128)(2,1)S(1)}, u32[]{:S(2)}, u32[]{:S(2)}) collective-permute-start(bf16[8,2,128,128]{3,2,1,0:T(8,128)(2,1)S(1)} %pad_maximum_fusion.2.refs_3_), channel_id=1, source_target_pairs={{0,16},{16,0},{1,17},{17,1},{2,18},{18,2},{3,19},{19,3},{4,20},{20... | collective-permute-start | bytes 1572872 | tf_op jit(solution)/shard_map/ppermute | solution.py:20
  20.4 25.1 %collective-permute-start.5 = (bf16[8,2,128,128]{3,2,1,0:T(8,128)(2,1)S(1)}, bf16[8,2,128,128]{3,2,1,0:T(8,128)(2,1)S(1)}, u32[]{:S(2)}, u32[]{:S(2)}) collective-permute-start(bf16[8,2,128,128]{3,2,1,0:T(8,128)(2,1)S(1)} %pad_maximum_fusion.2.refs_3_), channel_id=1, source_target_pairs={{0,12},{4,0},{8,4},{12,8},{1,13},{5,1},{9,5},{13,9},{2,14},{6,2},{... | collective-permute-start | bytes 1572872 | tf_op jit(solution)/shard_map/ppermute | solution.py:20
  23.2 23.4 %collective-permute-start.4 = (bf16[8,2,128,128]{3,2,1,0:T(8,128)(2,1)S(1)}, bf16[8,2,128,128]{3,2,1,0:T(8,128)(2,1)S(1)}, u32[]{:S(2)}, u32[]{:S(2)}) collective-permute-start(bf16[8,2,128,128]{3,2,1,0:T(8,128)(2,1)S(1)} %pad_maximum_fusion.2.refs_3_), channel_id=1, source_target_pairs={{0,8},{4,12},{8,0},{12,4},{1,9},{5,13},{9,1},{13,5},{2,10},{6,14},... | collective-permute-start | bytes 1572872 | tf_op jit(solution)/shard_map/ppermute | solution.py:20
  23.5 26.3 %collective-permute-start.3 = (bf16[8,2,128,128]{3,2,1,0:T(8,128)(2,1)S(1)}, bf16[8,2,128,128]{3,2,1,0:T(8,128)(2,1)S(1)}, u32[]{:S(2)}, u32[]{:S(2)}) collective-permute-start(bf16[8,2,128,128]{3,2,1,0:T(8,128)(2,1)S(1)} %pad_maximum_fusion.2.refs_3_), channel_id=1, source_target_pairs={{0,4},{4,8},{8,12},{12,0},{1,5},{5,9},{9,13},{13,1},{2,6},{6,10},{... | collective-permute-start | bytes 1572872 | tf_op jit(solution)/shard_map/ppermute | solution.py:20
  26.2 31.1 %collective-permute-start.16 = (bf16[2,4,3,128,128]{4,3,2,1,0:T(8,128)(2,1)}, bf16[2,4,3,128,128]{4,3,2,1,0:T(8,128)(2,1)}, u32[]{:S(2)}, u32[]{:S(2)}) collective-permute-start(bf16[2,4,3,128,128]{4,3,2,1,0:T(8,128)(2,1)} %pad_maximum_fusion.1.refs_11_), channel_id=1, source_target_pairs={{0,96},{32,0},{64,32},{96,64},{1,97},{33,1},{65,33},{97,65},{2,98}... | collective-permute-start | bytes 2359304 | tf_op jit(solution)/shard_map/ppermute | solution.py:20
  28.7 26.2 %collective-permute-start.11 = (bf16[2,4,3,128,128]{4,3,2,1,0:T(8,128)(2,1)}, bf16[2,4,3,128,128]{4,3,2,1,0:T(8,128)(2,1)}, u32[]{:S(2)}, u32[]{:S(2)}) collective-permute-start(bf16[2,4,3,128,128]{4,3,2,1,0:T(8,128)(2,1)} %pad_maximum_fusion.1.refs_11_), channel_id=1, source_target_pairs={{0,128},{128,0},{1,129},{129,1},{2,130},{130,2},{3,131},{131,3},{4... | collective-permute-start | bytes 2359304 | tf_op jit(solution)/shard_map/ppermute | solution.py:20
  45.6 6.2 %collective-permute-start.9 = (bf16[8,2,128,128]{3,2,1,0:T(8,128)(2,1)S(1)}, bf16[8,2,128,128]{3,2,1,0:T(8,128)(2,1)S(1)}, u32[]{:S(2)}, u32[]{:S(2)}) collective-permute-start(bf16[8,2,128,128]{3,2,1,0:T(8,128)(2,1)S(1)} %collective-permute-done.5.refs_6_), channel_id=1, source_target_pairs={{0,16},{16,0},{1,17},{17,1},{2,18},{18,2},{3,19},{19,3},{4,20},{20... | collective-permute-start | bytes 1572872 | tf_op jit(solution)/shard_map/ppermute | solution.py:20
  46.6 8.0 %collective-permute-start.8 = (bf16[8,2,128,128]{3,2,1,0:T(8,128)(2,1)S(1)}, bf16[8,2,128,128]{3,2,1,0:T(8,128)(2,1)}, u32[]{:S(2)}, u32[]{:S(2)}) collective-permute-start(bf16[8,2,128,128]{3,2,1,0:T(8,128)(2,1)S(1)} %collective-permute-done.4.refs_5_), channel_id=1, source_target_pairs={{0,16},{16,0},{1,17},{17,1},{2,18},{18,2},{3,19},{19,3},{4,20},{20... | collective-permute-start | bytes 1572872 | tf_op jit(solution)/shard_map/ppermute | solution.py:20
  49.9 7.4 %collective-permute-start.7 = (bf16[8,2,128,128]{3,2,1,0:T(8,128)(2,1)S(1)}, bf16[8,2,128,128]{3,2,1,0:T(8,128)(2,1)}, u32[]{:S(2)}, u32[]{:S(2)}) collective-permute-start(bf16[8,2,128,128]{3,2,1,0:T(8,128)(2,1)S(1)} %collective-permute-done.3.refs_4_), channel_id=1, source_target_pairs={{0,16},{16,0},{1,17},{17,1},{2,18},{18,2},{3,19},{19,3},{4,20},{20... | collective-permute-start | bytes 1572872 | tf_op jit(solution)/shard_map/ppermute | solution.py:20
  51.8 20.9 %collective-permute-start.14 = (bf16[2,4,3,128,128]{4,3,2,1,0:T(8,128)(2,1)}, bf16[2,4,3,128,128]{4,3,2,1,0:T(8,128)(2,1)S(1)}, u32[]{:S(2)}, u32[]{:S(2)}) collective-permute-start(bf16[2,4,3,128,128]{4,3,2,1,0:T(8,128)(2,1)} %pad_maximum_fusion.1.refs_11_), channel_id=1, source_target_pairs={{0,64},{32,96},{64,0},{96,32},{1,65},{33,97},{65,1},{97,33},{2,66}... | collective-permute-start | bytes 2359304 | tf_op jit(solution)/shard_map/ppermute | solution.py:20
  54.6 35.7 %collective-permute-start.12 = (bf16[2,4,3,128,128]{4,3,2,1,0:T(8,128)(2,1)}, bf16[2,4,3,128,128]{4,3,2,1,0:T(8,128)(2,1)S(1)}, u32[]{:S(2)}, u32[]{:S(2)}) collective-permute-start(bf16[2,4,3,128,128]{4,3,2,1,0:T(8,128)(2,1)} %pad_maximum_fusion.1.refs_11_), channel_id=1, source_target_pairs={{0,32},{32,64},{64,96},{96,0},{1,33},{33,65},{65,97},{97,1},{2,34}... | collective-permute-start | bytes 2359304 | tf_op jit(solution)/shard_map/ppermute | solution.py:20
  54.9 35.4 %collective-permute-start.17 = (bf16[2,4,3,128,128]{4,3,2,1,0:T(8,128)(2,1)}, bf16[2,4,3,128,128]{4,3,2,1,0:T(8,128)(2,1)S(1)}, u32[]{:S(2)}, u32[]{:S(2)}) collective-permute-start(bf16[2,4,3,128,128]{4,3,2,1,0:T(8,128)(2,1)} %collective-permute-done.11.refs_12_), channel_id=1, source_target_pairs={{0,96},{32,0},{64,32},{96,64},{1,97},{33,1},{65,33},{97,65},{2,98}... | collective-permute-start | bytes 2359304 | tf_op jit(solution)/shard_map/ppermute | solution.py:20
  57.3 49.1 %collective-permute-start.15 = (bf16[2,4,3,128,128]{4,3,2,1,0:T(8,128)(2,1)}, bf16[2,4,3,128,128]{4,3,2,1,0:T(8,128)(2,1)S(1)}, u32[]{:S(2)}, u32[]{:S(2)}) collective-permute-start(bf16[2,4,3,128,128]{4,3,2,1,0:T(8,128)(2,1)} %collective-permute-done.11.refs_12_), channel_id=1, source_target_pairs={{0,64},{32,96},{64,0},{96,32},{1,65},{33,97},{65,1},{97,33},{2,66}... | collective-permute-start | bytes 2359304 | tf_op jit(solution)/shard_map/ppermute | solution.py:20
  57.3 66.3 %collective-permute-start.13 = (bf16[2,4,3,128,128]{4,3,2,1,0:T(8,128)(2,1)}, bf16[2,4,3,128,128]{4,3,2,1,0:T(8,128)(2,1)S(1)}, u32[]{:S(2)}, u32[]{:S(2)}) collective-permute-start(bf16[2,4,3,128,128]{4,3,2,1,0:T(8,128)(2,1)} %collective-permute-done.11.refs_12_), channel_id=1, source_target_pairs={{0,32},{32,64},{64,96},{96,0},{1,33},{33,65},{65,97},{97,1},{2,34}... | collective-permute-start | bytes 2359304 | tf_op jit(solution)/shard_map/ppermute | solution.py:20
  139.7 18.9 %collective-permute-start.28 = (bf16[2,4,3,128,128]{4,3,2,1,0:T(8,128)(2,1)}, bf16[2,4,3,128,128]{4,3,2,1,0:T(8,128)(2,1)S(1)}, u32[]{:S(2)}, u32[]{:S(2)}) collective-permute-start(bf16[2,4,3,128,128]{4,3,2,1,0:T(8,128)(2,1)} %get-tuple-element.23), channel_id=1, source_target_pairs={{0,96},{32,0},{64,32},{96,64},{1,97},{33,1},{65,33},{97,65},{2,98}... | collective-permute-start | bytes 2359304 | tf_op jit(solution)/shard_map/ppermute | solution.py:20
  139.7 19.8 %collective-permute-start.29 = (bf16[2,4,3,128,128]{4,3,2,1,0:T(8,128)(2,1)}, bf16[2,4,3,128,128]{4,3,2,1,0:T(8,128)(2,1)S(1)}, u32[]{:S(2)}, u32[]{:S(2)}) collective-permute-start(bf16[2,4,3,128,128]{4,3,2,1,0:T(8,128)(2,1)} %get-tuple-element.24), channel_id=1, source_target_pairs={{0,64},{32,96},{64,0},{96,32},{1,65},{33,97},{65,1},{97,33},{2,66}... | collective-permute-start | bytes 2359304 | tf_op jit(solution)/shard_map/ppermute | solution.py:20
  142.4 36.9 %collective-permute-start.30 = (bf16[2,4,3,128,128]{4,3,2,1,0:T(8,128)(2,1)}, bf16[2,4,3,128,128]{4,3,2,1,0:T(8,128)(2,1)S(1)}, u32[]{:S(2)}, u32[]{:S(2)}) collective-permute-start(bf16[2,4,3,128,128]{4,3,2,1,0:T(8,128)(2,1)} %get-tuple-element.25), channel_id=1, source_target_pairs={{0,32},{32,64},{64,96},{96,0},{1,33},{33,65},{65,97},{97,1},{2,34}... | collective-permute-start | bytes 2359304 | tf_op jit(solution)/shard_map/ppermute | solution.py:20
  142.4 49.9 %collective-permute-start.25 = (bf16[2,4,3,128,128]{4,3,2,1,0:T(8,128)(2,1)}, bf16[2,4,3,128,128]{4,3,2,1,0:T(8,128)(2,1)S(1)}, u32[]{:S(2)}, u32[]{:S(2)}) collective-permute-start(bf16[2,4,3,128,128]{4,3,2,1,0:T(8,128)(2,1)} %get-tuple-element.19), channel_id=1, source_target_pairs={{0,96},{32,0},{64,32},{96,64},{1,97},{33,1},{65,33},{97,65},{2,98}... | collective-permute-start | bytes 2359304 | tf_op jit(solution)/shard_map/ppermute | solution.py:20
  145.1 48.3 %collective-permute-start.26 = (bf16[2,4,3,128,128]{4,3,2,1,0:T(8,128)(2,1)}, bf16[2,4,3,128,128]{4,3,2,1,0:T(8,128)(2,1)S(1)}, u32[]{:S(2)}, u32[]{:S(2)}) collective-permute-start(bf16[2,4,3,128,128]{4,3,2,1,0:T(8,128)(2,1)} %get-tuple-element.20), channel_id=1, source_target_pairs={{0,64},{32,96},{64,0},{96,32},{1,65},{33,97},{65,1},{97,33},{2,66}... | collective-permute-start | bytes 2359304 | tf_op jit(solution)/shard_map/ppermute | solution.py:20
  158.6 52.9 %collective-permute-start.27 = (bf16[2,4,3,128,128]{4,3,2,1,0:T(8,128)(2,1)}, bf16[2,4,3,128,128]{4,3,2,1,0:T(8,128)(2,1)S(1)}, u32[]{:S(2)}, u32[]{:S(2)}) collective-permute-start(bf16[2,4,3,128,128]{4,3,2,1,0:T(8,128)(2,1)} %get-tuple-element.21), channel_id=1, source_target_pairs={{0,32},{32,64},{64,96},{96,0},{1,33},{33,65},{65,97},{97,1},{2,34}... | collective-permute-start | bytes 2359304 | tf_op jit(solution)/shard_map/ppermute | solution.py:20
  179.9 31.6 %collective-permute-start.31 = (bf16[2,4,3,128,128]{4,3,2,1,0:T(8,128)(2,1)S(1)}, bf16[2,4,3,128,128]{4,3,2,1,0:T(8,128)(2,1)S(1)}, u32[]{:S(2)}, u32[]{:S(2)}) collective-permute-start(bf16[2,4,3,128,128]{4,3,2,1,0:T(8,128)(2,1)S(1)} %add_convert_fusion.1), channel_id=1, source_target_pairs={{0,128},{128,0},{1,129},{129,1},{2,130},{130,2},{3,131},{131,3},{4... | collective-permute-start | bytes 2359304 | tf_op jit(solution)/shard_map/ppermute | solution.py:20
  185.2 29.2 %collective-permute-start.18 = (bf16[32,2,128,128]{3,2,1,0:T(8,128)(2,1)}, bf16[32,2,128,128]{3,2,1,0:T(8,128)(2,1)}, u32[]{:S(2)}, u32[]{:S(2)}) collective-permute-start(bf16[32,2,128,128]{3,2,1,0:T(8,128)(2,1)} %get-tuple-element.17), channel_id=1, source_target_pairs={{0,16},{16,0},{1,17},{17,1},{2,18},{18,2},{3,19},{19,3},{4,20},{20... | collective-permute-start | bytes 6291464 | tf_op jit(solution)/shard_map/ppermute | solution.py:20
  217.0 13.5 %collective-permute-start.19 = (bf16[8,2,128,128]{3,2,1,0:T(8,128)(2,1)S(1)}, bf16[8,2,128,128]{3,2,1,0:T(8,128)(2,1)S(1)}, u32[]{:S(2)}, u32[]{:S(2)}) collective-permute-start(bf16[8,2,128,128]{3,2,1,0:T(8,128)(2,1)S(1)} %get-tuple-element.40), channel_id=1, source_target_pairs={{0,12},{4,0},{8,4},{12,8},{1,13},{5,1},{9,5},{13,9},{2,14},{6,2},{... | collective-permute-start | bytes 1572872 | tf_op jit(solution)/shard_map/ppermute | solution.py:20
  217.7 25.3 %collective-permute-start.21 = (bf16[8,2,128,128]{3,2,1,0:T(8,128)(2,1)S(1)}, bf16[8,2,128,128]{3,2,1,0:T(8,128)(2,1)S(1)}, u32[]{:S(2)}, u32[]{:S(2)}) collective-permute-start(bf16[8,2,128,128]{3,2,1,0:T(8,128)(2,1)S(1)} %get-tuple-element.41), channel_id=1, source_target_pairs={{0,4},{4,8},{8,12},{12,0},{1,5},{5,9},{9,13},{13,1},{2,6},{6,10},{... | collective-permute-start | bytes 1572872 | tf_op jit(solution)/shard_map/ppermute | solution.py:20
  218.8 24.2 %collective-permute-start.20 = (bf16[8,2,128,128]{3,2,1,0:T(8,128)(2,1)S(1)}, bf16[8,2,128,128]{3,2,1,0:T(8,128)(2,1)S(1)}, u32[]{:S(2)}, u32[]{:S(2)}) collective-permute-start(bf16[8,2,128,128]{3,2,1,0:T(8,128)(2,1)S(1)} %get-tuple-element.42), channel_id=1, source_target_pairs={{0,8},{4,12},{8,0},{12,4},{1,9},{5,13},{9,1},{13,5},{2,10},{6,14},... | collective-permute-start | bytes 1572872 | tf_op jit(solution)/shard_map/ppermute | solution.py:20
  243.4 14.0 %collective-permute-start.22 = (bf16[2,2,128,128]{3,2,1,0:T(8,128)(2,1)S(1)}, bf16[2,2,128,128]{3,2,1,0:T(8,128)(2,1)S(1)}, u32[]{:S(2)}, u32[]{:S(2)}) collective-permute-start(bf16[2,2,128,128]{3,2,1,0:T(8,128)(2,1)S(1)} %get-tuple-element.51), channel_id=1, source_target_pairs={{0,3},{1,0},{2,1},{3,2},{4,7},{5,4},{6,5},{7,6},{8,11},{9,8},{10,9... | collective-permute-start | bytes 393224 | tf_op jit(solution)/shard_map/ppermute | solution.py:20
  244.7 15.3 %collective-permute-start.24 = (bf16[2,2,128,128]{3,2,1,0:T(8,128)(2,1)S(1)}, bf16[2,2,128,128]{3,2,1,0:T(8,128)(2,1)S(1)}, u32[]{:S(2)}, u32[]{:S(2)}) collective-permute-start(bf16[2,2,128,128]{3,2,1,0:T(8,128)(2,1)S(1)} %get-tuple-element.52), channel_id=1, source_target_pairs={{0,1},{1,2},{2,3},{3,0},{4,5},{5,6},{6,7},{7,4},{8,9},{9,10},{10,1... | collective-permute-start | bytes 393224 | tf_op jit(solution)/shard_map/ppermute | solution.py:20
  252.7 12.2 %collective-permute-start.23 = (bf16[2,2,128,128]{3,2,1,0:T(8,128)(2,1)S(1)}, bf16[2,2,128,128]{3,2,1,0:T(8,128)(2,1)S(1)}, u32[]{:S(2)}, u32[]{:S(2)}) collective-permute-start(bf16[2,2,128,128]{3,2,1,0:T(8,128)(2,1)S(1)} %get-tuple-element.53), channel_id=1, source_target_pairs={{0,2},{1,3},{2,0},{3,1},{4,6},{5,7},{6,4},{7,5},{8,10},{9,11},{10,... | collective-permute-start | bytes 393224 | tf_op jit(solution)/shard_map/ppermute | solution.py:20
  (10 other events, 253.4 us)

commit v2 on v1

v2 whole, which is shorter than its diff:
```python
import functools

import jax
import jax.numpy as jnp
from jax import lax
from jax.experimental import pallas as pl
from jax.experimental.pallas import tpu as pltpu
from jax.sharding import Mesh, PartitionSpec as P

BF16 = jnp.bfloat16
F32 = jnp.float32
BLK = 128
HALF = 4
PLACES = [(0, 0), (0, 1), (1, 0), (1, 1), (2, 0), (2, 1), (3, 0), (4, 0)] + [(5 + p, j) for p in range(4) for j in (0, 1)]
PIECES = 9
CHUNKS = 2
LONG = 100_000_000_000


def rot(value, axis, step):
    n = lax.axis_size(axis)
    with jax.named_scope("Move_" + axis + str(step % n)):
        return lax.ppermute(value, axis, [(i, (i + step) % n) for i in range(n)])


def dot(a, b, ca, cb):
    return lax.dot_general(a, b, (((ca,), (cb,)), ((), ())), preferred_element_type=F32)


def layer_kernel(first, slots, *refs):
    up_ids, down_ids, live = refs[:3]
    acts = refs[3:5]
    at = 5
    carried = ()
    if not first:
        carried = refs[at : at + 2]
        at += 2 + 5
    weights = refs[at : at + PIECES]
    at += PIECES
    own_out, other_out = refs[at : at + 2]
    at += 2
    grads = refs[at : at + PIECES]
    at += PIECES
    xv, acc, pk, pg, wgu, wd, sems = refs[at:]
    s = pl.program_id(0)

    @pl.when(s == 0)
    def _():
        for i in range(2):
            pltpu.make_async_copy(acts[i], xv.at[i], sems.at[i]).start()
        acc[...] = jnp.zeros_like(acc)
        for i in range(2):
            pltpu.make_async_copy(acts[i], xv.at[i], sems.at[i]).wait()

    for b in range(16):
        u = up_ids[s, b]
        d = down_ids[s, b]
        cols = slice(b * BLK, (b + 1) * BLK)
        for c in range(2):
            rows = slice(c * BLK, (c + 1) * BLK)
            pk[rows, cols] = xv[c, u, 0]
            pg[rows, cols] = xv[c, d, 1]
        p, j = PLACES[b]
        wgu[cols, 0:BLK] = weights[p][j, 0, 0]
        wgu[cols, BLK : 2 * BLK] = weights[p][j, 0, 1]
        wd[:, cols] = weights[p][j, 0, 2]

    alive = live[s]
    gate_up = dot(pk[...], wgu[...], 1, 0)
    gate = gate_up[:, :BLK]
    up = gate_up[:, BLK:]
    grad_hidden = alive * dot(pg[...], wd[...], 1, 1)
    sig = jax.nn.sigmoid(gate)
    hidden = (alive * gate * sig * up).astype(BF16)
    up_term = (grad_hidden * gate * sig).astype(BF16)
    gate_term = (grad_hidden * up * sig * (1.0 + gate * (1.0 - sig))).astype(BF16)
    terms = jnp.concatenate([gate_term, up_term], axis=1)

    for q in range(4):
        cols = slice(q * 512, (q + 1) * 512)
        out_terms = dot(hidden, wd[:, cols], 1, 0)
        in_terms = dot(terms, wgu[cols, :], 1, 1)
        dgu = dot(pk[:, cols], terms, 0, 0)
        dd = dot(hidden, pg[:, cols], 0, 0)
        for r in range(4):
            b = q * 4 + r
            part = slice(r * BLK, (r + 1) * BLK)
            u = up_ids[s, b]
            d = down_ids[s, b]
            acc[d, 0] += out_terms[:, part]
            acc[u, 1] += in_terms[:, part]
            p, j = PLACES[b]
            grads[p][j, 0, 0] = dgu[part, :BLK].astype(BF16)
            grads[p][j, 0, 1] = dgu[part, BLK:].astype(BF16)
            grads[p][j, 0, 2] = dd[:, part].astype(BF16)

    @pl.when(s == slots - 1)
    def _():
        own = acc[:, :, :BLK, :]
        other = acc[:, :, BLK:, :]
        if not first:
            own = own + carried[0][...].astype(F32)
            other = other + carried[1][...].astype(F32)
        own_out[...] = own.astype(BF16)
        other_out[...] = other.astype(BF16)


def layer(start, up_ids, down_ids, live, acts, carried, weights):
    slots = HALF // CHUNKS
    first = not carried
    smem = pl.BlockSpec(memory_space=pltpu.SMEM)
    anys = pl.BlockSpec(memory_space=pl.ANY)
    whole = pl.BlockSpec((32, 2, BLK, BLK), lambda s: (0, 0, 0, 0), pipeline_mode=pl.Buffered(1))
    near = [pl.BlockSpec((w.shape[0], 1, 3, BLK, BLK), lambda s: (0, start + s, 0, 0, 0)) for w in weights[:5]]
    far = [pl.BlockSpec((w.shape[0], 1, 3, BLK, BLK), lambda s: (0, s, 0, 0, 0)) for w in weights[5:]]
    part = jax.ShapeDtypeStruct((32, 2, BLK, BLK), BF16)
    outs = pl.pallas_call(
        functools.partial(layer_kernel, first, slots),
        grid=(slots,),
        in_specs=[smem] * 3 + [anys] * 2 + [whole] * len(carried[:2]) + [anys] * len(carried[2:]) + near + far,
        out_specs=[whole] * 2 + near + far,
        out_shape=[part] * 2 + [jax.ShapeDtypeStruct(w.shape, BF16) for w in weights],
        input_output_aliases={} if first else {7 + i: 2 + i for i in range(5)},
        scratch_shapes=[
            pltpu.VMEM((2, 32, 2, BLK, BLK), BF16),
            pltpu.VMEM((32, 2, 2 * BLK, BLK), F32),
            pltpu.VMEM((2 * BLK, 2048), BF16),
            pltpu.VMEM((2 * BLK, 2048), BF16),
            pltpu.VMEM((2048, 2 * BLK), BF16),
            pltpu.VMEM((BLK, 2048), BF16),
            pltpu.SemaphoreType.DMA((2,)),
        ],
        compiler_params=pltpu.CompilerParams(vmem_limit_bytes=60 * 1024 * 1024),
        cost_estimate=pl.CostEstimate(
            flops=LONG, bytes_accessed=16 * 1024 * 1024, transcendentals=0
        ),
        name="layer",
    )(up_ids, down_ids, live, *acts, *carried, *weights)
    return outs[:2], outs[2:7], outs[7:]


def tables(owner, up_rows, down_cols):
    zh, x, c = (lax.axis_index(a) for a in ("zh", "x", "c"))
    zl = lax.axis_index("zl")
    me = lax.axis_index("y") * 4 + zl
    count = owner.shape[0]
    f = jnp.arange(count, dtype=jnp.int32)
    earlier = (owner[None, :] == me) & (f[None, :] < f[:, None])
    rank = jnp.sum(earlier.astype(jnp.int32), 1)
    slot = c * HALF + jnp.arange(HALF, dtype=jnp.int32)
    select = ((owner == me)[None, :] & (rank[None, :] == slot[:, None])).astype(jnp.int32)
    away = jnp.array([0, 0, 1, 1, 3, 3, 2, 2] * 2, jnp.int32)
    b = jnp.arange(16, dtype=jnp.int32)
    held = (zh ^ (b // 8)) * 8 + ((x - away) % 4) * 2 + (c ^ (b % 2))

    def ids(table):
        raw = jnp.sum(select[:, :, None] * jnp.take(table, held, axis=1)[None], 1)
        home = raw // 2
        return ((home // 4) * 4 + (zl - home % 4) % 4) * 2 + raw % 2

    live = jnp.sum(select, 1).astype(F32)
    return ids(up_rows), ids(down_cols), live


def add(*values):
    return sum(v.astype(F32) for v in values)


tie = lax.optimization_barrier


def neighbours(value):
    return rot(value, "x", 1), rot(value, "x", -1)


def opposite(left, right):
    return rot(left[:1], "x", 1), rot(right[1:], "x", -1)


def to_opposite(parts):
    return rot(parts[3], "x", -1), rot(parts[4], "x", 1)


def to_neighbours(parts, from_right, from_left):
    left = jnp.concatenate([add(parts[1][:1], from_right).astype(BF16), parts[1][1:]])
    right = jnp.concatenate([parts[2][:1], add(parts[2][1:], from_left).astype(BF16)])
    return add(parts[0], rot(left, "x", -1), rot(right, "x", 1))


def shards(tokens, cotangent, gate_blocks, up_blocks, down_blocks, owner, up_rows, down_cols):
    c = lax.axis_index("c")
    up_ids, down_ids, live = tables(owner, up_rows, down_cols)

    blocks = (gate_blocks, up_blocks, down_blocks)
    mine = jnp.stack([lax.dynamic_slice_in_dim(v, c * HALF, HALF, 0) for v in blocks], 1)
    theirs = jnp.stack([lax.dynamic_slice_in_dim(v, (1 - c) * HALF, HALF, 0) for v in blocks], 1)
    base = jnp.stack([mine, rot(theirs, "c", 1)])

    acts = jnp.stack([tokens, cotangent]).reshape(2, BLK, 2, BLK).transpose(2, 0, 1, 3)
    base, acts, up_ids, down_ids, live = tie((base, acts, up_ids, down_ids, live))
    lines = [acts] + [rot(acts, "zl", k) for k in (1, 2, 3)]
    near = neighbours(base)
    line, base = tie((jnp.concatenate(lines), base))
    ring = lax.all_gather(line, "y", axis=0, tiled=True)

    size = HALF // CHUNKS
    takes = [slice(n * size, (n + 1) * size) for n in range(CHUNKS)]
    first, second = [rot(base[:, take], "zh", 1) for take in takes]
    near = [base, *near, *opposite(*near)]
    first, near = tie((first, near))
    first = [first, *[rot(first, "x", k) for k in (1, 3)]]
    second, first = tie((second, first))
    first += [rot(first[0], "x", 2)]
    second, ring = tie((second, ring))
    second = [second, *[rot(second, "x", k) for k in (1, 3, 2)]]
    ring = [ring, rot(ring, "c", 1)]

    take = takes[0]
    parts, near_parts, far_parts = layer(0, up_ids[take], down_ids[take], live[take], ring, (), near + first)
    first_sum = add(far_parts[0], *[rot(far_parts[p], "x", k) for p, k in ((1, 3), (2, 1), (3, 2))]).astype(BF16)
    take = takes[1]
    parts, near_parts, far_parts = layer(
        size, up_ids[take], down_ids[take], live[take], ring, (*parts, *near_parts), near + second
    )
    parts, far_parts, near_parts, first_sum = tie((parts, far_parts, near_parts, first_sum))
    both = add(parts[0], rot(parts[1], "c", 1)).astype(BF16)
    first_sum = rot(first_sum, "zh", 1)
    second_sum = [far_parts[0], *[rot(far_parts[p], "x", k) for p, k in ((1, 3), (2, 1), (3, 2))]]
    both, second_sum = tie((both, second_sum))
    line = lax.psum_scatter(both, "y", scatter_dimension=0, tiled=True)
    some, near_parts, first_sum = tie((second_sum[:3], near_parts, first_sum))
    crossed = to_opposite(near_parts)
    second_sum = rot(add(*some, second_sum[3]).astype(BF16), "zh", 1)
    near_sum = to_neighbours(near_parts, *crossed)
    line, first_sum = tie((line, first_sum))
    line = line.reshape(4, 2, 2, BLK, BLK)
    lines = [line[0], *[rot(line[k], "zl", -k) for k in (1, 2, 3)]]
    near_sum, lines, second_sum = tie((near_sum, lines, second_sum))
    done = add(*lines).astype(BF16)
    done = done.transpose(1, 2, 0, 3).reshape(2, BLK, 2 * BLK)
    far_sums = [first_sum, second_sum]

    total = add(near_sum, jnp.concatenate(far_sums, 1))
    received = rot(total[1].astype(BF16), "c", 1).astype(F32)
    lower = jnp.where(c == 0, total[0], received)
    upper = jnp.where(c == 0, received, total[0])
    grads = [jnp.concatenate([lower[:, i], upper[:, i]]) for i in range(3)]
    return (done[0], done[1], *grads)


def solution(mesh):
    fine = Mesh(mesh.devices.reshape(2, 4, 2, 4, 4), ("zh", "x", "c", "y", "zl"))
    dp = ("zh", "x", "c")
    mp = ("y", "zl")
    return jax.shard_map(
        shards,
        mesh=fine,
        in_specs=(P(dp, mp), P(dp, mp), P(mp, dp, None), P(mp, dp, None), P(mp, None, dp), P(), P(), P()),
        out_specs=(P(dp, mp), P(dp, mp), P(mp, dp, None), P(mp, dp, None), P(mp, None, dp)),
        check_vma=False,
    )
```

time: 268 us -> 231 us (0.86)
  waiting for transfers between devices: 179 us -> 108 us
  between operations: 0.94 us -> 14.6 us
  Pallas kernels: 15.1 us -> 24.8 us
  starting transfers between devices: 54.3 us -> 60.9 us
  local copies, waits for them, and re-layouts: 7.17 us -> 10.3 us
    ppermute x33 -> x34, waiting for transfers between devices: 179 us -> 108 us  [rot(): return lax.ppermute(value, axis, [(i, (i + step) % n) for i in range(n)])]
    pallas_call x1 -> x2, Pallas kernels: 15.1 us -> 24.8 us  [layer(): pl.pallas_call(functools.partial(layer_kernel, first, slots), grid=(slots...]
    ppermute x33 -> x34, starting transfers between devices: 54.3 us -> 60.8 us  [rot(): return lax.ppermute(value, axis, [(i, (i + step) % n) for i in range(n)])]
    slice x2 -> x9, local copies, waits for them, and re-layouts: 0.19 us -> 3.04 us  [the longest x1 1.13 us: shards(): lines = [line[0], *[rot(line[k], 'zl', -k) for k in (1, 2, 3)]]]
  transfers between devices with their start and end apart: 33 -> 36, of which waited for: 18 -> 20; matrix products, arithmetic and copies ran while one was open for 4% -> 6% of each run, Pallas kernels for 0% -> 11%
where the time goes in v2:
time: 231 us
  waiting for transfers between devices  108 us (47%)
  starting transfers between devices  60.9 us (26%)
  Pallas kernels  24.8 us (11%)
  between operations  14.6 us (6%)
  other arithmetic  12.1 us (5%)
  local copies, waits for them, and re-layouts  10.3 us (4%)
    ppermute x34, waiting for transfers between devices, rot(): return lax.ppermute(value, axis, [(i, (i + step) % n) for i in range(n)])  108 us
    ppermute x34, starting transfers between devices, rot(): return lax.ppermute(value, axis, [(i, (i + step) % n) for i in range(n)])  60.8 us
    pallas_call x2, Pallas kernels, layer(): pl.pallas_call(functools.partial(layer_kernel, first, slots), grid=(slots...  24.8 us
  transfers between devices with their start and end apart: 36, of which 20 were waited for; matrix products, arithmetic and copies ran while one was open for 6% of the time, Pallas kernels for 11%

profile of v2, /device:TPU:1, one launch (start us, length us, event | category | flops | bytes accessed | tf_op | source)
XLA Modules:
  0.0 230.6 jit_solution(11672431762747619729)
XLA Ops:
  9.5 3.3 %collective-permute-start = (bf16[4,3,128,128]{3,2,1,0:T(8,128)(2,1)S(1)}, bf16[4,3,128,128]{3,2,1,0:T(8,128)(2,1)S(1)}, u32[]{:S(2)}, u32[]{:S(2)}) collective-permute-start(bf16[4,3,128,128]{3,2,1,0:T(8,128)(2,1)S(1)} %pad_maximum_fusion.7), channel_id=1, source_target_pairs={{0,16},{16,0},{1,17},{17,1},{2,18},{18,2},{3,19},{19,3},{4,20},{20... | collective-permute-start | bytes 1179656 | tf_op jit(solution)/shard_map/Move_c1/ppermute | solution.py:23
  15.3 2.9 %collective-permute-start.2 = (bf16[2,2,128,128]{2,3,0,1:T(8,128)(2,1)S(1)}, bf16[2,2,128,128]{2,3,0,1:T(8,128)(2,1)S(1)}, u32[]{:S(2)}, u32[]{:S(2)}) collective-permute-start(bf16[2,2,128,128]{2,3,0,1:T(8,128)(2,1)S(1)} %maximum_bitcast_fusion.1), channel_id=1, source_target_pairs={{0,2},{1,3},{2,0},{3,1},{4,6},{5,7},{6,4},{7,5},{8,10},{9,11},{10,... | collective-permute-start | bytes 393224 | tf_op jit(solution)/shard_map/Move_zl2/ppermute | solution.py:23
  18.9 3.3 %collective-permute-done.1 = bf16[2,2,128,128]{2,3,0,1:T(8,128)(2,1)S(1)} collective-permute-done((bf16[2,2,128,128]{2,3,0,1:T(8,128)(2,1)S(1)}, bf16[2,2,128,128]{2,3,0,1:T(8,128)(2,1)S(1)}, u32[]{:S(2)}, u32[]{:S(2)}) %collective-permute-start.1) | collective-permute-done | bytes 131104 | tf_op jit(solution)/shard_map/Move_zl1/ppermute | solution.py:23
  22.2 5.2 %collective-permute-done.2 = bf16[2,2,128,128]{2,3,0,1:T(8,128)(2,1)S(1)} collective-permute-done((bf16[2,2,128,128]{2,3,0,1:T(8,128)(2,1)S(1)}, bf16[2,2,128,128]{2,3,0,1:T(8,128)(2,1)S(1)}, u32[]{:S(2)}, u32[]{:S(2)}) %collective-permute-start.2) | collective-permute-done | bytes 131104 | tf_op jit(solution)/shard_map/Move_zl2/ppermute | solution.py:23
  31.4 5.7 %collective-permute-start.5 = (bf16[2,2,3,128,128]{4,3,2,1,0:T(8,128)(2,1)S(1)}, bf16[2,2,3,128,128]{4,3,2,1,0:T(8,128)(2,1)S(1)}, u32[]{:S(2)}, u32[]{:S(2)}) collective-permute-start(bf16[2,2,3,128,128]{4,3,2,1,0:T(8,128)(2,1)S(1)} %get-tuple-element.181), channel_id=1, source_target_pairs={{0,128},{128,0},{1,129},{129,1},{2,130},{130,2},{3,131},{131,3},{4... | collective-permute-start | bytes 1179656 | tf_op jit(solution)/shard_map/Move_zh1/ppermute | solution.py:23
  37.1 10.7 %collective-permute-done.6.refs_6_.refs_13_ = bf16[2,4,3,128,128]{4,3,2,1,0:T(8,128)(2,1)S(1)} collective-permute-done((bf16[2,4,3,128,128]{4,3,2,1,0:T(8,128)(2,1)S(1)}, bf16[2,4,3,128,128]{4,3,2,1,0:T(8,128)(2,1)S(1)}, u32[]{:S(2)}, u32[]{:S(2)}) %collective-permute-start.6) | collective-permute-done | bytes 786464 | tf_op jit(solution)/shard_map/Move_x1/ppermute | solution.py:23
  48.7 1.9 collective-permute-start.9
  50.6 5.9 %collective-permute-start.4 = (bf16[2,2,3,128,128]{4,3,2,1,0:T(8,128)(2,1)S(1)}, bf16[2,2,3,128,128]{4,3,2,1,0:T(8,128)(2,1)}, u32[]{:S(2)}, u32[]{:S(2)}) collective-permute-start(bf16[2,2,3,128,128]{4,3,2,1,0:T(8,128)(2,1)S(1)} %get-tuple-element.182), channel_id=1, source_target_pairs={{0,128},{128,0},{1,129},{129,1},{2,130},{130,2},{3,131},{131,3},{4... | collective-permute-start | bytes 1179656 | tf_op jit(solution)/shard_map/Move_zh1/ppermute | solution.py:23
  60.6 12.3 %collective-permute-done.4.refs_17_ = bf16[2,2,3,128,128]{4,3,2,1,0:T(8,128)(2,1)} collective-permute-done((bf16[2,2,3,128,128]{4,3,2,1,0:T(8,128)(2,1)S(1)}, bf16[2,2,3,128,128]{4,3,2,1,0:T(8,128)(2,1)}, u32[]{:S(2)}, u32[]{:S(2)}) %collective-permute-start.4) | collective-permute-done | bytes 393248 | tf_op jit(solution)/shard_map/Move_zh1/ppermute | solution.py:23
  74.4 5.5 %collective-permute-start.13 = (bf16[2,2,3,128,128]{4,3,2,1,0:T(8,128)(2,1)}, bf16[2,2,3,128,128]{4,3,2,1,0:T(8,128)(2,1)}, u32[]{:S(2)}, u32[]{:S(2)}) collective-permute-start(bf16[2,2,3,128,128]{4,3,2,1,0:T(8,128)(2,1)} %copy-done.20), channel_id=1, source_target_pairs={{0,64},{32,96},{64,0},{96,32},{1,65},{33,97},{65,1},{97,33},{2,66}... | collective-permute-start | bytes 1179656 | tf_op jit(solution)/shard_map/Move_x2/ppermute | solution.py:23
  81.3 2.4 %collective-permute-start.15 = (bf16[2,2,3,128,128]{4,3,2,1,0:T(8,128)(2,1)}, bf16[2,2,3,128,128]{4,3,2,1,0:T(8,128)(2,1)}, u32[]{:S(2)}, u32[]{:S(2)}) collective-permute-start(bf16[2,2,3,128,128]{4,3,2,1,0:T(8,128)(2,1)} %collective-permute-done.4.refs_17_), channel_id=1, source_target_pairs={{0,96},{32,0},{64,32},{96,64},{1,97},{33,1},{65,33},{97,65},{2,98}... | collective-permute-start | bytes 1179656 | tf_op jit(solution)/shard_map/Move_x3/ppermute | solution.py:23
  83.7 5.9 %collective-permute-done.13.refs_13_ = bf16[2,2,3,128,128]{4,3,2,1,0:T(8,128)(2,1)} collective-permute-done((bf16[2,2,3,128,128]{4,3,2,1,0:T(8,128)(2,1)}, bf16[2,2,3,128,128]{4,3,2,1,0:T(8,128)(2,1)}, u32[]{:S(2)}, u32[]{:S(2)}) %collective-permute-start.13) | collective-permute-done | bytes 393248 | tf_op jit(solution)/shard_map/Move_x2/ppermute | solution.py:23
  89.6 11.6 %layer.2 = (bf16[32,2,128,128]{3,2,1,0:T(8,128)(2,1)}, bf16[32,2,128,128]{3,2,1,0:T(8,128)(2,1)}, bf16[2,4,3,128,128]{4,3,2,1,0:T(8,128)(2,1)}, bf16[2,4,3,128,1...) custom-call(s32[2,16]{1,0:T(2,128)} %get-tuple-element.197.refs_0_, ...), custom_call_target="tpu_custom_call" | custom-call | flops 99999997952 | bytes 16777216 | tf_op jit(solution)/shard_map/layer/pallas_call | solution.py:117
  101.2 2.5 %collective-permute-start.17 = (bf16[2,2,3,128,128]{4,3,2,1,0:T(8,128)(2,1)}, bf16[2,2,3,128,128]{4,3,2,1,0:T(8,128)(2,1)S(1)}, u32[]{:S(2)}, u32[]{:S(2)}) collective-permute-start(bf16[2,2,3,128,128]{4,3,2,1,0:T(8,128)(2,1)} %get-tuple-element.119), channel_id=1, source_target_pairs={{0,96},{32,0},{64,32},{96,64},{1,97},{33,1},{65,33},{97,65},{2,98}... | collective-permute-start | bytes 1179656 | tf_op jit(solution)/shard_map/Move_x3/ppermute | solution.py:23
  106.4 13.3 %layer.3 = (bf16[32,2,128,128]{3,2,1,0:T(8,128)(2,1)}, bf16[32,2,128,128]{3,2,1,0:T(8,128)(2,1)}, bf16[2,4,3,128,128]{4,3,2,1,0:T(8,128)(2,1)}, bf16[2,4,3,128,1...) custom-call(s32[2,16]{1,0:T(2,128)} %get-tuple-element.198.refs_0_, ...), custom_call_target="tpu_custom_call", output_to_operand_aliasing={{2}: (7, {}), {3}: (8, {}), {4}: (9, {}), {5}: (10, {}), {6... | custom-call | flops 99999997952 | bytes 16777216 | tf_op jit(solution)/shard_map/layer/pallas_call | solution.py:117
  119.7 2.6 %collective-permute-done.19 = bf16[2,2,3,128,128]{4,3,2,1,0:T(8,128)(2,1)S(1)} collective-permute-done((bf16[2,2,3,128,128]{4,3,2,1,0:T(8,128)(2,1)}, bf16[2,2,3,128,128]{4,3,2,1,0:T(8,128)(2,1)S(1)}, u32[]{:S(2)}, u32[]{:S(2)}) %collective-permute-start.19) | collective-permute-done | bytes 393248 | tf_op jit(solution)/shard_map/Move_x2/ppermute | solution.py:23
  122.6 2.9 %collective-permute-start.20 = (bf16[32,2,128,128]{3,2,1,0:T(8,128)(2,1)}, bf16[32,2,128,128]{3,2,1,0:T(8,128)(2,1)S(1)}, u32[]{:S(2)}, u32[]{:S(2)}) collective-permute-start(bf16[32,2,128,128]{3,2,1,0:T(8,128)(2,1)} %get-tuple-element.123), channel_id=1, source_target_pairs={{0,16},{16,0},{1,17},{17,1},{2,18},{18,2},{3,19},{19,3},{4,20},{20... | collective-permute-start | bytes 6291464 | tf_op jit(solution)/shard_map/Move_c1/ppermute | solution.py:23
  126.9 1.7 collective-permute-start.23
  129.5 3.8 %add_convert_fusion = bf16[32,2,128,128]{3,2,1,0:T(8,128)(2,1)} fusion(bf16[32,2,128,128]{3,2,1,0:T(8,128)(2,1)S(1)} %collective-permute-done.20, bf16[32,2,128,128]{3,2,1,0:T(8,128)(2,1)} %get-tuple-element.122), kind=kLoop, calls=%fused_computation.2 | loop fusion | flops 4194304 | bytes 6291456 | tf_op jit(solution)/shard_map/convert_element_type | solution.py:226
  133.2 3.1 %collective-permute-done.21 = bf16[2,2,3,128,128]{4,3,2,1,0:T(8,128)(2,1)S(1)} collective-permute-done((bf16[2,2,3,128,128]{4,3,2,1,0:T(8,128)(2,1)}, bf16[2,2,3,128,128]{4,3,2,1,0:T(8,128)(2,1)S(1)}, u32[]{:S(2)}, u32[]{:S(2)}) %collective-permute-start.21) | collective-permute-done | bytes 393248 | tf_op jit(solution)/shard_map/Move_x3/ppermute | solution.py:23
  136.4 10.8 %collective-permute-done.22 = bf16[2,2,3,128,128]{4,3,2,1,0:T(8,128)(2,1)S(1)} collective-permute-done((bf16[2,2,3,128,128]{4,3,2,1,0:T(8,128)(2,1)}, bf16[2,2,3,128,128]{4,3,2,1,0:T(8,128)(2,1)S(1)}, u32[]{:S(2)}, u32[]{:S(2)}) %collective-permute-start.22) | collective-permute-done | bytes 393248 | tf_op jit(solution)/shard_map/Move_x1/ppermute | solution.py:23
  147.1 2.0 collective-permute-start.24
  149.1 19.9 %collective-permute-done.24 = bf16[2,2,3,128,128]{4,3,2,1,0:T(8,128)(2,1)S(1)} collective-permute-done((bf16[2,2,3,128,128]{4,3,2,1,0:T(8,128)(2,1)S(1)}, bf16[2,2,3,128,128]{4,3,2,1,0:T(8,128)(2,1)S(1)}, u32[]{:S(2)}, u32[]{:S(2)}) %collective-permute-start.24) | collective-permute-done | bytes 393248 | tf_op jit(solution)/shard_map/Move_zh1/ppermute | solution.py:23
  170.5 7.0 %collective-permute-done.25 = bf16[1,4,3,128,128]{4,3,2,1,0:T(8,128)(2,1)S(1)} collective-permute-done((bf16[1,4,3,128,128]{4,3,2,1,0:T(8,128)(2,1)S(1)}, bf16[1,4,3,128,128]{4,3,2,1,0:T(8,128)(2,1)S(1)}, u32[]{:S(2)}, u32[]{:S(2)}) %collective-permute-start.25) | collective-permute-done | bytes 393248 | tf_op jit(solution)/shard_map/Move_x3/ppermute | solution.py:23
  179.9 2.3 add_convert_fusion.1
  182.2 5.1 %collective-permute-start.32 = (bf16[2,2,3,128,128]{4,3,2,1,0:T(8,128)(2,1)}, bf16[2,2,3,128,128]{4,3,2,1,0:T(8,128)(2,1)S(1)}, u32[]{:S(2)}, u32[]{:S(2)}) collective-permute-start(bf16[2,2,3,128,128]{4,3,2,1,0:T(8,128)(2,1)} %add_convert_fusion.1), channel_id=1, source_target_pairs={{0,128},{128,0},{1,129},{129,1},{2,130},{130,2},{3,131},{131,3},{4... | collective-permute-start | bytes 1179656 | tf_op jit(solution)/shard_map/Move_zh1/ppermute | solution.py:23
  188.5 3.3 %collective-permute-start.29 = (bf16[2,2,128,128]{3,2,1,0:T(8,128)(2,1)S(1)}, bf16[2,2,128,128]{3,2,1,0:T(8,128)(2,1)S(1)}, u32[]{:S(2)}, u32[]{:S(2)}) collective-permute-start(bf16[2,2,128,128]{3,2,1,0:T(8,128)(2,1)S(1)} %get-tuple-element.185), channel_id=1, source_target_pairs={{0,3},{1,0},{2,1},{3,2},{4,7},{5,4},{6,5},{7,6},{8,11},{9,8},{10,9... | collective-permute-start | bytes 393224 | tf_op jit(solution)/shard_map/Move_zl3/ppermute | solution.py:23
  191.8 2.2 collective-permute-done.26
  195.3 1.9 collective-permute-done.28
  198.7 3.4 %collective-permute-done.32 = bf16[2,2,3,128,128]{4,3,2,1,0:T(8,128)(2,1)S(1)} collective-permute-done((bf16[2,2,3,128,128]{4,3,2,1,0:T(8,128)(2,1)}, bf16[2,2,3,128,128]{4,3,2,1,0:T(8,128)(2,1)S(1)}, u32[]{:S(2)}, u32[]{:S(2)}) %collective-permute-start.32) | collective-permute-done | bytes 393248 | tf_op jit(solution)/shard_map/Move_zh1/ppermute | solution.py:23
  202.1 2.1 collective-permute-done.29
  204.2 14.0 %collective-permute-done.30 = bf16[2,2,128,128]{3,2,1,0:T(8,128)(2,1)S(1)} collective-permute-done((bf16[2,2,128,128]{3,2,1,0:T(8,128)(2,1)S(1)}, bf16[2,2,128,128]{3,2,1,0:T(8,128)(2,1)S(1)}, u32[]{:S(2)}, u32[]{:S(2)}) %collective-permute-start.30) | collective-permute-done | bytes 131104 | tf_op jit(solution)/shard_map/Move_zl2/ppermute | solution.py:23
  (151 shorter events, 35.7 us)
Async XLA Ops:
  7.2 65.7 %all-gather.2.cloned.1.call-start = ((), (), s32[]{:S(2)}) async-start(), calls=%async_computation.1 | async-start | bytes 2621440 | tf_op jit(solution)/shard_map/all_gather | solution.py:204
  15.3 12.1 %collective-permute-start.2 = (bf16[2,2,128,128]{2,3,0,1:T(8,128)(2,1)S(1)}, bf16[2,2,128,128]{2,3,0,1:T(8,128)(2,1)S(1)}, u32[]{:S(2)}, u32[]{:S(2)}) collective-permute-start(bf16[2,2,128,128]{2,3,0,1:T(8,128)(2,1)S(1)} %maximum_bitcast_fusion.1), channel_id=1, source_target_pairs={{0,2},{1,3},{2,0},{3,1},{4,6},{5,7},{6,4},{7,5},{8,10},{9,11},{10,... | collective-permute-start | bytes 393224 | tf_op jit(solution)/shard_map/Move_zl2/ppermute | solution.py:23
  18.2 9.3 %collective-permute-start.3 = (bf16[2,2,128,128]{2,3,0,1:T(8,128)(2,1)S(1)}, bf16[2,2,128,128]{2,3,0,1:T(8,128)(2,1)S(1)}, u32[]{:S(2)}, u32[]{:S(2)}) collective-permute-start(bf16[2,2,128,128]{2,3,0,1:T(8,128)(2,1)S(1)} %maximum_bitcast_fusion.1), channel_id=1, source_target_pairs={{0,3},{1,0},{2,1},{3,2},{4,7},{5,4},{6,5},{7,6},{8,11},{9,8},{10,9... | collective-permute-start | bytes 393224 | tf_op jit(solution)/shard_map/Move_zl3/ppermute | solution.py:23
  28.5 158.8 %reduce-scatter.2.cloned.1.call-start = ((), (), s32[]{:S(2)}) async-start(), calls=%async_computation.2 | async-start | bytes 2621440 | tf_op jit(solution)/shard_map/reduce_scatter | solution.py:230
  28.6 19.1 %collective-permute-start.6 = (bf16[2,4,3,128,128]{4,3,2,1,0:T(8,128)(2,1)S(1)}, bf16[2,4,3,128,128]{4,3,2,1,0:T(8,128)(2,1)S(1)}, u32[]{:S(2)}, u32[]{:S(2)}) collective-permute-start(bf16[2,4,3,128,128]{4,3,2,1,0:T(8,128)(2,1)S(1)} %pad_maximum_fusion.refs_5_.refs_12_), channel_id=1, source_target_pairs={{0,32},{32,64},{64,96},{96,0},{1,33},{33,65},{65,97},{97,1},{2,34}... | collective-permute-start | bytes 2359304 | tf_op jit(solution)/shard_map/Move_x1/ppermute | solution.py:23
  30.0 18.7 %collective-permute-start.7 = (bf16[2,4,3,128,128]{4,3,2,1,0:T(8,128)(2,1)S(1)}, bf16[2,4,3,128,128]{4,3,2,1,0:T(8,128)(2,1)S(1)}, u32[]{:S(2)}, u32[]{:S(2)}) collective-permute-start(bf16[2,4,3,128,128]{4,3,2,1,0:T(8,128)(2,1)S(1)} %pad_maximum_fusion.refs_5_.refs_12_), channel_id=1, source_target_pairs={{0,96},{32,0},{64,32},{96,64},{1,97},{33,1},{65,33},{97,65},{2,98}... | collective-permute-start | bytes 2359304 | tf_op jit(solution)/shard_map/Move_x3/ppermute | solution.py:23
  31.4 25.1 %collective-permute-start.5 = (bf16[2,2,3,128,128]{4,3,2,1,0:T(8,128)(2,1)S(1)}, bf16[2,2,3,128,128]{4,3,2,1,0:T(8,128)(2,1)S(1)}, u32[]{:S(2)}, u32[]{:S(2)}) collective-permute-start(bf16[2,2,3,128,128]{4,3,2,1,0:T(8,128)(2,1)S(1)} %get-tuple-element.181), channel_id=1, source_target_pairs={{0,128},{128,0},{1,129},{129,1},{2,130},{130,2},{3,131},{131,3},{4... | collective-permute-start | bytes 1179656 | tf_op jit(solution)/shard_map/Move_zh1/ppermute | solution.py:23
  47.8 9.9 %collective-permute-start.8 = (bf16[1,4,3,128,128]{4,3,2,1,0:T(8,128)(2,1)S(1)}, bf16[1,4,3,128,128]{4,3,2,1,0:T(8,128)(2,1)S(1)}, u32[]{:S(2)}, u32[]{:S(2)}) collective-permute-start(bf16[1,4,3,128,128]{4,3,2,1,0:T(8,128)(2,1)S(1)} %slice.124), channel_id=1, source_target_pairs={{0,32},{32,64},{64,96},{96,0},{1,33},{33,65},{65,97},{97,1},{2,34}... | collective-permute-start | bytes 1179656 | tf_op jit(solution)/shard_map/Move_x1/ppermute | solution.py:23
  48.7 9.2 %collective-permute-start.9 = (bf16[1,4,3,128,128]{4,3,2,1,0:T(8,128)(2,1)S(1)}, bf16[1,4,3,128,128]{4,3,2,1,0:T(8,128)(2,1)S(1)}, u32[]{:S(2)}, u32[]{:S(2)}) collective-permute-start(bf16[1,4,3,128,128]{4,3,2,1,0:T(8,128)(2,1)S(1)} %slice.125), channel_id=1, source_target_pairs={{0,96},{32,0},{64,32},{96,64},{1,97},{33,1},{65,33},{97,65},{2,98}... | collective-permute-start | bytes 1179656 | tf_op jit(solution)/shard_map/Move_x3/ppermute | solution.py:23
  50.6 22.3 %collective-permute-start.4 = (bf16[2,2,3,128,128]{4,3,2,1,0:T(8,128)(2,1)S(1)}, bf16[2,2,3,128,128]{4,3,2,1,0:T(8,128)(2,1)}, u32[]{:S(2)}, u32[]{:S(2)}) collective-permute-start(bf16[2,2,3,128,128]{4,3,2,1,0:T(8,128)(2,1)S(1)} %get-tuple-element.182), channel_id=1, source_target_pairs={{0,128},{128,0},{1,129},{129,1},{2,130},{130,2},{3,131},{131,3},{4... | collective-permute-start | bytes 1179656 | tf_op jit(solution)/shard_map/Move_zh1/ppermute | solution.py:23
  57.9 15.0 %collective-permute-start.10 = (bf16[2,2,3,128,128]{4,3,2,1,0:T(8,128)(2,1)S(1)}, bf16[2,2,3,128,128]{4,3,2,1,0:T(8,128)(2,1)S(1)}, u32[]{:S(2)}, u32[]{:S(2)}) collective-permute-start(bf16[2,2,3,128,128]{4,3,2,1,0:T(8,128)(2,1)S(1)} %collective-permute-done.5.refs_10_), channel_id=1, source_target_pairs={{0,32},{32,64},{64,96},{96,0},{1,33},{33,65},{65,97},{97,1},{2,34}... | collective-permute-start | bytes 1179656 | tf_op jit(solution)/shard_map/Move_x1/ppermute | solution.py:23
  59.1 13.8 %collective-permute-start.11 = (bf16[2,2,3,128,128]{4,3,2,1,0:T(8,128)(2,1)S(1)}, bf16[2,2,3,128,128]{4,3,2,1,0:T(8,128)(2,1)S(1)}, u32[]{:S(2)}, u32[]{:S(2)}) collective-permute-start(bf16[2,2,3,128,128]{4,3,2,1,0:T(8,128)(2,1)S(1)} %collective-permute-done.5.refs_10_), channel_id=1, source_target_pairs={{0,96},{32,0},{64,32},{96,64},{1,97},{33,1},{65,33},{97,65},{2,98}... | collective-permute-start | bytes 1179656 | tf_op jit(solution)/shard_map/Move_x3/ppermute | solution.py:23
  73.0 16.6 %collective-permute-start.12 = (bf16[32,2,128,128]{3,2,1,0:T(8,128)(2,1)}, bf16[32,2,128,128]{3,2,1,0:T(8,128)(2,1)}, u32[]{:S(2)}, u32[]{:S(2)}) collective-permute-start(bf16[32,2,128,128]{3,2,1,0:T(8,128)(2,1)} %all-gather.2.cloned.1.call-done.refs_3_), channel_id=1, source_target_pairs={{0,16},{16,0},{1,17},{17,1},{2,18},{18,2},{3,19},{19,3},{4,20},{20... | collective-permute-start | bytes 6291464 | tf_op jit(solution)/shard_map/Move_c1/ppermute | solution.py:23
  74.4 15.2 %collective-permute-start.13 = (bf16[2,2,3,128,128]{4,3,2,1,0:T(8,128)(2,1)}, bf16[2,2,3,128,128]{4,3,2,1,0:T(8,128)(2,1)}, u32[]{:S(2)}, u32[]{:S(2)}) collective-permute-start(bf16[2,2,3,128,128]{4,3,2,1,0:T(8,128)(2,1)} %copy-done.20), channel_id=1, source_target_pairs={{0,64},{32,96},{64,0},{96,32},{1,65},{33,97},{65,1},{97,33},{2,66}... | collective-permute-start | bytes 1179656 | tf_op jit(solution)/shard_map/Move_x2/ppermute | solution.py:23
  81.0 22.8 %collective-permute-start.14 = (bf16[2,2,3,128,128]{4,3,2,1,0:T(8,128)(2,1)}, bf16[2,2,3,128,128]{4,3,2,1,0:T(8,128)(2,1)S(1)}, u32[]{:S(2)}, u32[]{:S(2)}) collective-permute-start(bf16[2,2,3,128,128]{4,3,2,1,0:T(8,128)(2,1)} %collective-permute-done.4.refs_17_), channel_id=1, source_target_pairs={{0,32},{32,64},{64,96},{96,0},{1,33},{33,65},{65,97},{97,1},{2,34}... | collective-permute-start | bytes 1179656 | tf_op jit(solution)/shard_map/Move_x1/ppermute | solution.py:23
  81.3 24.1 %collective-permute-start.15 = (bf16[2,2,3,128,128]{4,3,2,1,0:T(8,128)(2,1)}, bf16[2,2,3,128,128]{4,3,2,1,0:T(8,128)(2,1)}, u32[]{:S(2)}, u32[]{:S(2)}) collective-permute-start(bf16[2,2,3,128,128]{4,3,2,1,0:T(8,128)(2,1)} %collective-permute-done.4.refs_17_), channel_id=1, source_target_pairs={{0,96},{32,0},{64,32},{96,64},{1,97},{33,1},{65,33},{97,65},{2,98}... | collective-permute-start | bytes 1179656 | tf_op jit(solution)/shard_map/Move_x3/ppermute | solution.py:23
  83.7 22.7 %collective-permute-start.16 = (bf16[2,2,3,128,128]{4,3,2,1,0:T(8,128)(2,1)}, bf16[2,2,3,128,128]{4,3,2,1,0:T(8,128)(2,1)}, u32[]{:S(2)}, u32[]{:S(2)}) collective-permute-start(bf16[2,2,3,128,128]{4,3,2,1,0:T(8,128)(2,1)} %collective-permute-done.4.refs_17_), channel_id=1, source_target_pairs={{0,64},{32,96},{64,0},{96,32},{1,65},{33,97},{65,1},{97,33},{2,66}... | collective-permute-start | bytes 1179656 | tf_op jit(solution)/shard_map/Move_x2/ppermute | solution.py:23
  101.2 18.5 %collective-permute-start.17 = (bf16[2,2,3,128,128]{4,3,2,1,0:T(8,128)(2,1)}, bf16[2,2,3,128,128]{4,3,2,1,0:T(8,128)(2,1)S(1)}, u32[]{:S(2)}, u32[]{:S(2)}) collective-permute-start(bf16[2,2,3,128,128]{4,3,2,1,0:T(8,128)(2,1)} %get-tuple-element.119), channel_id=1, source_target_pairs={{0,96},{32,0},{64,32},{96,64},{1,97},{33,1},{65,33},{97,65},{2,98}... | collective-permute-start | bytes 1179656 | tf_op jit(solution)/shard_map/Move_x3/ppermute | solution.py:23
  103.8 16.0 %collective-permute-start.18 = (bf16[2,2,3,128,128]{4,3,2,1,0:T(8,128)(2,1)}, bf16[2,2,3,128,128]{4,3,2,1,0:T(8,128)(2,1)S(1)}, u32[]{:S(2)}, u32[]{:S(2)}) collective-permute-start(bf16[2,2,3,128,128]{4,3,2,1,0:T(8,128)(2,1)} %get-tuple-element.120), channel_id=1, source_target_pairs={{0,32},{32,64},{64,96},{96,0},{1,33},{33,65},{65,97},{97,1},{2,34}... | collective-permute-start | bytes 1179656 | tf_op jit(solution)/shard_map/Move_x1/ppermute | solution.py:23
  103.8 18.6 %collective-permute-start.19 = (bf16[2,2,3,128,128]{4,3,2,1,0:T(8,128)(2,1)}, bf16[2,2,3,128,128]{4,3,2,1,0:T(8,128)(2,1)S(1)}, u32[]{:S(2)}, u32[]{:S(2)}) collective-permute-start(bf16[2,2,3,128,128]{4,3,2,1,0:T(8,128)(2,1)} %get-tuple-element.121), channel_id=1, source_target_pairs={{0,64},{32,96},{64,0},{96,32},{1,65},{33,97},{65,1},{97,33},{2,66}... | collective-permute-start | bytes 1179656 | tf_op jit(solution)/shard_map/Move_x2/ppermute | solution.py:23
  125.5 10.9 %collective-permute-start.21 = (bf16[2,2,3,128,128]{4,3,2,1,0:T(8,128)(2,1)}, bf16[2,2,3,128,128]{4,3,2,1,0:T(8,128)(2,1)S(1)}, u32[]{:S(2)}, u32[]{:S(2)}) collective-permute-start(bf16[2,2,3,128,128]{4,3,2,1,0:T(8,128)(2,1)} %get-tuple-element.125), channel_id=1, source_target_pairs={{0,96},{32,0},{64,32},{96,64},{1,97},{33,1},{65,33},{97,65},{2,98}... | collective-permute-start | bytes 1179656 | tf_op jit(solution)/shard_map/Move_x3/ppermute | solution.py:23
  126.9 20.2 %collective-permute-start.22 = (bf16[2,2,3,128,128]{4,3,2,1,0:T(8,128)(2,1)}, bf16[2,2,3,128,128]{4,3,2,1,0:T(8,128)(2,1)S(1)}, u32[]{:S(2)}, u32[]{:S(2)}) collective-permute-start(bf16[2,2,3,128,128]{4,3,2,1,0:T(8,128)(2,1)} %get-tuple-element.126), channel_id=1, source_target_pairs={{0,32},{32,64},{64,96},{96,0},{1,33},{33,65},{65,97},{97,1},{2,34}... | collective-permute-start | bytes 1179656 | tf_op jit(solution)/shard_map/Move_x1/ppermute | solution.py:23
  126.9 20.2 %collective-permute-start.23 = (bf16[2,2,3,128,128]{4,3,2,1,0:T(8,128)(2,1)}, bf16[2,2,3,128,128]{4,3,2,1,0:T(8,128)(2,1)S(1)}, u32[]{:S(2)}, u32[]{:S(2)}) collective-permute-start(bf16[2,2,3,128,128]{4,3,2,1,0:T(8,128)(2,1)} %get-tuple-element.127), channel_id=1, source_target_pairs={{0,64},{32,96},{64,0},{96,32},{1,65},{33,97},{65,1},{97,33},{2,66}... | collective-permute-start | bytes 1179656 | tf_op jit(solution)/shard_map/Move_x2/ppermute | solution.py:23
  147.1 21.8 %collective-permute-start.24 = (bf16[2,2,3,128,128]{4,3,2,1,0:T(8,128)(2,1)S(1)}, bf16[2,2,3,128,128]{4,3,2,1,0:T(8,128)(2,1)S(1)}, u32[]{:S(2)}, u32[]{:S(2)}) collective-permute-start(bf16[2,2,3,128,128]{4,3,2,1,0:T(8,128)(2,1)S(1)} %add_convert_fusion.4), channel_id=1, source_target_pairs={{0,128},{128,0},{1,129},{129,1},{2,130},{130,2},{3,131},{131,3},{4... | collective-permute-start | bytes 1179656 | tf_op jit(solution)/shard_map/Move_zh1/ppermute | solution.py:23
  169.0 8.6 %collective-permute-start.25 = (bf16[1,4,3,128,128]{4,3,2,1,0:T(8,128)(2,1)S(1)}, bf16[1,4,3,128,128]{4,3,2,1,0:T(8,128)(2,1)S(1)}, u32[]{:S(2)}, u32[]{:S(2)}) collective-permute-start(bf16[1,4,3,128,128]{4,3,2,1,0:T(8,128)(2,1)S(1)} %copy-done.23), channel_id=1, source_target_pairs={{0,96},{32,0},{64,32},{96,64},{1,97},{33,1},{65,33},{97,65},{2,98}... | collective-permute-start | bytes 1179656 | tf_op jit(solution)/shard_map/Move_x3/ppermute | solution.py:23
  169.7 9.9 %collective-permute-start.27 = (bf16[1,4,3,128,128]{4,3,2,1,0:T(8,128)(2,1)}, bf16[1,4,3,128,128]{4,3,2,1,0:T(8,128)(2,1)S(1)}, u32[]{:S(2)}, u32[]{:S(2)}) collective-permute-start(bf16[1,4,3,128,128]{4,3,2,1,0:T(8,128)(2,1)} %get-tuple-element.141), channel_id=1, source_target_pairs={{0,32},{32,64},{64,96},{96,0},{1,33},{33,65},{65,97},{97,1},{2,34}... | collective-permute-start | bytes 1179656 | tf_op jit(solution)/shard_map/Move_x1/ppermute | solution.py:23
  177.8 16.2 %collective-permute-start.26 = (bf16[2,4,3,128,128]{4,3,2,1,0:T(8,128)(2,1)S(1)}, bf16[2,4,3,128,128]{4,3,2,1,0:T(8,128)(2,1)S(1)}, u32[]{:S(2)}, u32[]{:S(2)}) collective-permute-start(bf16[2,4,3,128,128]{4,3,2,1,0:T(8,128)(2,1)S(1)} %pad_maximum_fusion.1), channel_id=1, source_target_pairs={{0,96},{32,0},{64,32},{96,64},{1,97},{33,1},{65,33},{97,65},{2,98}... | collective-permute-start | bytes 2359304 | tf_op jit(solution)/shard_map/Move_x3/ppermute | solution.py:23
  179.8 17.4 %collective-permute-start.28 = (bf16[2,4,3,128,128]{4,3,2,1,0:T(8,128)(2,1)S(1)}, bf16[2,4,3,128,128]{4,3,2,1,0:T(8,128)(2,1)}, u32[]{:S(2)}, u32[]{:S(2)}) collective-permute-start(bf16[2,4,3,128,128]{4,3,2,1,0:T(8,128)(2,1)S(1)} %pad_maximum_fusion.2), channel_id=1, source_target_pairs={{0,32},{32,64},{64,96},{96,0},{1,33},{33,65},{65,97},{97,1},{2,34}... | collective-permute-start | bytes 2359304 | tf_op jit(solution)/shard_map/Move_x1/ppermute | solution.py:23
  182.2 19.9 %collective-permute-start.32 = (bf16[2,2,3,128,128]{4,3,2,1,0:T(8,128)(2,1)}, bf16[2,2,3,128,128]{4,3,2,1,0:T(8,128)(2,1)S(1)}, u32[]{:S(2)}, u32[]{:S(2)}) collective-permute-start(bf16[2,2,3,128,128]{4,3,2,1,0:T(8,128)(2,1)} %add_convert_fusion.1), channel_id=1, source_target_pairs={{0,128},{128,0},{1,129},{129,1},{2,130},{130,2},{3,131},{131,3},{4... | collective-permute-start | bytes 1179656 | tf_op jit(solution)/shard_map/Move_zh1/ppermute | solution.py:23
  188.5 15.7 %collective-permute-start.29 = (bf16[2,2,128,128]{3,2,1,0:T(8,128)(2,1)S(1)}, bf16[2,2,128,128]{3,2,1,0:T(8,128)(2,1)S(1)}, u32[]{:S(2)}, u32[]{:S(2)}) collective-permute-start(bf16[2,2,128,128]{3,2,1,0:T(8,128)(2,1)S(1)} %get-tuple-element.185), channel_id=1, source_target_pairs={{0,3},{1,0},{2,1},{3,2},{4,7},{5,4},{6,5},{7,6},{8,11},{9,8},{10,9... | collective-permute-start | bytes 393224 | tf_op jit(solution)/shard_map/Move_zl3/ppermute | solution.py:23
  191.8 26.4 %collective-permute-start.30 = (bf16[2,2,128,128]{3,2,1,0:T(8,128)(2,1)S(1)}, bf16[2,2,128,128]{3,2,1,0:T(8,128)(2,1)S(1)}, u32[]{:S(2)}, u32[]{:S(2)}) collective-permute-start(bf16[2,2,128,128]{3,2,1,0:T(8,128)(2,1)S(1)} %get-tuple-element.184), channel_id=1, source_target_pairs={{0,2},{1,3},{2,0},{3,1},{4,6},{5,7},{6,4},{7,5},{8,10},{9,11},{10,... | collective-permute-start | bytes 393224 | tf_op jit(solution)/shard_map/Move_zl2/ppermute | solution.py:23
  194.0 24.1 %collective-permute-start.31 = (bf16[2,2,128,128]{3,2,1,0:T(8,128)(2,1)S(1)}, bf16[2,2,128,128]{3,2,1,0:T(8,128)(2,1)S(1)}, u32[]{:S(2)}, u32[]{:S(2)}) collective-permute-start(bf16[2,2,128,128]{3,2,1,0:T(8,128)(2,1)S(1)} %get-tuple-element.183), channel_id=1, source_target_pairs={{0,1},{1,2},{2,3},{3,0},{4,5},{5,6},{6,7},{7,4},{8,9},{9,10},{10,1... | collective-permute-start | bytes 393224 | tf_op jit(solution)/shard_map/Move_zl1/ppermute | solution.py:23
  (30 other events, 545.9 us)
Sparse Core Ops, SparseCore 0:
  28.7 36.9 all-gather.1
  147.3 31.5 reduce-scatter.1

commit v3 on v2

--- a/solution.py
+++ b/solution.py
@@ -14,6 +14,7 @@
 PLACES = [(0, 0), (0, 1), (1, 0), (1, 1), (2, 0), (2, 1), (3, 0), (4, 0)] + [(5 + p, j) for p in range(4) for j in (0, 1)]
 PIECES = 9
 CHUNKS = 2
+SHORT = 17_000_000_000
 LONG = 100_000_000_000
 
 
@@ -173,18 +174,39 @@
     return rot(value, "x", 1), rot(value, "x", -1)
 
 
-def opposite(left, right):
-    return rot(left[:1], "x", 1), rot(right[1:], "x", -1)
-
-
-def to_opposite(parts):
-    return rot(parts[3], "x", -1), rot(parts[4], "x", 1)
-
-
-def to_neighbours(parts, from_right, from_left):
-    left = jnp.concatenate([add(parts[1][:1], from_right).astype(BF16), parts[1][1:]])
-    right = jnp.concatenate([parts[2][:1], add(parts[2][1:], from_left).astype(BF16)])
-    return add(parts[0], rot(left, "x", -1), rot(right, "x", 1))
+def copy_kernel(*refs):
+    for source, target in zip(refs[: len(refs) // 2], refs[len(refs) // 2 :]):
+        target[...] = source[...]
+
+
+def add_kernel(left, right, from_right, from_left, new_left, new_right):
+    new_left[0] = (left[0].astype(F32) + from_right[0].astype(F32)).astype(BF16)
+    new_left[1] = left[1]
+    new_right[0] = right[0]
+    new_right[1] = (right[1].astype(F32) + from_left[0].astype(F32)).astype(BF16)
+
+
+def small(kernel, values, shapes, earlier=()):
+    whole = [pl.BlockSpec(memory_space=pltpu.VMEM)] * len(shapes)
+    count = len(values)
+
+    def body(*refs):
+        kernel(*refs[:count], *refs[count + len(earlier) :])
+
+    return pl.pallas_call(
+        body,
+        in_specs=[pl.BlockSpec(memory_space=pltpu.VMEM)] * count + [pl.BlockSpec(memory_space=pl.ANY)] * len(earlier),
+        out_specs=whole,
+        out_shape=[jax.ShapeDtypeStruct(v, BF16) for v in shapes],
+        compiler_params=pltpu.CompilerParams(vmem_limit_bytes=32 * 1024 * 1024),
+        cost_estimate=pl.CostEstimate(flops=SHORT, bytes_accessed=2 * 1024 * 1024, transcendentals=0),
+        name=kernel.__name__,
+    )(*values, *earlier)
+
+
+def halves_kernel(left, right, first, second):
+    first[...] = left[0:1]
+    second[...] = right[1:2]
 
 
 def shards(tokens, cotangent, gate_blocks, up_blocks, down_blocks, owner, up_rows, down_cols):
@@ -198,7 +220,7 @@
 
     acts = jnp.stack([tokens, cotangent]).reshape(2, BLK, 2, BLK).transpose(2, 0, 1, 3)
     base, acts, up_ids, down_ids, live = tie((base, acts, up_ids, down_ids, live))
-    lines = [acts] + [rot(acts, "zl", k) for k in (1, 2, 3)]
+    lines = [small(copy_kernel, (acts,), [acts.shape])[0]] + [rot(acts, "zl", k) for k in (1, 2, 3)]
     near = neighbours(base)
     line, base = tie((jnp.concatenate(lines), base))
     ring = lax.all_gather(line, "y", axis=0, tiled=True)
@@ -206,12 +228,11 @@
     size = HALF // CHUNKS
     takes = [slice(n * size, (n + 1) * size) for n in range(CHUNKS)]
     first, second = [rot(base[:, take], "zh", 1) for take in takes]
-    near = [base, *near, *opposite(*near)]
+    cut = small(halves_kernel, near, [(1, *base.shape[1:])] * 2)
+    near = [base, *near, rot(cut[0], "x", 1), rot(cut[1], "x", -1)]
     first, near = tie((first, near))
-    first = [first, *[rot(first, "x", k) for k in (1, 3)]]
-    second, first = tie((second, first))
-    first += [rot(first[0], "x", 2)]
-    second, ring = tie((second, ring))
+    first = [first, *[rot(first, "x", k) for k in (1, 3, 2)]]
+    second, first, ring = tie((second, first, ring))
     second = [second, *[rot(second, "x", k) for k in (1, 3, 2)]]
     ring = [ring, rot(ring, "c", 1)]
 
@@ -226,13 +247,14 @@
     both = add(parts[0], rot(parts[1], "c", 1)).astype(BF16)
     first_sum = rot(first_sum, "zh", 1)
     second_sum = [far_parts[0], *[rot(far_parts[p], "x", k) for p, k in ((1, 3), (2, 1), (3, 2))]]
-    both, second_sum = tie((both, second_sum))
     line = lax.psum_scatter(both, "y", scatter_dimension=0, tiled=True)
-    some, near_parts, first_sum = tie((second_sum[:3], near_parts, first_sum))
-    crossed = to_opposite(near_parts)
-    second_sum = rot(add(*some, second_sum[3]).astype(BF16), "zh", 1)
-    near_sum = to_neighbours(near_parts, *crossed)
-    line, first_sum = tie((line, first_sum))
+    sent = small(copy_kernel, near_parts[3:], [v.shape for v in near_parts[3:]], [both])
+    second_sum, sent, first_sum = tie((second_sum, sent, first_sum))
+    second_sum = add(*second_sum).astype(BF16)
+    crossed = rot(sent[0], "x", -1), rot(sent[1], "x", 1)
+    left, right = small(add_kernel, (*near_parts[1:3], *crossed), [near_parts[1].shape] * 2, [second_sum])
+    second_sum = rot(second_sum, "zh", 1)
+    near_sum = add(near_parts[0], rot(left, "x", -1), rot(right, "x", 1))
     line = line.reshape(4, 2, 2, BLK, BLK)
     lines = [line[0], *[rot(line[k], "zl", -k) for k in (1, 2, 3)]]
     near_sum, lines, second_sum = tie((near_sum, lines, second_sum))

time: 231 us -> 210 us (0.909)
  waiting for transfers between devices: 108 us -> 69 us
  starting transfers between devices: 60.9 us -> 77.4 us
    ppermute x34, waiting for transfers between devices: 108 us -> 60.8 us  [rot(): return lax.ppermute(value, axis, [(i, (i + step) % n) for i in range(n)])]
    ppermute x34, starting transfers between devices: 60.8 us -> 77.3 us  [rot(): return lax.ppermute(value, axis, [(i, (i + step) % n) for i in range(n)])]
    reduce_scatter x1, waiting for transfers between devices: 0.01 us -> 8.12 us  [shards(): line = lax.psum_scatter(both, 'y', scatter_dimension=0, tiled=True)]
    unnamed x56, local copies, waits for them, and re-layouts: 2.56 us -> 5.75 us
  transfers between devices with their start and end apart: 36 -> 36, of which waited for: 20 -> 16; matrix products, arithmetic and copies ran while one was open for 6% -> 5% of each run, Pallas kernels for 11% -> 12%
where the time goes in v3:
time: 210 us
  starting transfers between devices  77.4 us (37%)
  waiting for transfers between devices  69 us (33%)
  Pallas kernels  25.2 us (12%)
  between operations  14.6 us (7%)
  local copies, waits for them, and re-layouts  12.6 us (6%)
  other arithmetic  11.5 us (5%)
    ppermute x34, starting transfers between devices, rot(): return lax.ppermute(value, axis, [(i, (i + step) % n) for i in range(n)])  77.3 us
    ppermute x34, waiting for transfers between devices, rot(): return lax.ppermute(value, axis, [(i, (i + step) % n) for i in range(n)])  60.8 us
    pallas_call x2, Pallas kernels, layer(): pl.pallas_call(functools.partial(layer_kernel, first, slots), grid=(slots...  24.9 us
    reduce_scatter x1, waiting for transfers between devices, shards(): line = lax.psum_scatter(both, 'y', scatter_dimension=0, tiled=True)  8.12 us
    unnamed x56, local copies, waits for them, and re-layouts  5.75 us
  transfers between devices with their start and end apart: 36, of which 16 were waited for; matrix products, arithmetic and copies ran while one was open for 5% of the time, Pallas kernels for 12%

profile of v3, /device:TPU:1, one launch (start us, length us, event | category | flops | bytes accessed | tf_op | source)
XLA Modules:
  0.0 210.2 jit_solution(14256545668559392494)
XLA Ops:
  9.5 3.3 %collective-permute-start = (bf16[4,3,128,128]{3,2,1,0:T(8,128)(2,1)S(1)}, bf16[4,3,128,128]{3,2,1,0:T(8,128)(2,1)S(1)}, u32[]{:S(2)}, u32[]{:S(2)}) collective-permute-start(bf16[4,3,128,128]{3,2,1,0:T(8,128)(2,1)S(1)} %pad_maximum_fusion.5), channel_id=1, source_target_pairs={{0,16},{16,0},{1,17},{17,1},{2,18},{18,2},{3,19},{19,3},{4,20},{20... | collective-permute-start | bytes 1179656 | tf_op jit(solution)/shard_map/Move_c1/ppermute | solution.py:24
  15.5 2.7 %collective-permute-start.7 = (bf16[2,4,3,128,128]{4,3,2,1,0:T(8,128)(2,1)S(1)}, bf16[2,4,3,128,128]{4,3,2,1,0:T(8,128)(2,1)S(1)}, u32[]{:S(2)}, u32[]{:S(2)}) collective-permute-start(bf16[2,4,3,128,128]{4,3,2,1,0:T(8,128)(2,1)S(1)} %pad_maximum_fusion.refs_5_.refs_12_), channel_id=1, source_target_pairs={{0,96},{32,0},{64,32},{96,64},{1,97},{33,1},{65,33},{97,65},{2,98}... | collective-permute-start | bytes 2359304 | tf_op jit(solution)/shard_map/Move_x3/ppermute | solution.py:24
  18.2 2.9 %collective-permute-start.2 = (bf16[2,2,128,128]{3,2,1,0:T(8,128)(2,1)S(1)}, bf16[2,2,128,128]{3,2,1,0:T(8,128)(2,1)S(1)}, u32[]{:S(2)}, u32[]{:S(2)}) collective-permute-start(bf16[2,2,128,128]{3,2,1,0:T(8,128)(2,1)S(1)} %maximum_bitcast_fusion.1.refs_0_), channel_id=1, source_target_pairs={{0,2},{1,3},{2,0},{3,1},{4,6},{5,7},{6,4},{7,5},{8,10},{9,11},{10,... | collective-permute-start | bytes 393224 | tf_op jit(solution)/shard_map/Move_zl2/ppermute | solution.py:24
  21.8 2.7 %collective-permute-done.1 = bf16[2,2,128,128]{3,2,1,0:T(8,128)(2,1)S(1)} collective-permute-done((bf16[2,2,128,128]{3,2,1,0:T(8,128)(2,1)S(1)}, bf16[2,2,128,128]{3,2,1,0:T(8,128)(2,1)S(1)}, u32[]{:S(2)}, u32[]{:S(2)}) %collective-permute-start.1) | collective-permute-done | bytes 131104 | tf_op jit(solution)/shard_map/Move_zl1/ppermute | solution.py:24
  24.6 5.7 %collective-permute-done.2 = bf16[2,2,128,128]{3,2,1,0:T(8,128)(2,1)S(1)} collective-permute-done((bf16[2,2,128,128]{3,2,1,0:T(8,128)(2,1)S(1)}, bf16[2,2,128,128]{3,2,1,0:T(8,128)(2,1)S(1)}, u32[]{:S(2)}, u32[]{:S(2)}) %collective-permute-start.2) | collective-permute-done | bytes 131104 | tf_op jit(solution)/shard_map/Move_zl2/ppermute | solution.py:24
  31.3 5.7 %collective-permute-start.5 = (bf16[2,2,3,128,128]{4,3,2,1,0:T(8,128)(2,1)S(1)}, bf16[2,2,3,128,128]{4,3,2,1,0:T(8,128)(2,1)S(1)}, u32[]{:S(2)}, u32[]{:S(2)}) collective-permute-start(bf16[2,2,3,128,128]{4,3,2,1,0:T(8,128)(2,1)S(1)} %get-tuple-element.175), channel_id=1, source_target_pairs={{0,128},{128,0},{1,129},{129,1},{2,130},{130,2},{3,131},{131,3},{4... | collective-permute-start | bytes 1179656 | tf_op jit(solution)/shard_map/Move_zh1/ppermute | solution.py:24
  38.2 2.7 %collective-permute-start.9 = (bf16[1,4,3,128,128]{4,3,2,1,0:T(8,128)(2,1)S(1)}, bf16[1,4,3,128,128]{4,3,2,1,0:T(8,128)(2,1)S(1)}, u32[]{:S(2)}, u32[]{:S(2)}) collective-permute-start(bf16[1,4,3,128,128]{4,3,2,1,0:T(8,128)(2,1)S(1)} %get-tuple-element.85), channel_id=1, source_target_pairs={{0,96},{32,0},{64,32},{96,64},{1,97},{33,1},{65,33},{97,65},{2,98}... | collective-permute-start | bytes 1179656 | tf_op jit(solution)/shard_map/Move_x3/ppermute | solution.py:24
  40.8 4.0 %collective-permute-start.4 = (bf16[2,2,3,128,128]{4,3,2,1,0:T(8,128)(2,1)S(1)}, bf16[2,2,3,128,128]{4,3,2,1,0:T(8,128)(2,1)S(1)}, u32[]{:S(2)}, u32[]{:S(2)}) collective-permute-start(bf16[2,2,3,128,128]{4,3,2,1,0:T(8,128)(2,1)S(1)} %get-tuple-element.176), channel_id=1, source_target_pairs={{0,128},{128,0},{1,129},{129,1},{2,130},{130,2},{3,131},{131,3},{4... | collective-permute-start | bytes 1179656 | tf_op jit(solution)/shard_map/Move_zh1/ppermute | solution.py:24
  45.2 3.6 %collective-permute-done.8.refs_8_.refs_15_ = bf16[1,4,3,128,128]{4,3,2,1,0:T(8,128)(2,1)S(1)} collective-permute-done((bf16[1,4,3,128,128]{4,3,2,1,0:T(8,128)(2,1)S(1)}, bf16[1,4,3,128,128]{4,3,2,1,0:T(8,128)(2,1)S(1)}, u32[]{:S(2)}, u32[]{:S(2)}) %collective-permute-start.8) | collective-permute-done | bytes 393248 | tf_op jit(solution)/shard_map/Move_x1/ppermute | solution.py:24
  48.9 2.7 %collective-permute-start.11 = (bf16[2,2,3,128,128]{4,3,2,1,0:T(8,128)(2,1)S(1)}, bf16[2,2,3,128,128]{4,3,2,1,0:T(8,128)(2,1)S(1)}, u32[]{:S(2)}, u32[]{:S(2)}) collective-permute-start(bf16[2,2,3,128,128]{4,3,2,1,0:T(8,128)(2,1)S(1)} %collective-permute-done.5.refs_10_), channel_id=1, source_target_pairs={{0,96},{32,0},{64,32},{96,64},{1,97},{33,1},{65,33},{97,65},{2,98}... | collective-permute-start | bytes 1179656 | tf_op jit(solution)/shard_map/Move_x3/ppermute | solution.py:24
  52.4 3.1 %collective-permute-done.4.refs_17_ = bf16[2,2,3,128,128]{4,3,2,1,0:T(8,128)(2,1)S(1)} collective-permute-done((bf16[2,2,3,128,128]{4,3,2,1,0:T(8,128)(2,1)S(1)}, bf16[2,2,3,128,128]{4,3,2,1,0:T(8,128)(2,1)S(1)}, u32[]{:S(2)}, u32[]{:S(2)}) %collective-permute-start.4) | collective-permute-done | bytes 393248 | tf_op jit(solution)/shard_map/Move_zh1/ppermute | solution.py:24
  55.4 3.2 %collective-permute-done.10.refs_11_ = bf16[2,2,3,128,128]{4,3,2,1,0:T(8,128)(2,1)S(1)} collective-permute-done((bf16[2,2,3,128,128]{4,3,2,1,0:T(8,128)(2,1)S(1)}, bf16[2,2,3,128,128]{4,3,2,1,0:T(8,128)(2,1)S(1)}, u32[]{:S(2)}, u32[]{:S(2)}) %collective-permute-start.10) | collective-permute-done | bytes 393248 | tf_op jit(solution)/shard_map/Move_x1/ppermute | solution.py:24
  60.2 7.4 %collective-permute-done.12.refs_13_ = bf16[2,2,3,128,128]{4,3,2,1,0:T(8,128)(2,1)} collective-permute-done((bf16[2,2,3,128,128]{4,3,2,1,0:T(8,128)(2,1)S(1)}, bf16[2,2,3,128,128]{4,3,2,1,0:T(8,128)(2,1)}, u32[]{:S(2)}, u32[]{:S(2)}) %collective-permute-start.12) | collective-permute-done | bytes 393248 | tf_op jit(solution)/shard_map/Move_x2/ppermute | solution.py:24
  67.7 3.3 %collective-permute-start.13 = (bf16[32,2,128,128]{3,2,1,0:T(8,128)(2,1)}, bf16[32,2,128,128]{3,2,1,0:T(8,128)(2,1)S(1)}, u32[]{:S(2)}, u32[]{:S(2)}) collective-permute-start(bf16[32,2,128,128]{3,2,1,0:T(8,128)(2,1)} %all-gather.2.cloned.1.call-done.refs_3_), channel_id=1, source_target_pairs={{0,16},{16,0},{1,17},{17,1},{2,18},{18,2},{3,19},{19,3},{4,20},{20... | collective-permute-start | bytes 6291464 | tf_op jit(solution)/shard_map/Move_c1/ppermute | solution.py:24
  77.8 11.6 %layer.2 = (bf16[32,2,128,128]{3,2,1,0:T(8,128)(2,1)}, bf16[32,2,128,128]{3,2,1,0:T(8,128)(2,1)}, bf16[2,4,3,128,128]{4,3,2,1,0:T(8,128)(2,1)}, bf16[2,4,3,128,1...) custom-call(s32[2,16]{1,0:T(2,128)} %get-tuple-element.191.refs_0_, ...), custom_call_target="tpu_custom_call" | custom-call | flops 99999997952 | bytes 16777216 | tf_op jit(solution)/shard_map/layer/pallas_call | solution.py:118
  90.9 1.9 collective-permute-start.19
  94.2 13.3 %layer.3 = (bf16[32,2,128,128]{3,2,1,0:T(8,128)(2,1)}, bf16[32,2,128,128]{3,2,1,0:T(8,128)(2,1)}, bf16[2,4,3,128,128]{4,3,2,1,0:T(8,128)(2,1)}, bf16[2,4,3,128,1...) custom-call(s32[2,16]{1,0:T(2,128)} %get-tuple-element.192.refs_0_, ...), custom_call_target="tpu_custom_call", output_to_operand_aliasing={{2}: (7, {}), {3}: (8, {}), {4}: (9, {}), {5}: (10, {}), {6... | custom-call | flops 99999997952 | bytes 16777216 | tf_op jit(solution)/shard_map/layer/pallas_call | solution.py:118
  107.5 2.4 %collective-permute-done.19 = bf16[2,2,3,128,128]{4,3,2,1,0:T(8,128)(2,1)S(1)} collective-permute-done((bf16[2,2,3,128,128]{4,3,2,1,0:T(8,128)(2,1)}, bf16[2,2,3,128,128]{4,3,2,1,0:T(8,128)(2,1)S(1)}, u32[]{:S(2)}, u32[]{:S(2)}) %collective-permute-start.19) | collective-permute-done | bytes 393248 | tf_op jit(solution)/shard_map/Move_x2/ppermute | solution.py:24
  110.2 2.0 collective-permute-start.23
  112.2 4.0 %collective-permute-done.23 = bf16[32,2,128,128]{3,2,1,0:T(8,128)(2,1)S(1)} collective-permute-done((bf16[32,2,128,128]{3,2,1,0:T(8,128)(2,1)}, bf16[32,2,128,128]{3,2,1,0:T(8,128)(2,1)S(1)}, u32[]{:S(2)}, u32[]{:S(2)}) %collective-permute-start.23) | collective-permute-done | bytes 2097184 | tf_op jit(solution)/shard_map/Move_c1/ppermute | solution.py:24
  116.2 3.9 %add_convert_fusion.refs_2_ = bf16[32,2,128,128]{3,2,1,0:T(8,128)(2,1)} fusion(bf16[32,2,128,128]{3,2,1,0:T(8,128)(2,1)S(1)} %collective-permute-done.23, bf16[32,2,128,128]{3,2,1,0:T(8,128)(2,1)} %get-tuple-element.130), kind=kLoop, calls=%fused_computation.2 | loop fusion | flops 4194304 | bytes 6291456 | tf_op jit(solution)/shard_map/convert_element_type | solution.py:247
  123.2 8.4 %collective-permute-start.24 = (bf16[2,2,3,128,128]{4,3,2,1,0:T(8,128)(2,1)S(1)}, bf16[2,2,3,128,128]{4,3,2,1,0:T(8,128)(2,1)S(1)}, u32[]{:S(2)}, u32[]{:S(2)}) collective-permute-start(bf16[2,2,3,128,128]{4,3,2,1,0:T(8,128)(2,1)S(1)} %add_convert_fusion.2), channel_id=1, source_target_pairs={{0,128},{128,0},{1,129},{129,1},{2,130},{130,2},{3,131},{131,3},{4... | collective-permute-start | bytes 1179656 | tf_op jit(solution)/shard_map/Move_zh1/ppermute | solution.py:24
  131.6 2.3 %collective-permute-done.21 = bf16[2,2,3,128,128]{4,3,2,1,0:T(8,128)(2,1)S(1)} collective-permute-done((bf16[2,2,3,128,128]{4,3,2,1,0:T(8,128)(2,1)}, bf16[2,2,3,128,128]{4,3,2,1,0:T(8,128)(2,1)S(1)}, u32[]{:S(2)}, u32[]{:S(2)}) %collective-permute-start.21) | collective-permute-done | bytes 393248 | tf_op jit(solution)/shard_map/Move_x1/ppermute | solution.py:24
  133.9 6.8 %collective-permute-done.22 = bf16[2,2,3,128,128]{4,3,2,1,0:T(8,128)(2,1)S(1)} collective-permute-done((bf16[2,2,3,128,128]{4,3,2,1,0:T(8,128)(2,1)}, bf16[2,2,3,128,128]{4,3,2,1,0:T(8,128)(2,1)S(1)}, u32[]{:S(2)}, u32[]{:S(2)}) %collective-permute-start.22) | collective-permute-done | bytes 393248 | tf_op jit(solution)/shard_map/Move_x2/ppermute | solution.py:24
  142.5 6.5 %collective-permute-done.25.refs_2_ = bf16[1,4,3,128,128]{4,3,2,1,0:T(8,128)(2,1)S(1)} collective-permute-done((bf16[1,4,3,128,128]{4,3,2,1,0:T(8,128)(2,1)S(1)}, bf16[1,4,3,128,128]{4,3,2,1,0:T(8,128)(2,1)S(1)}, u32[]{:S(2)}, u32[]{:S(2)}) %collective-permute-start.25) | collective-permute-done | bytes 393248 | tf_op jit(solution)/shard_map/Move_x3/ppermute | solution.py:24
  148.9 2.7 %collective-permute-done.26.refs_3_ = bf16[1,4,3,128,128]{4,3,2,1,0:T(8,128)(2,1)S(1)} collective-permute-done((bf16[1,4,3,128,128]{4,3,2,1,0:T(8,128)(2,1)S(1)}, bf16[1,4,3,128,128]{4,3,2,1,0:T(8,128)(2,1)S(1)}, u32[]{:S(2)}, u32[]{:S(2)}) %collective-permute-start.26) | collective-permute-done | bytes 393248 | tf_op jit(solution)/shard_map/Move_x1/ppermute | solution.py:24
  153.4 7.6 %collective-permute-start.32 = (bf16[2,2,3,128,128]{4,3,2,1,0:T(8,128)(2,1)S(1)}, bf16[2,2,3,128,128]{4,3,2,1,0:T(8,128)(2,1)}, u32[]{:S(2)}, u32[]{:S(2)}) collective-permute-start(bf16[2,2,3,128,128]{4,3,2,1,0:T(8,128)(2,1)S(1)} %add_convert_fusion.1.refs_4_), channel_id=1, source_target_pairs={{0,128},{128,0},{1,129},{129,1},{2,130},{130,2},{3,131},{131,3},{4... | collective-permute-start | bytes 1179656 | tf_op jit(solution)/shard_map/Move_zh1/ppermute | solution.py:24
  161.0 8.1 %reduce-scatter.2.cloned.1.call-done = bf16[8,2,128,128]{3,2,1,0:T(8,128)(2,1)} async-done(((bf16[32,2,128,128]{3,2,1,0:T(8,128)(2,1)}), bf16[8,2,128,128]{3,2,1,0:T(8,128)(2,1)}) %reduce-scatter.2.cloned.1.call-update) | async-done | bytes 524304 | tf_op jit(solution)/shard_map/reduce_scatter | solution.py:250
  170.3 3.3 %collective-permute-start.29 = (bf16[2,2,128,128]{3,2,1,0:T(8,128)(2,1)S(1)}, bf16[2,2,128,128]{3,2,1,0:T(8,128)(2,1)S(1)}, u32[]{:S(2)}, u32[]{:S(2)}) collective-permute-start(bf16[2,2,128,128]{3,2,1,0:T(8,128)(2,1)S(1)} %get-tuple-element.179), channel_id=1, source_target_pairs={{0,3},{1,0},{2,1},{3,2},{4,7},{5,4},{6,5},{7,6},{8,11},{9,8},{10,9... | collective-permute-start | bytes 393224 | tf_op jit(solution)/shard_map/Move_zl3/ppermute | solution.py:24
  173.6 4.8 %collective-permute-start.30 = (bf16[2,2,128,128]{3,2,1,0:T(8,128)(2,1)S(1)}, bf16[2,2,128,128]{3,2,1,0:T(8,128)(2,1)S(1)}, u32[]{:S(2)}, u32[]{:S(2)}) collective-permute-start(bf16[2,2,128,128]{3,2,1,0:T(8,128)(2,1)S(1)} %get-tuple-element.178), channel_id=1, source_target_pairs={{0,2},{1,3},{2,0},{3,1},{4,6},{5,7},{6,4},{7,5},{8,10},{9,11},{10,... | collective-permute-start | bytes 393224 | tf_op jit(solution)/shard_map/Move_zl2/ppermute | solution.py:24
  178.4 7.1 %collective-permute-start.31 = (bf16[2,2,128,128]{3,2,1,0:T(8,128)(2,1)S(1)}, bf16[2,2,128,128]{3,2,1,0:T(8,128)(2,1)S(1)}, u32[]{:S(2)}, u32[]{:S(2)}) collective-permute-start(bf16[2,2,128,128]{3,2,1,0:T(8,128)(2,1)S(1)} %get-tuple-element.177), channel_id=1, source_target_pairs={{0,1},{1,2},{2,3},{3,0},{4,5},{5,6},{6,7},{7,4},{8,9},{9,10},{10,1... | collective-permute-start | bytes 393224 | tf_op jit(solution)/shard_map/Move_zl1/ppermute | solution.py:24
  187.0 8.6 %collective-permute-done.30 = bf16[2,2,128,128]{3,2,1,0:T(8,128)(2,1)S(1)} collective-permute-done((bf16[2,2,128,128]{3,2,1,0:T(8,128)(2,1)S(1)}, bf16[2,2,128,128]{3,2,1,0:T(8,128)(2,1)S(1)}, u32[]{:S(2)}, u32[]{:S(2)}) %collective-permute-start.30) | collective-permute-done | bytes 131104 | tf_op jit(solution)/shard_map/Move_zl2/ppermute | solution.py:24
  (148 shorter events, 37.3 us)
Async XLA Ops:
  7.2 60.4 %all-gather.2.cloned.1.call-start = ((), (), s32[]{:S(2)}) async-start(), calls=%async_computation.1 | async-start | bytes 2621440 | tf_op jit(solution)/shard_map/all_gather | solution.py:226
  15.5 21.6 %collective-permute-start.6 = (bf16[2,4,3,128,128]{4,3,2,1,0:T(8,128)(2,1)S(1)}, bf16[2,4,3,128,128]{4,3,2,1,0:T(8,128)(2,1)S(1)}, u32[]{:S(2)}, u32[]{:S(2)}) collective-permute-start(bf16[2,4,3,128,128]{4,3,2,1,0:T(8,128)(2,1)S(1)} %pad_maximum_fusion.refs_5_.refs_12_), channel_id=1, source_target_pairs={{0,32},{32,64},{64,96},{96,0},{1,33},{33,65},{65,97},{97,1},{2,34}... | collective-permute-start | bytes 2359304 | tf_op jit(solution)/shard_map/Move_x1/ppermute | solution.py:24
  15.5 21.5 %collective-permute-start.7 = (bf16[2,4,3,128,128]{4,3,2,1,0:T(8,128)(2,1)S(1)}, bf16[2,4,3,128,128]{4,3,2,1,0:T(8,128)(2,1)S(1)}, u32[]{:S(2)}, u32[]{:S(2)}) collective-permute-start(bf16[2,4,3,128,128]{4,3,2,1,0:T(8,128)(2,1)S(1)} %pad_maximum_fusion.refs_5_.refs_12_), channel_id=1, source_target_pairs={{0,96},{32,0},{64,32},{96,64},{1,97},{33,1},{65,33},{97,65},{2,98}... | collective-permute-start | bytes 2359304 | tf_op jit(solution)/shard_map/Move_x3/ppermute | solution.py:24
  18.2 12.1 %collective-permute-start.2 = (bf16[2,2,128,128]{3,2,1,0:T(8,128)(2,1)S(1)}, bf16[2,2,128,128]{3,2,1,0:T(8,128)(2,1)S(1)}, u32[]{:S(2)}, u32[]{:S(2)}) collective-permute-start(bf16[2,2,128,128]{3,2,1,0:T(8,128)(2,1)S(1)} %maximum_bitcast_fusion.1.refs_0_), channel_id=1, source_target_pairs={{0,2},{1,3},{2,0},{3,1},{4,6},{5,7},{6,4},{7,5},{8,10},{9,11},{10,... | collective-permute-start | bytes 393224 | tf_op jit(solution)/shard_map/Move_zl2/ppermute | solution.py:24
  21.1 9.2 %collective-permute-start.3 = (bf16[2,2,128,128]{3,2,1,0:T(8,128)(2,1)S(1)}, bf16[2,2,128,128]{3,2,1,0:T(8,128)(2,1)S(1)}, u32[]{:S(2)}, u32[]{:S(2)}) collective-permute-start(bf16[2,2,128,128]{3,2,1,0:T(8,128)(2,1)S(1)} %maximum_bitcast_fusion.1.refs_0_), channel_id=1, source_target_pairs={{0,3},{1,0},{2,1},{3,2},{4,7},{5,4},{6,5},{7,6},{8,11},{9,8},{10,9... | collective-permute-start | bytes 393224 | tf_op jit(solution)/shard_map/Move_zl3/ppermute | solution.py:24
  31.2 137.9 %reduce-scatter.2.cloned.1.call-start = ((), (), s32[]{:S(2)}) async-start(), calls=%async_computation.2 | async-start | bytes 2621440 | tf_op jit(solution)/shard_map/reduce_scatter | solution.py:250
  31.3 13.9 %collective-permute-start.5 = (bf16[2,2,3,128,128]{4,3,2,1,0:T(8,128)(2,1)S(1)}, bf16[2,2,3,128,128]{4,3,2,1,0:T(8,128)(2,1)S(1)}, u32[]{:S(2)}, u32[]{:S(2)}) collective-permute-start(bf16[2,2,3,128,128]{4,3,2,1,0:T(8,128)(2,1)S(1)} %get-tuple-element.175), channel_id=1, source_target_pairs={{0,128},{128,0},{1,129},{129,1},{2,130},{130,2},{3,131},{131,3},{4... | collective-permute-start | bytes 1179656 | tf_op jit(solution)/shard_map/Move_zh1/ppermute | solution.py:24
  38.2 10.6 %collective-permute-start.8 = (bf16[1,4,3,128,128]{4,3,2,1,0:T(8,128)(2,1)S(1)}, bf16[1,4,3,128,128]{4,3,2,1,0:T(8,128)(2,1)S(1)}, u32[]{:S(2)}, u32[]{:S(2)}) collective-permute-start(bf16[1,4,3,128,128]{4,3,2,1,0:T(8,128)(2,1)S(1)} %get-tuple-element.84), channel_id=1, source_target_pairs={{0,32},{32,64},{64,96},{96,0},{1,33},{33,65},{65,97},{97,1},{2,34}... | collective-permute-start | bytes 1179656 | tf_op jit(solution)/shard_map/Move_x1/ppermute | solution.py:24
  38.2 10.6 %collective-permute-start.9 = (bf16[1,4,3,128,128]{4,3,2,1,0:T(8,128)(2,1)S(1)}, bf16[1,4,3,128,128]{4,3,2,1,0:T(8,128)(2,1)S(1)}, u32[]{:S(2)}, u32[]{:S(2)}) collective-permute-start(bf16[1,4,3,128,128]{4,3,2,1,0:T(8,128)(2,1)S(1)} %get-tuple-element.85), channel_id=1, source_target_pairs={{0,96},{32,0},{64,32},{96,64},{1,97},{33,1},{65,33},{97,65},{2,98}... | collective-permute-start | bytes 1179656 | tf_op jit(solution)/shard_map/Move_x3/ppermute | solution.py:24
  40.8 14.6 %collective-permute-start.4 = (bf16[2,2,3,128,128]{4,3,2,1,0:T(8,128)(2,1)S(1)}, bf16[2,2,3,128,128]{4,3,2,1,0:T(8,128)(2,1)S(1)}, u32[]{:S(2)}, u32[]{:S(2)}) collective-permute-start(bf16[2,2,3,128,128]{4,3,2,1,0:T(8,128)(2,1)S(1)} %get-tuple-element.176), channel_id=1, source_target_pairs={{0,128},{128,0},{1,129},{129,1},{2,130},{130,2},{3,131},{131,3},{4... | collective-permute-start | bytes 1179656 | tf_op jit(solution)/shard_map/Move_zh1/ppermute | solution.py:24
  48.8 9.9 %collective-permute-start.10 = (bf16[2,2,3,128,128]{4,3,2,1,0:T(8,128)(2,1)S(1)}, bf16[2,2,3,128,128]{4,3,2,1,0:T(8,128)(2,1)S(1)}, u32[]{:S(2)}, u32[]{:S(2)}) collective-permute-start(bf16[2,2,3,128,128]{4,3,2,1,0:T(8,128)(2,1)S(1)} %collective-permute-done.5.refs_10_), channel_id=1, source_target_pairs={{0,32},{32,64},{64,96},{96,0},{1,33},{33,65},{65,97},{97,1},{2,34}... | collective-permute-start | bytes 1179656 | tf_op jit(solution)/shard_map/Move_x1/ppermute | solution.py:24
  48.9 9.8 %collective-permute-start.11 = (bf16[2,2,3,128,128]{4,3,2,1,0:T(8,128)(2,1)S(1)}, bf16[2,2,3,128,128]{4,3,2,1,0:T(8,128)(2,1)S(1)}, u32[]{:S(2)}, u32[]{:S(2)}) collective-permute-start(bf16[2,2,3,128,128]{4,3,2,1,0:T(8,128)(2,1)S(1)} %collective-permute-done.5.refs_10_), channel_id=1, source_target_pairs={{0,96},{32,0},{64,32},{96,64},{1,97},{33,1},{65,33},{97,65},{2,98}... | collective-permute-start | bytes 1179656 | tf_op jit(solution)/shard_map/Move_x3/ppermute | solution.py:24
  51.5 16.1 %collective-permute-start.12 = (bf16[2,2,3,128,128]{4,3,2,1,0:T(8,128)(2,1)S(1)}, bf16[2,2,3,128,128]{4,3,2,1,0:T(8,128)(2,1)}, u32[]{:S(2)}, u32[]{:S(2)}) collective-permute-start(bf16[2,2,3,128,128]{4,3,2,1,0:T(8,128)(2,1)S(1)} %collective-permute-done.5.refs_10_), channel_id=1, source_target_pairs={{0,64},{32,96},{64,0},{96,32},{1,65},{33,97},{65,1},{97,33},{2,66}... | collective-permute-start | bytes 1179656 | tf_op jit(solution)/shard_map/Move_x2/ppermute | solution.py:24
  67.7 8.8 %collective-permute-start.13 = (bf16[32,2,128,128]{3,2,1,0:T(8,128)(2,1)}, bf16[32,2,128,128]{3,2,1,0:T(8,128)(2,1)S(1)}, u32[]{:S(2)}, u32[]{:S(2)}) collective-permute-start(bf16[32,2,128,128]{3,2,1,0:T(8,128)(2,1)} %all-gather.2.cloned.1.call-done.refs_3_), channel_id=1, source_target_pairs={{0,16},{16,0},{1,17},{17,1},{2,18},{18,2},{3,19},{19,3},{4,20},{20... | collective-permute-start | bytes 6291464 | tf_op jit(solution)/shard_map/Move_c1/ppermute | solution.py:24
  72.7 18.2 %collective-permute-start.14 = (bf16[2,2,3,128,128]{4,3,2,1,0:T(8,128)(2,1)S(1)}, bf16[2,2,3,128,128]{4,3,2,1,0:T(8,128)(2,1)}, u32[]{:S(2)}, u32[]{:S(2)}) collective-permute-start(bf16[2,2,3,128,128]{4,3,2,1,0:T(8,128)(2,1)S(1)} %collective-permute-done.4.refs_17_), channel_id=1, source_target_pairs={{0,32},{32,64},{64,96},{96,0},{1,33},{33,65},{65,97},{97,1},{2,34}... | collective-permute-start | bytes 1179656 | tf_op jit(solution)/shard_map/Move_x1/ppermute | solution.py:24
  73.6 19.3 %collective-permute-start.15 = (bf16[2,2,3,128,128]{4,3,2,1,0:T(8,128)(2,1)S(1)}, bf16[2,2,3,128,128]{4,3,2,1,0:T(8,128)(2,1)}, u32[]{:S(2)}, u32[]{:S(2)}) collective-permute-start(bf16[2,2,3,128,128]{4,3,2,1,0:T(8,128)(2,1)S(1)} %collective-permute-done.4.refs_17_), channel_id=1, source_target_pairs={{0,96},{32,0},{64,32},{96,64},{1,97},{33,1},{65,33},{97,65},{2,98}... | collective-permute-start | bytes 1179656 | tf_op jit(solution)/shard_map/Move_x3/ppermute | solution.py:24
  75.4 18.8 %collective-permute-start.16 = (bf16[2,2,3,128,128]{4,3,2,1,0:T(8,128)(2,1)S(1)}, bf16[2,2,3,128,128]{4,3,2,1,0:T(8,128)(2,1)}, u32[]{:S(2)}, u32[]{:S(2)}) collective-permute-start(bf16[2,2,3,128,128]{4,3,2,1,0:T(8,128)(2,1)S(1)} %collective-permute-done.4.refs_17_), channel_id=1, source_target_pairs={{0,64},{32,96},{64,0},{96,32},{1,65},{33,97},{65,1},{97,33},{2,66}... | collective-permute-start | bytes 1179656 | tf_op jit(solution)/shard_map/Move_x2/ppermute | solution.py:24
  89.3 18.2 %collective-permute-start.17 = (bf16[2,2,3,128,128]{4,3,2,1,0:T(8,128)(2,1)}, bf16[2,2,3,128,128]{4,3,2,1,0:T(8,128)(2,1)S(1)}, u32[]{:S(2)}, u32[]{:S(2)}) collective-permute-start(bf16[2,2,3,128,128]{4,3,2,1,0:T(8,128)(2,1)} %get-tuple-element.118), channel_id=1, source_target_pairs={{0,96},{32,0},{64,32},{96,64},{1,97},{33,1},{65,33},{97,65},{2,98}... | collective-permute-start | bytes 1179656 | tf_op jit(solution)/shard_map/Move_x3/ppermute | solution.py:24
  90.5 17.0 %collective-permute-start.18 = (bf16[2,2,3,128,128]{4,3,2,1,0:T(8,128)(2,1)}, bf16[2,2,3,128,128]{4,3,2,1,0:T(8,128)(2,1)S(1)}, u32[]{:S(2)}, u32[]{:S(2)}) collective-permute-start(bf16[2,2,3,128,128]{4,3,2,1,0:T(8,128)(2,1)} %get-tuple-element.119), channel_id=1, source_target_pairs={{0,32},{32,64},{64,96},{96,0},{1,33},{33,65},{65,97},{97,1},{2,34}... | collective-permute-start | bytes 1179656 | tf_op jit(solution)/shard_map/Move_x1/ppermute | solution.py:24
  90.9 19.1 %collective-permute-start.19 = (bf16[2,2,3,128,128]{4,3,2,1,0:T(8,128)(2,1)}, bf16[2,2,3,128,128]{4,3,2,1,0:T(8,128)(2,1)S(1)}, u32[]{:S(2)}, u32[]{:S(2)}) collective-permute-start(bf16[2,2,3,128,128]{4,3,2,1,0:T(8,128)(2,1)} %get-tuple-element.120), channel_id=1, source_target_pairs={{0,64},{32,96},{64,0},{96,32},{1,65},{33,97},{65,1},{97,33},{2,66}... | collective-permute-start | bytes 1179656 | tf_op jit(solution)/shard_map/Move_x2/ppermute | solution.py:24
  120.1 11.5 %collective-permute-start.20 = (bf16[2,2,3,128,128]{4,3,2,1,0:T(8,128)(2,1)}, bf16[2,2,3,128,128]{4,3,2,1,0:T(8,128)(2,1)S(1)}, u32[]{:S(2)}, u32[]{:S(2)}) collective-permute-start(bf16[2,2,3,128,128]{4,3,2,1,0:T(8,128)(2,1)} %get-tuple-element.125), channel_id=1, source_target_pairs={{0,96},{32,0},{64,32},{96,64},{1,97},{33,1},{65,33},{97,65},{2,98}... | collective-permute-start | bytes 1179656 | tf_op jit(solution)/shard_map/Move_x3/ppermute | solution.py:24
  121.7 12.2 %collective-permute-start.21 = (bf16[2,2,3,128,128]{4,3,2,1,0:T(8,128)(2,1)}, bf16[2,2,3,128,128]{4,3,2,1,0:T(8,128)(2,1)S(1)}, u32[]{:S(2)}, u32[]{:S(2)}) collective-permute-start(bf16[2,2,3,128,128]{4,3,2,1,0:T(8,128)(2,1)} %get-tuple-element.126), channel_id=1, source_target_pairs={{0,32},{32,64},{64,96},{96,0},{1,33},{33,65},{65,97},{97,1},{2,34}... | collective-permute-start | bytes 1179656 | tf_op jit(solution)/shard_map/Move_x1/ppermute | solution.py:24
  121.7 19.0 %collective-permute-start.22 = (bf16[2,2,3,128,128]{4,3,2,1,0:T(8,128)(2,1)}, bf16[2,2,3,128,128]{4,3,2,1,0:T(8,128)(2,1)S(1)}, u32[]{:S(2)}, u32[]{:S(2)}) collective-permute-start(bf16[2,2,3,128,128]{4,3,2,1,0:T(8,128)(2,1)} %get-tuple-element.127), channel_id=1, source_target_pairs={{0,64},{32,96},{64,0},{96,32},{1,65},{33,97},{65,1},{97,33},{2,66}... | collective-permute-start | bytes 1179656 | tf_op jit(solution)/shard_map/Move_x2/ppermute | solution.py:24
  123.2 17.5 %collective-permute-start.24 = (bf16[2,2,3,128,128]{4,3,2,1,0:T(8,128)(2,1)S(1)}, bf16[2,2,3,128,128]{4,3,2,1,0:T(8,128)(2,1)S(1)}, u32[]{:S(2)}, u32[]{:S(2)}) collective-permute-start(bf16[2,2,3,128,128]{4,3,2,1,0:T(8,128)(2,1)S(1)} %add_convert_fusion.2), channel_id=1, source_target_pairs={{0,128},{128,0},{1,129},{129,1},{2,130},{130,2},{3,131},{131,3},{4... | collective-permute-start | bytes 1179656 | tf_op jit(solution)/shard_map/Move_zh1/ppermute | solution.py:24
  140.8 8.2 %collective-permute-start.25 = (bf16[1,4,3,128,128]{4,3,2,1,0:T(8,128)(2,1)S(1)}, bf16[1,4,3,128,128]{4,3,2,1,0:T(8,128)(2,1)S(1)}, u32[]{:S(2)}, u32[]{:S(2)}) collective-permute-start(bf16[1,4,3,128,128]{4,3,2,1,0:T(8,128)(2,1)S(1)} %get-tuple-element.135), channel_id=1, source_target_pairs={{0,96},{32,0},{64,32},{96,64},{1,97},{33,1},{65,33},{97,65},{2,98}... | collective-permute-start | bytes 1179656 | tf_op jit(solution)/shard_map/Move_x3/ppermute | solution.py:24
  141.6 10.0 %collective-permute-start.26 = (bf16[1,4,3,128,128]{4,3,2,1,0:T(8,128)(2,1)S(1)}, bf16[1,4,3,128,128]{4,3,2,1,0:T(8,128)(2,1)S(1)}, u32[]{:S(2)}, u32[]{:S(2)}) collective-permute-start(bf16[1,4,3,128,128]{4,3,2,1,0:T(8,128)(2,1)S(1)} %get-tuple-element.136), channel_id=1, source_target_pairs={{0,32},{32,64},{64,96},{96,0},{1,33},{33,65},{65,97},{97,1},{2,34}... | collective-permute-start | bytes 1179656 | tf_op jit(solution)/shard_map/Move_x1/ppermute | solution.py:24
  151.8 26.6 %collective-permute-start.27 = (bf16[2,4,3,128,128]{4,3,2,1,0:T(8,128)(2,1)S(1)}, bf16[2,4,3,128,128]{4,3,2,1,0:T(8,128)(2,1)S(1)}, u32[]{:S(2)}, u32[]{:S(2)}) collective-permute-start(bf16[2,4,3,128,128]{4,3,2,1,0:T(8,128)(2,1)S(1)} %get-tuple-element.141), channel_id=1, source_target_pairs={{0,96},{32,0},{64,32},{96,64},{1,97},{33,1},{65,33},{97,65},{2,98}... | collective-permute-start | bytes 2359304 | tf_op jit(solution)/shard_map/Move_x3/ppermute | solution.py:24
  152.2 33.3 %collective-permute-start.28 = (bf16[2,4,3,128,128]{4,3,2,1,0:T(8,128)(2,1)S(1)}, bf16[2,4,3,128,128]{4,3,2,1,0:T(8,128)(2,1)}, u32[]{:S(2)}, u32[]{:S(2)}) collective-permute-start(bf16[2,4,3,128,128]{4,3,2,1,0:T(8,128)(2,1)S(1)} %get-tuple-element.142), channel_id=1, source_target_pairs={{0,32},{32,64},{64,96},{96,0},{1,33},{33,65},{65,97},{97,1},{2,34}... | collective-permute-start | bytes 2359304 | tf_op jit(solution)/shard_map/Move_x1/ppermute | solution.py:24
  153.4 33.7 %collective-permute-start.32 = (bf16[2,2,3,128,128]{4,3,2,1,0:T(8,128)(2,1)S(1)}, bf16[2,2,3,128,128]{4,3,2,1,0:T(8,128)(2,1)}, u32[]{:S(2)}, u32[]{:S(2)}) collective-permute-start(bf16[2,2,3,128,128]{4,3,2,1,0:T(8,128)(2,1)S(1)} %add_convert_fusion.1.refs_4_), channel_id=1, source_target_pairs={{0,128},{128,0},{1,129},{129,1},{2,130},{130,2},{3,131},{131,3},{4... | collective-permute-start | bytes 1179656 | tf_op jit(solution)/shard_map/Move_zh1/ppermute | solution.py:24
  170.3 16.8 %collective-permute-start.29 = (bf16[2,2,128,128]{3,2,1,0:T(8,128)(2,1)S(1)}, bf16[2,2,128,128]{3,2,1,0:T(8,128)(2,1)S(1)}, u32[]{:S(2)}, u32[]{:S(2)}) collective-permute-start(bf16[2,2,128,128]{3,2,1,0:T(8,128)(2,1)S(1)} %get-tuple-element.179), channel_id=1, source_target_pairs={{0,3},{1,0},{2,1},{3,2},{4,7},{5,4},{6,5},{7,6},{8,11},{9,8},{10,9... | collective-permute-start | bytes 393224 | tf_op jit(solution)/shard_map/Move_zl3/ppermute | solution.py:24
  173.6 22.0 %collective-permute-start.30 = (bf16[2,2,128,128]{3,2,1,0:T(8,128)(2,1)S(1)}, bf16[2,2,128,128]{3,2,1,0:T(8,128)(2,1)S(1)}, u32[]{:S(2)}, u32[]{:S(2)}) collective-permute-start(bf16[2,2,128,128]{3,2,1,0:T(8,128)(2,1)S(1)} %get-tuple-element.178), channel_id=1, source_target_pairs={{0,2},{1,3},{2,0},{3,1},{4,6},{5,7},{6,4},{7,5},{8,10},{9,11},{10,... | collective-permute-start | bytes 393224 | tf_op jit(solution)/shard_map/Move_zl2/ppermute | solution.py:24
  178.4 17.2 %collective-permute-start.31 = (bf16[2,2,128,128]{3,2,1,0:T(8,128)(2,1)S(1)}, bf16[2,2,128,128]{3,2,1,0:T(8,128)(2,1)S(1)}, u32[]{:S(2)}, u32[]{:S(2)}) collective-permute-start(bf16[2,2,128,128]{3,2,1,0:T(8,128)(2,1)S(1)} %get-tuple-element.177), channel_id=1, source_target_pairs={{0,1},{1,2},{2,3},{3,0},{4,5},{5,6},{6,7},{7,4},{8,9},{9,10},{10,1... | collective-permute-start | bytes 393224 | tf_op jit(solution)/shard_map/Move_zl1/ppermute | solution.py:24
  (30 other events, 403.6 us)
Sparse Core Ops, SparseCore 0:
  31.3 35.7 all-gather.1
  120.2 48.8 reduce-scatter.1

commit v4 on v3

--- a/solution.py
+++ b/solution.py
@@ -186,7 +186,7 @@
     new_right[1] = (right[1].astype(F32) + from_left[0].astype(F32)).astype(BF16)
 
 
-def small(kernel, values, shapes, earlier=()):
+def small(kernel, values, shapes, earlier=(), flops=SHORT):
     whole = [pl.BlockSpec(memory_space=pltpu.VMEM)] * len(shapes)
     count = len(values)
 
@@ -199,7 +199,7 @@
         out_specs=whole,
         out_shape=[jax.ShapeDtypeStruct(v, BF16) for v in shapes],
         compiler_params=pltpu.CompilerParams(vmem_limit_bytes=32 * 1024 * 1024),
-        cost_estimate=pl.CostEstimate(flops=SHORT, bytes_accessed=2 * 1024 * 1024, transcendentals=0),
+        cost_estimate=pl.CostEstimate(flops=flops, bytes_accessed=2 * 1024 * 1024, transcendentals=0),
         name=kernel.__name__,
     )(*values, *earlier)
 
@@ -248,7 +248,7 @@
     first_sum = rot(first_sum, "zh", 1)
     second_sum = [far_parts[0], *[rot(far_parts[p], "x", k) for p, k in ((1, 3), (2, 1), (3, 2))]]
     line = lax.psum_scatter(both, "y", scatter_dimension=0, tiled=True)
-    sent = small(copy_kernel, near_parts[3:], [v.shape for v in near_parts[3:]], [both])
+    sent = small(copy_kernel, near_parts[3:], [v.shape for v in near_parts[3:]], [both], LONG)
     second_sum, sent, first_sum = tie((second_sum, sent, first_sum))
     second_sum = add(*second_sum).astype(BF16)
     crossed = rot(sent[0], "x", -1), rot(sent[1], "x", 1)

time: 210 us -> 207 us (0.986)
  starting transfers between devices: 77.4 us -> 70.9 us
    ppermute x34, waiting for transfers between devices: 60.8 us -> 53.7 us  [rot(): return lax.ppermute(value, axis, [(i, (i + step) % n) for i in range(n)])]
    reduce_scatter x1, waiting for transfers between devices: 8.12 us -> 14.9 us  [shards(): line = lax.psum_scatter(both, 'y', scatter_dimension=0, tiled=True)]
    ppermute x34, starting transfers between devices: 77.3 us -> 70.8 us  [rot(): return lax.ppermute(value, axis, [(i, (i + step) % n) for i in range(n)])]
    unnamed x56 -> x54, local copies, waits for them, and re-layouts: 5.75 us -> 7.27 us
  transfers between devices with their start and end apart: 36 -> 36, of which waited for: 16 -> 14; matrix products, arithmetic and copies ran while one was open for 5% -> 7% of each run, Pallas kernels for 12% -> 12%
where the time goes in v4:
time: 207 us; the launch traced here: 206 us
  starting transfers between devices  70.9 us (34%)
  waiting for transfers between devices  68.7 us (33%)
  Pallas kernels  24.5 us (12%)
  between operations  14.6 us (7%)
  local copies, waits for them, and re-layouts  14.2 us (7%)
  other arithmetic  13.4 us (6%)
    ppermute x34, starting transfers between devices, rot(): return lax.ppermute(value, axis, [(i, (i + step) % n) for i in range(n)])  70.8 us
    ppermute x34, waiting for transfers between devices, rot(): return lax.ppermute(value, axis, [(i, (i + step) % n) for i in range(n)])  53.7 us
    pallas_call x2, Pallas kernels, layer(): pl.pallas_call(functools.partial(layer_kernel, first, slots), grid=(slots...  24.2 us
    reduce_scatter x1, waiting for transfers between devices, shards(): line = lax.psum_scatter(both, 'y', scatter_dimension=0, tiled=True)  14.9 us
    unnamed x54, local copies, waits for them, and re-layouts  7.27 us
  transfers between devices with their start and end apart: 36, of which 14 were waited for; matrix products, arithmetic and copies ran while one was open for 7% of the time, Pallas kernels for 12%

profile of v4, /device:TPU:1, one launch (start us, length us, event | category | flops | bytes accessed | tf_op | source)
XLA Modules:
  0.0 206.3 jit_solution(4247736843954507464)
XLA Ops:
  9.5 3.3 %collective-permute-start = (bf16[4,3,128,128]{3,2,1,0:T(8,128)(2,1)S(1)}, bf16[4,3,128,128]{3,2,1,0:T(8,128)(2,1)S(1)}, u32[]{:S(2)}, u32[]{:S(2)}) collective-permute-start(bf16[4,3,128,128]{3,2,1,0:T(8,128)(2,1)S(1)} %pad_maximum_fusion.5), channel_id=1, source_target_pairs={{0,16},{16,0},{1,17},{17,1},{2,18},{18,2},{3,19},{19,3},{4,20},{20... | collective-permute-start | bytes 1179656 | tf_op jit(solution)/shard_map/Move_c1/ppermute | solution.py:24
  15.5 2.7 %collective-permute-start.7 = (bf16[2,4,3,128,128]{4,3,2,1,0:T(8,128)(2,1)S(1)}, bf16[2,4,3,128,128]{4,3,2,1,0:T(8,128)(2,1)S(1)}, u32[]{:S(2)}, u32[]{:S(2)}) collective-permute-start(bf16[2,4,3,128,128]{4,3,2,1,0:T(8,128)(2,1)S(1)} %pad_maximum_fusion.refs_5_.refs_12_), channel_id=1, source_target_pairs={{0,96},{32,0},{64,32},{96,64},{1,97},{33,1},{65,33},{97,65},{2,98}... | collective-permute-start | bytes 2359304 | tf_op jit(solution)/shard_map/Move_x3/ppermute | solution.py:24
  18.2 2.9 %collective-permute-start.2 = (bf16[2,2,128,128]{3,2,1,0:T(8,128)(2,1)S(1)}, bf16[2,2,128,128]{3,2,1,0:T(8,128)(2,1)S(1)}, u32[]{:S(2)}, u32[]{:S(2)}) collective-permute-start(bf16[2,2,128,128]{3,2,1,0:T(8,128)(2,1)S(1)} %maximum_bitcast_fusion.1.refs_0_), channel_id=1, source_target_pairs={{0,2},{1,3},{2,0},{3,1},{4,6},{5,7},{6,4},{7,5},{8,10},{9,11},{10,... | collective-permute-start | bytes 393224 | tf_op jit(solution)/shard_map/Move_zl2/ppermute | solution.py:24
  21.8 2.7 %collective-permute-done.1 = bf16[2,2,128,128]{3,2,1,0:T(8,128)(2,1)S(1)} collective-permute-done((bf16[2,2,128,128]{3,2,1,0:T(8,128)(2,1)S(1)}, bf16[2,2,128,128]{3,2,1,0:T(8,128)(2,1)S(1)}, u32[]{:S(2)}, u32[]{:S(2)}) %collective-permute-start.1) | collective-permute-done | bytes 131104 | tf_op jit(solution)/shard_map/Move_zl1/ppermute | solution.py:24
  24.6 5.7 %collective-permute-done.2 = bf16[2,2,128,128]{3,2,1,0:T(8,128)(2,1)S(1)} collective-permute-done((bf16[2,2,128,128]{3,2,1,0:T(8,128)(2,1)S(1)}, bf16[2,2,128,128]{3,2,1,0:T(8,128)(2,1)S(1)}, u32[]{:S(2)}, u32[]{:S(2)}) %collective-permute-start.2) | collective-permute-done | bytes 131104 | tf_op jit(solution)/shard_map/Move_zl2/ppermute | solution.py:24
  31.3 5.7 %collective-permute-start.5 = (bf16[2,2,3,128,128]{4,3,2,1,0:T(8,128)(2,1)S(1)}, bf16[2,2,3,128,128]{4,3,2,1,0:T(8,128)(2,1)S(1)}, u32[]{:S(2)}, u32[]{:S(2)}) collective-permute-start(bf16[2,2,3,128,128]{4,3,2,1,0:T(8,128)(2,1)S(1)} %get-tuple-element.175), channel_id=1, source_target_pairs={{0,128},{128,0},{1,129},{129,1},{2,130},{130,2},{3,131},{131,3},{4... | collective-permute-start | bytes 1179656 | tf_op jit(solution)/shard_map/Move_zh1/ppermute | solution.py:24
  38.2 2.7 %collective-permute-start.9 = (bf16[1,4,3,128,128]{4,3,2,1,0:T(8,128)(2,1)S(1)}, bf16[1,4,3,128,128]{4,3,2,1,0:T(8,128)(2,1)S(1)}, u32[]{:S(2)}, u32[]{:S(2)}) collective-permute-start(bf16[1,4,3,128,128]{4,3,2,1,0:T(8,128)(2,1)S(1)} %get-tuple-element.85), channel_id=1, source_target_pairs={{0,96},{32,0},{64,32},{96,64},{1,97},{33,1},{65,33},{97,65},{2,98}... | collective-permute-start | bytes 1179656 | tf_op jit(solution)/shard_map/Move_x3/ppermute | solution.py:24
  40.8 4.0 %collective-permute-start.4 = (bf16[2,2,3,128,128]{4,3,2,1,0:T(8,128)(2,1)S(1)}, bf16[2,2,3,128,128]{4,3,2,1,0:T(8,128)(2,1)}, u32[]{:S(2)}, u32[]{:S(2)}) collective-permute-start(bf16[2,2,3,128,128]{4,3,2,1,0:T(8,128)(2,1)S(1)} %get-tuple-element.176), channel_id=1, source_target_pairs={{0,128},{128,0},{1,129},{129,1},{2,130},{130,2},{3,131},{131,3},{4... | collective-permute-start | bytes 1179656 | tf_op jit(solution)/shard_map/Move_zh1/ppermute | solution.py:24
  45.2 3.6 %collective-permute-done.8.refs_8_.refs_15_ = bf16[1,4,3,128,128]{4,3,2,1,0:T(8,128)(2,1)S(1)} collective-permute-done((bf16[1,4,3,128,128]{4,3,2,1,0:T(8,128)(2,1)S(1)}, bf16[1,4,3,128,128]{4,3,2,1,0:T(8,128)(2,1)S(1)}, u32[]{:S(2)}, u32[]{:S(2)}) %collective-permute-start.8) | collective-permute-done | bytes 393248 | tf_op jit(solution)/shard_map/Move_x1/ppermute | solution.py:24
  48.9 2.7 %collective-permute-start.11 = (bf16[2,2,3,128,128]{4,3,2,1,0:T(8,128)(2,1)S(1)}, bf16[2,2,3,128,128]{4,3,2,1,0:T(8,128)(2,1)S(1)}, u32[]{:S(2)}, u32[]{:S(2)}) collective-permute-start(bf16[2,2,3,128,128]{4,3,2,1,0:T(8,128)(2,1)S(1)} %collective-permute-done.5.refs_10_), channel_id=1, source_target_pairs={{0,96},{32,0},{64,32},{96,64},{1,97},{33,1},{65,33},{97,65},{2,98}... | collective-permute-start | bytes 1179656 | tf_op jit(solution)/shard_map/Move_x3/ppermute | solution.py:24
  52.5 3.0 %collective-permute-done.4.refs_17_ = bf16[2,2,3,128,128]{4,3,2,1,0:T(8,128)(2,1)} collective-permute-done((bf16[2,2,3,128,128]{4,3,2,1,0:T(8,128)(2,1)S(1)}, bf16[2,2,3,128,128]{4,3,2,1,0:T(8,128)(2,1)}, u32[]{:S(2)}, u32[]{:S(2)}) %collective-permute-start.4) | collective-permute-done | bytes 393248 | tf_op jit(solution)/shard_map/Move_zh1/ppermute | solution.py:24
  55.4 3.2 %collective-permute-done.10.refs_11_ = bf16[2,2,3,128,128]{4,3,2,1,0:T(8,128)(2,1)S(1)} collective-permute-done((bf16[2,2,3,128,128]{4,3,2,1,0:T(8,128)(2,1)S(1)}, bf16[2,2,3,128,128]{4,3,2,1,0:T(8,128)(2,1)S(1)}, u32[]{:S(2)}, u32[]{:S(2)}) %collective-permute-start.10) | collective-permute-done | bytes 393248 | tf_op jit(solution)/shard_map/Move_x1/ppermute | solution.py:24
  59.4 8.3 %collective-permute-done.12.refs_13_ = bf16[2,2,3,128,128]{4,3,2,1,0:T(8,128)(2,1)S(1)} collective-permute-done((bf16[2,2,3,128,128]{4,3,2,1,0:T(8,128)(2,1)S(1)}, bf16[2,2,3,128,128]{4,3,2,1,0:T(8,128)(2,1)S(1)}, u32[]{:S(2)}, u32[]{:S(2)}) %collective-permute-start.12) | collective-permute-done | bytes 393248 | tf_op jit(solution)/shard_map/Move_x2/ppermute | solution.py:24
  68.5 3.2 %collective-permute-start.13 = (bf16[32,2,128,128]{3,2,1,0:T(8,128)(2,1)}, bf16[32,2,128,128]{3,2,1,0:T(8,128)(2,1)S(1)}, u32[]{:S(2)}, u32[]{:S(2)}) collective-permute-start(bf16[32,2,128,128]{3,2,1,0:T(8,128)(2,1)} %all-gather.2.cloned.1.call-done.refs_3_), channel_id=1, source_target_pairs={{0,16},{16,0},{1,17},{17,1},{2,18},{18,2},{3,19},{19,3},{4,20},{20... | collective-permute-start | bytes 6291464 | tf_op jit(solution)/shard_map/Move_c1/ppermute | solution.py:24
  74.4 1.8 collective-permute-start.15
  78.6 11.3 %layer.2 = (bf16[32,2,128,128]{3,2,1,0:T(8,128)(2,1)}, bf16[32,2,128,128]{3,2,1,0:T(8,128)(2,1)}, bf16[2,4,3,128,128]{4,3,2,1,0:T(8,128)(2,1)}, bf16[2,4,3,128,1...) custom-call(s32[2,16]{1,0:T(2,128)} %get-tuple-element.191.refs_0_, ...), custom_call_target="tpu_custom_call" | custom-call | flops 99999997952 | bytes 16777216 | tf_op jit(solution)/shard_map/layer/pallas_call | solution.py:118
  91.4 1.9 collective-permute-start.19
  93.3 1.9 collective-permute-done.16.refs_20_
  95.2 13.0 %layer.3 = (bf16[32,2,128,128]{3,2,1,0:T(8,128)(2,1)}, bf16[32,2,128,128]{3,2,1,0:T(8,128)(2,1)}, bf16[2,4,3,128,128]{4,3,2,1,0:T(8,128)(2,1)}, bf16[2,4,3,128,1...) custom-call(s32[2,16]{1,0:T(2,128)} %get-tuple-element.192.refs_0_, ...), custom_call_target="tpu_custom_call", output_to_operand_aliasing={{2}: (7, {}), {3}: (8, {}), {4}: (9, {}), {5}: (10, {}), {6... | custom-call | flops 99999997952 | bytes 16777216 | tf_op jit(solution)/shard_map/layer/pallas_call | solution.py:118
  108.2 3.2 %collective-permute-done.19 = bf16[2,2,3,128,128]{4,3,2,1,0:T(8,128)(2,1)S(1)} collective-permute-done((bf16[2,2,3,128,128]{4,3,2,1,0:T(8,128)(2,1)}, bf16[2,2,3,128,128]{4,3,2,1,0:T(8,128)(2,1)S(1)}, u32[]{:S(2)}, u32[]{:S(2)}) %collective-permute-start.19) | collective-permute-done | bytes 393248 | tf_op jit(solution)/shard_map/Move_x2/ppermute | solution.py:24
  113.7 1.7 collective-permute-start.20
  116.6 8.4 %collective-permute-start.24 = (bf16[2,2,3,128,128]{4,3,2,1,0:T(8,128)(2,1)}, bf16[2,2,3,128,128]{4,3,2,1,0:T(8,128)(2,1)}, u32[]{:S(2)}, u32[]{:S(2)}) collective-permute-start(bf16[2,2,3,128,128]{4,3,2,1,0:T(8,128)(2,1)} %add_convert_fusion.2), channel_id=1, source_target_pairs={{0,128},{128,0},{1,129},{129,1},{2,130},{130,2},{3,131},{131,3},{4... | collective-permute-start | bytes 1179656 | tf_op jit(solution)/shard_map/Move_zh1/ppermute | solution.py:24
  125.0 3.8 %add_convert_fusion.refs_2_ = bf16[32,2,128,128]{3,2,1,0:T(8,128)(2,1)} fusion(bf16[32,2,128,128]{3,2,1,0:T(8,128)(2,1)S(1)} %collective-permute-done.23, bf16[32,2,128,128]{3,2,1,0:T(8,128)(2,1)} %get-tuple-element.130), kind=kLoop, calls=%fused_computation.2 | loop fusion | flops 4194304 | bytes 6291456 | tf_op jit(solution)/shard_map/convert_element_type | solution.py:247
  128.9 1.5 copy-done.1
  130.5 5.3 %collective-permute-done.21 = bf16[2,2,3,128,128]{4,3,2,1,0:T(8,128)(2,1)} collective-permute-done((bf16[2,2,3,128,128]{4,3,2,1,0:T(8,128)(2,1)}, bf16[2,2,3,128,128]{4,3,2,1,0:T(8,128)(2,1)}, u32[]{:S(2)}, u32[]{:S(2)}) %collective-permute-start.21) | collective-permute-done | bytes 393248 | tf_op jit(solution)/shard_map/Move_x1/ppermute | solution.py:24
  138.6 6.7 %collective-permute-done.25.refs_2_ = bf16[1,4,3,128,128]{4,3,2,1,0:T(8,128)(2,1)S(1)} collective-permute-done((bf16[1,4,3,128,128]{4,3,2,1,0:T(8,128)(2,1)S(1)}, bf16[1,4,3,128,128]{4,3,2,1,0:T(8,128)(2,1)S(1)}, u32[]{:S(2)}, u32[]{:S(2)}) %collective-permute-start.25) | collective-permute-done | bytes 393248 | tf_op jit(solution)/shard_map/Move_x3/ppermute | solution.py:24
  148.2 8.8 %collective-permute-start.32 = (bf16[2,2,3,128,128]{4,3,2,1,0:T(8,128)(2,1)S(1)}, bf16[2,2,3,128,128]{4,3,2,1,0:T(8,128)(2,1)}, u32[]{:S(2)}, u32[]{:S(2)}) collective-permute-start(bf16[2,2,3,128,128]{4,3,2,1,0:T(8,128)(2,1)S(1)} %add_convert_fusion.1.refs_4_), channel_id=1, source_target_pairs={{0,128},{128,0},{1,129},{129,1},{2,130},{130,2},{3,131},{131,3},{4... | collective-permute-start | bytes 1179656 | tf_op jit(solution)/shard_map/Move_zh1/ppermute | solution.py:24
  157.0 14.9 %reduce-scatter.2.cloned.1.call-done = bf16[8,2,128,128]{3,2,1,0:T(8,128)(2,1)} async-done(((bf16[32,2,128,128]{3,2,1,0:T(8,128)(2,1)}), bf16[8,2,128,128]{3,2,1,0:T(8,128)(2,1)}) %reduce-scatter.2.cloned.1.call-update) | async-done | bytes 524304 | tf_op jit(solution)/shard_map/reduce_scatter | solution.py:250
  173.1 3.3 %collective-permute-start.29 = (bf16[2,2,128,128]{3,2,1,0:T(8,128)(2,1)S(1)}, bf16[2,2,128,128]{3,2,1,0:T(8,128)(2,1)S(1)}, u32[]{:S(2)}, u32[]{:S(2)}) collective-permute-start(bf16[2,2,128,128]{3,2,1,0:T(8,128)(2,1)S(1)} %get-tuple-element.179), channel_id=1, source_target_pairs={{0,3},{1,0},{2,1},{3,2},{4,7},{5,4},{6,5},{7,6},{8,11},{9,8},{10,9... | collective-permute-start | bytes 393224 | tf_op jit(solution)/shard_map/Move_zl3/ppermute | solution.py:24
  176.4 6.3 %collective-permute-start.31 = (bf16[2,2,128,128]{3,2,1,0:T(8,128)(2,1)S(1)}, bf16[2,2,128,128]{3,2,1,0:T(8,128)(2,1)S(1)}, u32[]{:S(2)}, u32[]{:S(2)}) collective-permute-start(bf16[2,2,128,128]{3,2,1,0:T(8,128)(2,1)S(1)} %get-tuple-element.177), channel_id=1, source_target_pairs={{0,1},{1,2},{2,3},{3,0},{4,5},{5,6},{6,7},{7,4},{8,9},{9,10},{10,1... | collective-permute-start | bytes 393224 | tf_op jit(solution)/shard_map/Move_zl1/ppermute | solution.py:24
  182.7 1.5 convert_add_fusion.1
  184.2 8.5 %collective-permute-done.30 = bf16[2,2,128,128]{3,2,1,0:T(8,128)(2,1)S(1)} collective-permute-done((bf16[2,2,128,128]{3,2,1,0:T(8,128)(2,1)S(1)}, bf16[2,2,128,128]{3,2,1,0:T(8,128)(2,1)S(1)}, u32[]{:S(2)}, u32[]{:S(2)}) %collective-permute-start.30) | collective-permute-done | bytes 131104 | tf_op jit(solution)/shard_map/Move_zl2/ppermute | solution.py:24
  (146 shorter events, 34.0 us)
Async XLA Ops:
  7.2 61.3 %all-gather.2.cloned.1.call-start = ((), (), s32[]{:S(2)}) async-start(), calls=%async_computation.1 | async-start | bytes 2621440 | tf_op jit(solution)/shard_map/all_gather | solution.py:226
  15.5 21.6 %collective-permute-start.6 = (bf16[2,4,3,128,128]{4,3,2,1,0:T(8,128)(2,1)S(1)}, bf16[2,4,3,128,128]{4,3,2,1,0:T(8,128)(2,1)S(1)}, u32[]{:S(2)}, u32[]{:S(2)}) collective-permute-start(bf16[2,4,3,128,128]{4,3,2,1,0:T(8,128)(2,1)S(1)} %pad_maximum_fusion.refs_5_.refs_12_), channel_id=1, source_target_pairs={{0,32},{32,64},{64,96},{96,0},{1,33},{33,65},{65,97},{97,1},{2,34}... | collective-permute-start | bytes 2359304 | tf_op jit(solution)/shard_map/Move_x1/ppermute | solution.py:24
  15.5 21.5 %collective-permute-start.7 = (bf16[2,4,3,128,128]{4,3,2,1,0:T(8,128)(2,1)S(1)}, bf16[2,4,3,128,128]{4,3,2,1,0:T(8,128)(2,1)S(1)}, u32[]{:S(2)}, u32[]{:S(2)}) collective-permute-start(bf16[2,4,3,128,128]{4,3,2,1,0:T(8,128)(2,1)S(1)} %pad_maximum_fusion.refs_5_.refs_12_), channel_id=1, source_target_pairs={{0,96},{32,0},{64,32},{96,64},{1,97},{33,1},{65,33},{97,65},{2,98}... | collective-permute-start | bytes 2359304 | tf_op jit(solution)/shard_map/Move_x3/ppermute | solution.py:24
  18.2 12.1 %collective-permute-start.2 = (bf16[2,2,128,128]{3,2,1,0:T(8,128)(2,1)S(1)}, bf16[2,2,128,128]{3,2,1,0:T(8,128)(2,1)S(1)}, u32[]{:S(2)}, u32[]{:S(2)}) collective-permute-start(bf16[2,2,128,128]{3,2,1,0:T(8,128)(2,1)S(1)} %maximum_bitcast_fusion.1.refs_0_), channel_id=1, source_target_pairs={{0,2},{1,3},{2,0},{3,1},{4,6},{5,7},{6,4},{7,5},{8,10},{9,11},{10,... | collective-permute-start | bytes 393224 | tf_op jit(solution)/shard_map/Move_zl2/ppermute | solution.py:24
  21.1 9.2 %collective-permute-start.3 = (bf16[2,2,128,128]{3,2,1,0:T(8,128)(2,1)S(1)}, bf16[2,2,128,128]{3,2,1,0:T(8,128)(2,1)S(1)}, u32[]{:S(2)}, u32[]{:S(2)}) collective-permute-start(bf16[2,2,128,128]{3,2,1,0:T(8,128)(2,1)S(1)} %maximum_bitcast_fusion.1.refs_0_), channel_id=1, source_target_pairs={{0,3},{1,0},{2,1},{3,2},{4,7},{5,4},{6,5},{7,6},{8,11},{9,8},{10,9... | collective-permute-start | bytes 393224 | tf_op jit(solution)/shard_map/Move_zl3/ppermute | solution.py:24
  31.2 140.8 %reduce-scatter.2.cloned.1.call-start = ((), (), s32[]{:S(2)}) async-start(), calls=%async_computation.2 | async-start | bytes 2621440 | tf_op jit(solution)/shard_map/reduce_scatter | solution.py:250
  31.3 13.9 %collective-permute-start.5 = (bf16[2,2,3,128,128]{4,3,2,1,0:T(8,128)(2,1)S(1)}, bf16[2,2,3,128,128]{4,3,2,1,0:T(8,128)(2,1)S(1)}, u32[]{:S(2)}, u32[]{:S(2)}) collective-permute-start(bf16[2,2,3,128,128]{4,3,2,1,0:T(8,128)(2,1)S(1)} %get-tuple-element.175), channel_id=1, source_target_pairs={{0,128},{128,0},{1,129},{129,1},{2,130},{130,2},{3,131},{131,3},{4... | collective-permute-start | bytes 1179656 | tf_op jit(solution)/shard_map/Move_zh1/ppermute | solution.py:24
  38.2 10.6 %collective-permute-start.8 = (bf16[1,4,3,128,128]{4,3,2,1,0:T(8,128)(2,1)S(1)}, bf16[1,4,3,128,128]{4,3,2,1,0:T(8,128)(2,1)S(1)}, u32[]{:S(2)}, u32[]{:S(2)}) collective-permute-start(bf16[1,4,3,128,128]{4,3,2,1,0:T(8,128)(2,1)S(1)} %get-tuple-element.84), channel_id=1, source_target_pairs={{0,32},{32,64},{64,96},{96,0},{1,33},{33,65},{65,97},{97,1},{2,34}... | collective-permute-start | bytes 1179656 | tf_op jit(solution)/shard_map/Move_x1/ppermute | solution.py:24
  38.2 10.6 %collective-permute-start.9 = (bf16[1,4,3,128,128]{4,3,2,1,0:T(8,128)(2,1)S(1)}, bf16[1,4,3,128,128]{4,3,2,1,0:T(8,128)(2,1)S(1)}, u32[]{:S(2)}, u32[]{:S(2)}) collective-permute-start(bf16[1,4,3,128,128]{4,3,2,1,0:T(8,128)(2,1)S(1)} %get-tuple-element.85), channel_id=1, source_target_pairs={{0,96},{32,0},{64,32},{96,64},{1,97},{33,1},{65,33},{97,65},{2,98}... | collective-permute-start | bytes 1179656 | tf_op jit(solution)/shard_map/Move_x3/ppermute | solution.py:24
  40.8 14.6 %collective-permute-start.4 = (bf16[2,2,3,128,128]{4,3,2,1,0:T(8,128)(2,1)S(1)}, bf16[2,2,3,128,128]{4,3,2,1,0:T(8,128)(2,1)}, u32[]{:S(2)}, u32[]{:S(2)}) collective-permute-start(bf16[2,2,3,128,128]{4,3,2,1,0:T(8,128)(2,1)S(1)} %get-tuple-element.176), channel_id=1, source_target_pairs={{0,128},{128,0},{1,129},{129,1},{2,130},{130,2},{3,131},{131,3},{4... | collective-permute-start | bytes 1179656 | tf_op jit(solution)/shard_map/Move_zh1/ppermute | solution.py:24
  48.8 9.9 %collective-permute-start.10 = (bf16[2,2,3,128,128]{4,3,2,1,0:T(8,128)(2,1)S(1)}, bf16[2,2,3,128,128]{4,3,2,1,0:T(8,128)(2,1)S(1)}, u32[]{:S(2)}, u32[]{:S(2)}) collective-permute-start(bf16[2,2,3,128,128]{4,3,2,1,0:T(8,128)(2,1)S(1)} %collective-permute-done.5.refs_10_), channel_id=1, source_target_pairs={{0,32},{32,64},{64,96},{96,0},{1,33},{33,65},{65,97},{97,1},{2,34}... | collective-permute-start | bytes 1179656 | tf_op jit(solution)/shard_map/Move_x1/ppermute | solution.py:24
  48.9 9.8 %collective-permute-start.11 = (bf16[2,2,3,128,128]{4,3,2,1,0:T(8,128)(2,1)S(1)}, bf16[2,2,3,128,128]{4,3,2,1,0:T(8,128)(2,1)S(1)}, u32[]{:S(2)}, u32[]{:S(2)}) collective-permute-start(bf16[2,2,3,128,128]{4,3,2,1,0:T(8,128)(2,1)S(1)} %collective-permute-done.5.refs_10_), channel_id=1, source_target_pairs={{0,96},{32,0},{64,32},{96,64},{1,97},{33,1},{65,33},{97,65},{2,98}... | collective-permute-start | bytes 1179656 | tf_op jit(solution)/shard_map/Move_x3/ppermute | solution.py:24
  51.5 16.2 %collective-permute-start.12 = (bf16[2,2,3,128,128]{4,3,2,1,0:T(8,128)(2,1)S(1)}, bf16[2,2,3,128,128]{4,3,2,1,0:T(8,128)(2,1)S(1)}, u32[]{:S(2)}, u32[]{:S(2)}) collective-permute-start(bf16[2,2,3,128,128]{4,3,2,1,0:T(8,128)(2,1)S(1)} %collective-permute-done.5.refs_10_), channel_id=1, source_target_pairs={{0,64},{32,96},{64,0},{96,32},{1,65},{33,97},{65,1},{97,33},{2,66}... | collective-permute-start | bytes 1179656 | tf_op jit(solution)/shard_map/Move_x2/ppermute | solution.py:24
  73.5 17.9 %collective-permute-start.14 = (bf16[2,2,3,128,128]{4,3,2,1,0:T(8,128)(2,1)}, bf16[2,2,3,128,128]{4,3,2,1,0:T(8,128)(2,1)S(1)}, u32[]{:S(2)}, u32[]{:S(2)}) collective-permute-start(bf16[2,2,3,128,128]{4,3,2,1,0:T(8,128)(2,1)} %collective-permute-done.4.refs_17_), channel_id=1, source_target_pairs={{0,32},{32,64},{64,96},{96,0},{1,33},{33,65},{65,97},{97,1},{2,34}... | collective-permute-start | bytes 1179656 | tf_op jit(solution)/shard_map/Move_x1/ppermute | solution.py:24
  74.4 18.9 %collective-permute-start.15 = (bf16[2,2,3,128,128]{4,3,2,1,0:T(8,128)(2,1)}, bf16[2,2,3,128,128]{4,3,2,1,0:T(8,128)(2,1)}, u32[]{:S(2)}, u32[]{:S(2)}) collective-permute-start(bf16[2,2,3,128,128]{4,3,2,1,0:T(8,128)(2,1)} %collective-permute-done.4.refs_17_), channel_id=1, source_target_pairs={{0,96},{32,0},{64,32},{96,64},{1,97},{33,1},{65,33},{97,65},{2,98}... | collective-permute-start | bytes 1179656 | tf_op jit(solution)/shard_map/Move_x3/ppermute | solution.py:24
  76.2 19.0 %collective-permute-start.16 = (bf16[2,2,3,128,128]{4,3,2,1,0:T(8,128)(2,1)}, bf16[2,2,3,128,128]{4,3,2,1,0:T(8,128)(2,1)}, u32[]{:S(2)}, u32[]{:S(2)}) collective-permute-start(bf16[2,2,3,128,128]{4,3,2,1,0:T(8,128)(2,1)} %collective-permute-done.4.refs_17_), channel_id=1, source_target_pairs={{0,64},{32,96},{64,0},{96,32},{1,65},{33,97},{65,1},{97,33},{2,66}... | collective-permute-start | bytes 1179656 | tf_op jit(solution)/shard_map/Move_x2/ppermute | solution.py:24
  89.8 18.4 %collective-permute-start.17 = (bf16[2,2,3,128,128]{4,3,2,1,0:T(8,128)(2,1)}, bf16[2,2,3,128,128]{4,3,2,1,0:T(8,128)(2,1)S(1)}, u32[]{:S(2)}, u32[]{:S(2)}) collective-permute-start(bf16[2,2,3,128,128]{4,3,2,1,0:T(8,128)(2,1)} %get-tuple-element.118), channel_id=1, source_target_pairs={{0,96},{32,0},{64,32},{96,64},{1,97},{33,1},{65,33},{97,65},{2,98}... | collective-permute-start | bytes 1179656 | tf_op jit(solution)/shard_map/Move_x3/ppermute | solution.py:24
  90.9 17.3 %collective-permute-start.18 = (bf16[2,2,3,128,128]{4,3,2,1,0:T(8,128)(2,1)}, bf16[2,2,3,128,128]{4,3,2,1,0:T(8,128)(2,1)S(1)}, u32[]{:S(2)}, u32[]{:S(2)}) collective-permute-start(bf16[2,2,3,128,128]{4,3,2,1,0:T(8,128)(2,1)} %get-tuple-element.119), channel_id=1, source_target_pairs={{0,32},{32,64},{64,96},{96,0},{1,33},{33,65},{65,97},{97,1},{2,34}... | collective-permute-start | bytes 1179656 | tf_op jit(solution)/shard_map/Move_x1/ppermute | solution.py:24
  91.4 20.1 %collective-permute-start.19 = (bf16[2,2,3,128,128]{4,3,2,1,0:T(8,128)(2,1)}, bf16[2,2,3,128,128]{4,3,2,1,0:T(8,128)(2,1)S(1)}, u32[]{:S(2)}, u32[]{:S(2)}) collective-permute-start(bf16[2,2,3,128,128]{4,3,2,1,0:T(8,128)(2,1)} %get-tuple-element.120), channel_id=1, source_target_pairs={{0,64},{32,96},{64,0},{96,32},{1,65},{33,97},{65,1},{97,33},{2,66}... | collective-permute-start | bytes 1179656 | tf_op jit(solution)/shard_map/Move_x2/ppermute | solution.py:24
  112.4 12.6 %collective-permute-start.23 = (bf16[32,2,128,128]{3,2,1,0:T(8,128)(2,1)}, bf16[32,2,128,128]{3,2,1,0:T(8,128)(2,1)S(1)}, u32[]{:S(2)}, u32[]{:S(2)}) collective-permute-start(bf16[32,2,128,128]{3,2,1,0:T(8,128)(2,1)} %get-tuple-element.131), channel_id=1, source_target_pairs={{0,16},{16,0},{1,17},{17,1},{2,18},{18,2},{3,19},{19,3},{4,20},{20... | collective-permute-start | bytes 6291464 | tf_op jit(solution)/shard_map/Move_c1/ppermute | solution.py:24
  113.7 16.8 %collective-permute-start.20 = (bf16[2,2,3,128,128]{4,3,2,1,0:T(8,128)(2,1)}, bf16[2,2,3,128,128]{4,3,2,1,0:T(8,128)(2,1)S(1)}, u32[]{:S(2)}, u32[]{:S(2)}) collective-permute-start(bf16[2,2,3,128,128]{4,3,2,1,0:T(8,128)(2,1)} %get-tuple-element.125), channel_id=1, source_target_pairs={{0,96},{32,0},{64,32},{96,64},{1,97},{33,1},{65,33},{97,65},{2,98}... | collective-permute-start | bytes 1179656 | tf_op jit(solution)/shard_map/Move_x3/ppermute | solution.py:24
  115.4 20.4 %collective-permute-start.21 = (bf16[2,2,3,128,128]{4,3,2,1,0:T(8,128)(2,1)}, bf16[2,2,3,128,128]{4,3,2,1,0:T(8,128)(2,1)}, u32[]{:S(2)}, u32[]{:S(2)}) collective-permute-start(bf16[2,2,3,128,128]{4,3,2,1,0:T(8,128)(2,1)} %get-tuple-element.126), channel_id=1, source_target_pairs={{0,32},{32,64},{64,96},{96,0},{1,33},{33,65},{65,97},{97,1},{2,34}... | collective-permute-start | bytes 1179656 | tf_op jit(solution)/shard_map/Move_x1/ppermute | solution.py:24
  115.4 20.4 %collective-permute-start.22 = (bf16[2,2,3,128,128]{4,3,2,1,0:T(8,128)(2,1)}, bf16[2,2,3,128,128]{4,3,2,1,0:T(8,128)(2,1)}, u32[]{:S(2)}, u32[]{:S(2)}) collective-permute-start(bf16[2,2,3,128,128]{4,3,2,1,0:T(8,128)(2,1)} %get-tuple-element.127), channel_id=1, source_target_pairs={{0,64},{32,96},{64,0},{96,32},{1,65},{33,97},{65,1},{97,33},{2,66}... | collective-permute-start | bytes 1179656 | tf_op jit(solution)/shard_map/Move_x2/ppermute | solution.py:24
  116.6 19.2 %collective-permute-start.24 = (bf16[2,2,3,128,128]{4,3,2,1,0:T(8,128)(2,1)}, bf16[2,2,3,128,128]{4,3,2,1,0:T(8,128)(2,1)}, u32[]{:S(2)}, u32[]{:S(2)}) collective-permute-start(bf16[2,2,3,128,128]{4,3,2,1,0:T(8,128)(2,1)} %add_convert_fusion.2), channel_id=1, source_target_pairs={{0,128},{128,0},{1,129},{129,1},{2,130},{130,2},{3,131},{131,3},{4... | collective-permute-start | bytes 1179656 | tf_op jit(solution)/shard_map/Move_zh1/ppermute | solution.py:24
  135.8 9.5 %collective-permute-start.25 = (bf16[1,4,3,128,128]{4,3,2,1,0:T(8,128)(2,1)S(1)}, bf16[1,4,3,128,128]{4,3,2,1,0:T(8,128)(2,1)S(1)}, u32[]{:S(2)}, u32[]{:S(2)}) collective-permute-start(bf16[1,4,3,128,128]{4,3,2,1,0:T(8,128)(2,1)S(1)} %get-tuple-element.135), channel_id=1, source_target_pairs={{0,96},{32,0},{64,32},{96,64},{1,97},{33,1},{65,33},{97,65},{2,98}... | collective-permute-start | bytes 1179656 | tf_op jit(solution)/shard_map/Move_x3/ppermute | solution.py:24
  135.8 10.6 %collective-permute-start.26 = (bf16[1,4,3,128,128]{4,3,2,1,0:T(8,128)(2,1)S(1)}, bf16[1,4,3,128,128]{4,3,2,1,0:T(8,128)(2,1)S(1)}, u32[]{:S(2)}, u32[]{:S(2)}) collective-permute-start(bf16[1,4,3,128,128]{4,3,2,1,0:T(8,128)(2,1)S(1)} %get-tuple-element.136), channel_id=1, source_target_pairs={{0,32},{32,64},{64,96},{96,0},{1,33},{33,65},{65,97},{97,1},{2,34}... | collective-permute-start | bytes 1179656 | tf_op jit(solution)/shard_map/Move_x1/ppermute | solution.py:24
  146.6 29.8 %collective-permute-start.27 = (bf16[2,4,3,128,128]{4,3,2,1,0:T(8,128)(2,1)S(1)}, bf16[2,4,3,128,128]{4,3,2,1,0:T(8,128)(2,1)S(1)}, u32[]{:S(2)}, u32[]{:S(2)}) collective-permute-start(bf16[2,4,3,128,128]{4,3,2,1,0:T(8,128)(2,1)S(1)} %get-tuple-element.141), channel_id=1, source_target_pairs={{0,96},{32,0},{64,32},{96,64},{1,97},{33,1},{65,33},{97,65},{2,98}... | collective-permute-start | bytes 2359304 | tf_op jit(solution)/shard_map/Move_x3/ppermute | solution.py:24
  146.8 35.9 %collective-permute-start.28 = (bf16[2,4,3,128,128]{4,3,2,1,0:T(8,128)(2,1)S(1)}, bf16[2,4,3,128,128]{4,3,2,1,0:T(8,128)(2,1)}, u32[]{:S(2)}, u32[]{:S(2)}) collective-permute-start(bf16[2,4,3,128,128]{4,3,2,1,0:T(8,128)(2,1)S(1)} %get-tuple-element.142), channel_id=1, source_target_pairs={{0,32},{32,64},{64,96},{96,0},{1,33},{33,65},{65,97},{97,1},{2,34}... | collective-permute-start | bytes 2359304 | tf_op jit(solution)/shard_map/Move_x1/ppermute | solution.py:24
  148.2 36.0 %collective-permute-start.32 = (bf16[2,2,3,128,128]{4,3,2,1,0:T(8,128)(2,1)S(1)}, bf16[2,2,3,128,128]{4,3,2,1,0:T(8,128)(2,1)}, u32[]{:S(2)}, u32[]{:S(2)}) collective-permute-start(bf16[2,2,3,128,128]{4,3,2,1,0:T(8,128)(2,1)S(1)} %add_convert_fusion.1.refs_4_), channel_id=1, source_target_pairs={{0,128},{128,0},{1,129},{129,1},{2,130},{130,2},{3,131},{131,3},{4... | collective-permute-start | bytes 1179656 | tf_op jit(solution)/shard_map/Move_zh1/ppermute | solution.py:24
  173.1 11.1 %collective-permute-start.29 = (bf16[2,2,128,128]{3,2,1,0:T(8,128)(2,1)S(1)}, bf16[2,2,128,128]{3,2,1,0:T(8,128)(2,1)S(1)}, u32[]{:S(2)}, u32[]{:S(2)}) collective-permute-start(bf16[2,2,128,128]{3,2,1,0:T(8,128)(2,1)S(1)} %get-tuple-element.179), channel_id=1, source_target_pairs={{0,3},{1,0},{2,1},{3,2},{4,7},{5,4},{6,5},{7,6},{8,11},{9,8},{10,9... | collective-permute-start | bytes 393224 | tf_op jit(solution)/shard_map/Move_zl3/ppermute | solution.py:24
  176.4 16.3 %collective-permute-start.30 = (bf16[2,2,128,128]{3,2,1,0:T(8,128)(2,1)S(1)}, bf16[2,2,128,128]{3,2,1,0:T(8,128)(2,1)S(1)}, u32[]{:S(2)}, u32[]{:S(2)}) collective-permute-start(bf16[2,2,128,128]{3,2,1,0:T(8,128)(2,1)S(1)} %get-tuple-element.178), channel_id=1, source_target_pairs={{0,2},{1,3},{2,0},{3,1},{4,6},{5,7},{6,4},{7,5},{8,10},{9,11},{10,... | collective-permute-start | bytes 393224 | tf_op jit(solution)/shard_map/Move_zl2/ppermute | solution.py:24
  176.4 16.3 %collective-permute-start.31 = (bf16[2,2,128,128]{3,2,1,0:T(8,128)(2,1)S(1)}, bf16[2,2,128,128]{3,2,1,0:T(8,128)(2,1)S(1)}, u32[]{:S(2)}, u32[]{:S(2)}) collective-permute-start(bf16[2,2,128,128]{3,2,1,0:T(8,128)(2,1)S(1)} %get-tuple-element.177), channel_id=1, source_target_pairs={{0,1},{1,2},{2,3},{3,0},{4,5},{5,6},{6,7},{7,4},{8,9},{9,10},{10,1... | collective-permute-start | bytes 393224 | tf_op jit(solution)/shard_map/Move_zl1/ppermute | solution.py:24
  (29 other events, 271.0 us)
Sparse Core Ops, SparseCore 0:
  31.3 35.7 all-gather.1
  129.0 42.9 reduce-scatter.1
